TPU v7x, 256 devices: a whole 4x4x8 slice. The times are simulated.
256 devices in a mesh: replica: 32 (over z_hi, y, core), shard: 8 (over x, z_lo).
Axes of the slice: x: 4, y: 4, z: 8 (z_hi: 4, z_lo: 2; z = z_hi * 2 + z_lo), core: 2. Of those that a mesh axis runs over, the one named last changes fastest.
Arguments:
- weight: bfloat16 [256, 8192], P(None, 'shard'), may hold values from -6 to 6
- momentum: float32 [32, 256, 8192], P('replica', None, 'shard'), may hold values from -6 to 6
- grad: bfloat16 [32, 256, 8192], P('replica', None, 'shard'), may hold values from -6 to 6
- positions: int32 [32, 4, 128, 32], P('replica', None, 'shard'), may hold values from 0 to 4095, as said below
Outputs:
- kept_state: float32 [32, 256, 8192], P('replica', None, 'shard')
- direction: bfloat16 [256, 8192], P(None, 'shard')
- new_weight: bfloat16 [256, 8192], replicated
Inputs may be any that keep to these rules, and one draw needn't show every extreme that they name: The 32 positions of one block on one replica are distinct; replicas choose independently.
All inputs are finite; a program needn't handle non-finite values.
Results may differ from a plain program's by a relative error of at most 0.001.
Values may be sent and summed in bfloat16 or wider, within the bound.
No kernel may reach another device: no remote copies, remote signals or barrier semaphores. Data moves between devices by JAX's collectives and lax.ppermute only.
A program may use at most 64 MiB of HBM per device.

v0:
```python
import math

import jax
import jax.numpy as jnp
from jax import lax
from jax.sharding import Mesh
from jax.sharding import PartitionSpec as P

GROUP = 64
REPLICA = ("replica_0", "replica_1", "replica_2")


beta_decay = 0.9
step_rate = 0.02


def padded_to(lines, size):
    spare = -len(lines) % size
    return jnp.pad(lines, [(0, spare)] + [(0, 0)] * (lines.ndim - 1))


def copy_for_each(array, axis):
    copies = jnp.broadcast_to(array, (lax.axis_size(axis), *array.shape))
    return lax.all_to_all(copies, axis, split_axis=0, concat_axis=0, tiled=True)


def laid_out(blocks, dim):
    blocks = jnp.moveaxis(blocks, 0, dim)
    shape = blocks.shape
    return blocks.reshape(*shape[:dim], shape[dim] * shape[dim + 1], *shape[dim + 2 :])


def whole_of(array, axes, dim):
    far, near = axes
    blocks = copy_for_each(copy_for_each(array, far), near)
    return laid_out(blocks.swapaxes(0, 1).reshape(-1, *array.shape), dim)


def in_blocks(array, dim, size):
    before, after = (array.shape[:dim], array.shape[dim + 1 :])
    return jnp.moveaxis(array.reshape(*before, size, -1, *after), dim, 0)


def sent_and_summed(array, axis, dim):
    size = lax.axis_size(axis)
    blocks = lax.all_to_all(in_blocks(array, dim, size), axis, 0, 0, tiled=True)
    return jnp.sum(blocks, axis=0)


def sum_in_two_steps(array, axes, dim):
    far, near = axes
    blocks = in_blocks(array, dim, lax.axis_size(far))
    nearer = sent_and_summed(blocks, near, dim + 1)
    arrived = lax.all_to_all(nearer, far, split_axis=0, concat_axis=0, tiled=True)
    return arrived.sum(axis=0)


def sum_by_parts(array, axes):
    lines = array.reshape(-1, array.shape[-1])
    padded = padded_to(lines, lax.axis_size(axes[0]) * lax.axis_size(axes[1]))
    whole = whole_of(sum_in_two_steps(padded, axes, 0), axes, 0)
    return lax.slice_in_dim(whole, 0, len(lines)).reshape(array.shape)


def dct_basis():
    freq = jnp.arange(GROUP, dtype=jnp.float32)[:, None]
    cells = jnp.arange(GROUP, dtype=jnp.float32)[None, :]
    scales = jnp.where(freq == 0, math.sqrt(1.0 / GROUP), math.sqrt(2.0 / GROUP))
    return scales * jnp.cos(math.pi * (2.0 * cells + 1.0) * freq / (2.0 * GROUP))


def basis_rows(index, basis_table):
    one_hot = (index[..., None] == jnp.arange(GROUP, dtype=jnp.int32)).astype(jnp.float32)
    return jnp.einsum("xyka,ai->xyki", one_hot, basis_table, precision=lax.Precision.HIGHEST)


def extract(field, pos_table, basis_table):
    row_blocks, col_blocks = (pos_table.shape[0], pos_table.shape[1])
    left_rows = basis_rows(pos_table // GROUP, basis_table)
    right_rows = basis_rows(pos_table % GROUP, basis_table)
    block_view = field.reshape(row_blocks, GROUP, col_blocks, GROUP)
    inner_prod = jnp.einsum(
        "xyki,xiyj->xykj", left_rows, block_view, precision=lax.Precision.HIGHEST
    )
    return jnp.sum(inner_prod * right_rows, axis=-1)


def expand(values, pos_table, basis_table):
    row_blocks, col_blocks = (pos_table.shape[0], pos_table.shape[1])
    left_rows = basis_rows(pos_table // GROUP, basis_table)
    right_rows = basis_rows(pos_table % GROUP, basis_table)
    dense = jnp.einsum(
        "xyki,xyk,xykj->xiyj", left_rows, values, right_rows, precision=lax.Precision.HIGHEST
    )
    return dense.reshape(row_blocks * GROUP, col_blocks * GROUP)


def fill_grid(values, pos_table):
    row_blocks, col_blocks = (pos_table.shape[0], pos_table.shape[1])
    row_index = jnp.arange(row_blocks, dtype=jnp.int32)[:, None, None]
    col_index = jnp.arange(col_blocks, dtype=jnp.int32)[None, :, None]
    flat = jnp.zeros((row_blocks, col_blocks, GROUP * GROUP), jnp.float32)
    return flat.at[row_index, col_index, pos_table].add(values)


def decode(grid, basis_table):
    row_blocks, col_blocks = (grid.shape[0], grid.shape[1])
    square = grid.reshape(row_blocks, col_blocks, GROUP, GROUP)
    dense = jnp.einsum(
        "ai,xyab,bj->xiyj", basis_table, square, basis_table, precision=lax.Precision.HIGHEST
    )
    return dense.reshape(row_blocks * GROUP, col_blocks * GROUP)


def per_device(weight, momentum, grad, positions):
    basis_table = dct_basis()
    own_pos = positions[0]
    moved = beta_decay * momentum[0] + grad[0].astype(jnp.float32)
    picked = extract(moved, own_pos, basis_table)
    kept_state = moved - expand(picked, own_pos, basis_table)
    summed = sum_by_parts(fill_grid(picked, own_pos), (("replica_0", "replica_1"), "replica_2"))
    smooth = jnp.tanh(decode(summed, basis_table))
    updated = (weight.astype(jnp.float32) - step_rate * smooth).astype(jnp.bfloat16)
    new_weight = lax.all_gather(updated, "shard", axis=1, tiled=True)
    direction = smooth.astype(jnp.bfloat16)
    return (kept_state[None], direction, new_weight)


def solution(mesh):
    split = Mesh(
        mesh.devices.reshape(4, 4, 2, mesh.shape["shard"]),
        ("replica_0", "replica_1", "replica_2", "shard"),
    )
    in_specs = (
        P(None, "shard"),
        P(REPLICA, None, "shard"),
        P(REPLICA, None, "shard"),
        P(REPLICA, None, "shard", None),
    )
    out_specs = (P(REPLICA, None, "shard"), P(None, "shard"), P())
    return jax.shard_map(
        per_device, mesh=split, in_specs=in_specs, out_specs=out_specs, check_vma=False
    )
```

profile of v0, /device:TPU:1, one launch (start us, length us, event | category | flops | bytes accessed | tf_op | source)
XLA Modules:
  0.0 219.4 jit_solution(12417028372073017833)
XLA Ops:
  7.2 0.0 all-gather.2.cloned.1.call-start
  7.2 0.0 copy-start.1
  7.2 0.0 copy-start.2
  7.2 0.9 add_select_fusion
  8.2 0.8 compare_select_fusion
  8.9 0.8 fusion.10
  9.7 0.8 fusion.11
  10.5 0.0 copy-done.1
  10.5 0.0 copy-done.2
  10.5 0.1 convert_add_fusion
  10.7 0.0 copy-start.3
  10.7 0.0 copy-start.4
  10.7 1.9 add.62
  12.6 0.0 copy-done.3
  12.6 0.1 and_reduce_fusion
  12.7 0.0 copy-done.4
  12.7 0.1 multiply_reduce_fusion
  12.8 0.1 reshape.127
  12.8 4.2 %fusion.5 = f32[4,16,32]{2,1,0:T(8,128)S(1)} fusion(f32[4,16,32,64]{3,2,1,0:T(8,128)S(1)} %fusion.11, f32[4,16,32,64]{3,2,1,0:T(8,128)S(1)} %fusion.10, f32[4,64,16,64]{3,2,1,0:T(8,128)} %add.62), kind=kOutput, calls=%fused_computation.7 | convolution fusion | flops 100923392 | bytes 2105344 | tf_op jit(solution)/shard_map/xyki,xiyj->xykj/dot_general | solution.py:82
  17.0 0.1 reshape.129
  17.1 12.2 %scatter_custom_fusion = f32[262144]{0:T(1024)} fusion(s32[2048]{0:T(1024)S(1)} %reshape.127, f32[2048]{0:T(1024)S(1)} %reshape.129, f32[]{:T(128)} %constant.54.clone.1), kind=kCustom, calls=%fused_computation.16 | custom fusion | flops 2048 | bytes 1048580
  29.4 2.7 %reshape_reshape.3 = f32[16,2,2,4096]{3,2,1,0:T(2,128)} reshape(f32[262144]{0:T(1024)} %scatter_custom_fusion) | data formatting | bytes 2097152 | tf_op jit(solution)/shard_map/reshape;reshape | solution.py:41
  32.1 1.3 copy.37
  33.4 8.2 %all_to_all.20 = f32[2,16,2,4096]{3,2,1,0:T(2,128)} all-to-all(f32[2,16,2,4096]{3,2,1,0:T(2,128)S(1)} %copy.37), channel_id=1, replica_groups=mesh['replica_0'=4,'replica_1'=4,'replica_2'=2,'shard'=8] {'replica_2'}, dimensions={0} | all-to-all | bytes 2097152 | tf_op jit(solution)/shard_map/all_to_all | solution.py:46
  41.6 2.9 %reduce_sum.28 = f32[16,2,4096]{2,1,0:T(2,128)} reduce(f32[2,16,2,4096]{3,2,1,0:T(2,128)} %all_to_all.20, f32[]{:T(128)} %constant.54.clone.1), dimensions={0}, to_apply=%region_2.3 | reduce | flops 131072 | bytes 1572868 | tf_op jit(solution)/shard_map/reduce_sum | solution.py:47
  44.5 24.6 %all_to_all.21 = f32[16,2,4096]{2,1,0:T(2,128)} all-to-all(f32[16,2,4096]{2,1,0:T(2,128)} %reduce_sum.28), channel_id=1, replica_groups=mesh['replica_0'=4,'replica_1'=4,'replica_2'=2,'shard'=8] {'replica_0','..., dimensions={0} | all-to-all | bytes 1048576 | tf_op jit(solution)/shard_map/all_to_all | solution.py:54
  69.1 1.2 reduce_sum.29
  70.3 0.2 broadcast_in_dim.23
  70.5 19.6 %all_to_all.22 = f32[16,2,4096]{2,1,0:T(2,128)S(1)} all-to-all(f32[16,2,4096]{2,1,0:T(2,128)S(1)} %broadcast_in_dim.23), channel_id=1, replica_groups=mesh['replica_0'=4,'replica_1'=4,'replica_2'=2,'shard'=8] {'replica_0','..., dimensions={0} | all-to-all | bytes 1048576 | tf_op jit(solution)/shard_map/all_to_all | solution.py:24
  90.1 0.6 broadcast_in_dim.24
  90.7 8.0 %all_to_all.23 = f32[2,16,2,4096]{3,2,1,0:T(2,128)S(1)} all-to-all(f32[2,16,2,4096]{3,2,1,0:T(2,128)S(1)} %broadcast_in_dim.24), channel_id=1, replica_groups=mesh['replica_0'=4,'replica_1'=4,'replica_2'=2,'shard'=8] {'replica_2'}, dimensions={0} | all-to-all | bytes 2097152 | tf_op jit(solution)/shard_map/all_to_all | solution.py:24
  98.7 1.0 copy.39
  99.7 3.2 %reshape_reshape_reshape_reshape.3 = f32[4,16,64,64]{3,2,1,0:T(8,128)} reshape(f32[16,2,2,4096]{3,2,1,0:T(2,128)} %copy.39) | data formatting | bytes 2097152 | tf_op jit(solution)/shard_map/reshape;reshape;reshape;reshape | solution.py:108
  102.9 3.6 %fusion.19 = f32[4,16,64,64]{2,3,1,0:T(8,128)S(1)} fusion(f32[4,16,64,64]{3,2,1,0:T(8,128)} %reshape_reshape_reshape_reshape.3, f32[64]{0:T(128)S(1)} %get-tuple-element.8, f32[64]{0:T(128)S(1)} %get-tuple-element.7), kind=kOutput, calls=%fused_computation.32 | convolution fusion | flops 201338880 | bytes 2097664 | tf_op jit(solution)/shard_map/ai,xyab,bj->xiyj/dot_general | solution.py:109
  106.5 3.0 %multiply_bitcast_fusion = (f32[4,64,16,64]{3,1,2,0:T(8,128)S(1)}, bf16[4,64,16,64]{3,1,2,0:T(8,128)(2,1)}) fusion(f32[4,16,64,64]{2,3,1,0:T(8,128)S(1)} %fusion.19, f32[64]{0:T(128)S(1)} %get-tuple-element.8, f32[64]{0:T(128)S(1)} %get-tuple-element.7), kind=kOutput, calls=%fused_computation.3 | convolution fusion | flops 201863168 | bytes 2621952 | tf_op jit(solution)/shard_map/ai,xyab,bj->xiyj/dot_general | solution.py:109
  109.5 2.5 %copy.43 = f32[4,64,16,64]{3,2,1,0:T(8,128)} copy(f32[4,64,16,64]{3,1,2,0:T(8,128)S(1)} %get-tuple-element.3) | data formatting | bytes 2097152 | tf_op jit(solution)/shard_map/mul | solution.py:123
  112.0 2.7 %mul.124 = f32[256,1024]{1,0:T(8,128)} reshape(f32[4,64,16,64]{3,2,1,0:T(8,128)} %copy.43) | data formatting | bytes 2097152 | tf_op jit(solution)/shard_map/mul | solution.py:123
  114.8 2.3 %subtract_convert_fusion = bf16[256,1024]{1,0:T(8,128)(2,1)} fusion(f32[256,1024]{1,0:T(8,128)} %mul.124, bf16[256,1024]{1,0:T(8,128)(2,1)} %param.4), kind=kLoop, calls=%fused_computation.9 | loop fusion | flops 786432 | bytes 2097152 | tf_op jit(solution)/shard_map/convert_element_type | solution.py:123
  117.1 0.0 all-gather.2.cloned.1.call-update
  117.1 5.1 %convolution_bitcast_fusion = f32[4,64,16,64]{1,3,2,0:T(8,128)} fusion(f32[4,16,32,64]{3,2,1,0:T(8,128)S(1)} %fusion.10, f32[4,16,32,64]{3,2,1,0:T(8,128)S(1)} %fusion.11, f32[4,16,32]{2,1,0:T(8,128)S(1)} %fusion.5), kind=kOutput, calls=%fused_computation.5 | convolution fusion | flops 100794368 | bytes 2105344 | tf_op jit(solution)/shard_map/xyki,xyk,xykj->xiyj/dot_general | solution.py:92
  122.2 2.5 %copy.36 = f32[4,64,16,64]{3,2,1,0:T(8,128)S(1)} copy(f32[4,64,16,64]{1,3,2,0:T(8,128)} %convolution_bitcast_fusion) | data formatting | bytes 2097152 | tf_op jit(solution)/shard_map/xyki,xyk,xykj->xiyj/transpose | solution.py:92
  124.7 1.5 reshape.121
  126.2 0.0 copy-start
  126.2 2.5 %sub.16 = f32[1,256,1024]{2,1,0:T(8,128)} subtract(f32[1,256,1024]{2,1,0:T(8,128)S(1)} %convert_add_fusion, f32[1,256,1024]{2,1,0:T(8,128)} %reshape.121) | non-fusion elementwise | flops 262144 | bytes 3145728 | tf_op jit(solution)/shard_map/sub | solution.py:120
  128.7 0.0 copy-done
  128.7 0.7 copy.42
  129.4 1.5 convert_element_type.28
  130.9 77.0 %all-gather.2.cloned.1.call-done = bf16[256,8192]{1,0:T(8,128)(2,1)} async-done(((bf16[256,1024]{1,0:T(8,128)(2,1)}), bf16[256,8192]{1,0:T(8,128)(2,1)}) %all-gather.2.cloned.1.call-update) | async-done | bytes 4194320 | tf_op jit(solution)/shard_map/all_gather | solution.py:124
  207.9 4.6 %copy.55 = bf16[256,8192]{1,0:T(8,128)(2,1)} copy(bf16[256,8192]{1,0:T(8,128)(2,1)} %all-gather.2.cloned.1.call-done) | data formatting | bytes 8388608
  (4 shorter events, 0.0 us)
Async XLA Ops:
  7.2 200.7 %all-gather.2.cloned.1.call-start = ((), (), s32[]{:S(2)}) async-start(), calls=%async_computation.4 | async-start | bytes 4718592 | tf_op jit(solution)/shard_map/all_gather | solution.py:124
  7.2 3.3 %copy-start.1 = (f32[1,256,1024]{2,1,0:T(8,128)S(1)}, f32[1,256,1024]{2,1,0:T(8,128)}, u32[]{:S(2)}) copy-start(f32[1,256,1024]{2,1,0:T(8,128)} %param.5) | copy-start | bytes 3145732
  7.2 3.3 %copy-start.2 = (bf16[1,256,1024]{2,1,0:T(8,128)(2,1)S(1)}, bf16[1,256,1024]{2,1,0:T(8,128)(2,1)}, u32[]{:S(2)}) copy-start(bf16[1,256,1024]{2,1,0:T(8,128)(2,1)} %param.6) | copy-start | bytes 1572868
  10.7 1.9 copy-start.3
  10.7 2.0 copy-start.4
  126.2 2.5 %copy-start = (bf16[4,64,16,64]{3,1,2,0:T(8,128)(2,1)S(1)}, bf16[4,64,16,64]{3,1,2,0:T(8,128)(2,1)}, u32[]{:S(2)}) copy-start(bf16[4,64,16,64]{3,1,2,0:T(8,128)(2,1)} %get-tuple-element.4) | copy-start | bytes 1572868
Sparse Core Ops, SparseCore 0:
  117.2 90.6 all-gather.1
where the time goes:
time: 220 us; the launch traced here: 219 us
  waiting for transfers between devices  77 us (35%)
  blocking collectives  60.4 us (27%)
  local copies, waits for them, and re-layouts  27.2 us (12%)
  other arithmetic  23.1 us (10%)
  matrix products  17.4 us (8%)
  between operations  14.2 us (6%)
    all_gather x1, waiting for transfers between devices, per_device(): new_weight = lax.all_gather(updated, 'shard', axis=1, tiled=True)  77 us
    all_to_all x2, blocking collectives, copy_for_each(): return lax.all_to_all(copies, axis, split_axis=0, concat_axis=0, tiled=True)  27.6 us
    all_to_all x1, blocking collectives, sum_in_two_steps(): lax.all_to_all(nearer, far, split_axis=0, concat_axis=0, tiled=True)  24.6 us
    unnamed x4, other arithmetic  12.4 us
    all_to_all x1, blocking collectives, sent_and_summed(): blocks = lax.all_to_all(in_blocks(array, dim, size), axis, 0, 0, tiled=True)  8.22 us
    dot_general x2, matrix products, decode(): jnp.einsum('ai,xyab,bj->xiyj', basis_table, square, basis_table, precisio...  6.6 us
    mul x2, local copies, waits for them, and re-layouts, per_device(): step_rate * smooth  5.27 us
    dot_general x1, matrix products, expand(): jnp.einsum('xyki,xyk,xykj->xiyj', left_rows, values, right_rows, precisio...  5.07 us
  transfers between devices with their start and end apart: 1, of which 1 were waited for; matrix products, arithmetic and copies ran while one was open for 6% of the time, Pallas kernels for 0%

commit v1 on v0

v1 whole, which is shorter than its diff:
```python
import functools
import math

import jax
import jax.numpy as jnp
import numpy as np
from jax import lax
from jax.experimental import pallas as pl
from jax.experimental.pallas import tpu as pltpu
from jax.sharding import Mesh
from jax.sharding import PartitionSpec as P

GROUP = 64
REPLICA = ("zh", "y", "c")
SHARD = ("x", "zl")
beta_decay = 0.9
step_rate = 0.02
F32, BF16 = jnp.float32, jnp.bfloat16
VMEM = pl.BlockSpec(memory_space=pltpu.VMEM)
ANY = pl.BlockSpec(memory_space=pl.ANY)


def basis_parts():
    freq, cells = np.arange(GROUP)[:, None], np.arange(GROUP)[None, :]
    scales = np.where(freq == 0, math.sqrt(1.0 / GROUP), math.sqrt(2.0 / GROUP))
    table = scales * np.cos(math.pi * (2.0 * cells + 1.0) * freq / (2.0 * GROUP))
    four = np.kron(np.eye(4), table)
    high = four.astype(jnp.bfloat16)
    low = (four - high.astype(np.float64)).astype(jnp.bfloat16)
    return [np.ascontiguousarray(part) for part in (high, low, high.T, low.T)]


def two_parts(value):
    high = value.astype(BF16)
    return high, (value - high.astype(F32)).astype(BF16)


def rows_by_rows(left, right):
    return lax.dot_general(left, right, (((1,), (1,)), ((), ())), preferred_element_type=F32)


def rows_by_cols(left, right):
    return lax.dot_general(left, right, (((1,), (0,)), ((), ())), preferred_element_type=F32)


def product(dot, left, right):
    return dot(left[0], right[0]) + dot(left[0], right[1]) + dot(left[1], right[0])


def one_hot_rows(place, lines, dtype):
    line = lax.broadcasted_iota(jnp.int32, (lines, place.shape[1]), 0)
    return jnp.where(line == place, 1.0, 0.0).astype(dtype)


def split_place(flat):
    lane = lax.broadcasted_iota(jnp.int32, flat.shape, 1)
    return (flat >> 6) + ((lane >> 5) << 6), flat & 63


def spread(values, column):
    line = lax.broadcasted_iota(jnp.int32, (GROUP, values.shape[1]), 0)
    return two_parts(jnp.where(line == column, values, 0.0))


def extract_kernel(momentum, grad, positions, bh, bl, out, places):
    g = pl.program_id(0)
    mine = lax.axis_index("y")

    @pl.when(g == 0)
    def _():
        for x in range(4):
            places[:, 32 * x : 32 * x + 32] = positions[x]

    basis = (bh[...], bl[...])
    moved = beta_decay * momentum[...] + grad[...].astype(F32)
    half = product(rows_by_rows, basis, two_parts(moved))
    coeff = jnp.stack(two_parts(product(rows_by_rows, two_parts(half), basis)))
    lines = []
    for q in range(4):
        flat = places[pl.ds(4 * g + q, 1), :]
        row, column = split_place(flat)
        block = coeff[:, GROUP * q : GROUP * (q + 1)].reshape(2 * GROUP, 4 * GROUP)
        found = rows_by_cols(block, one_hot_rows(row, 4 * GROUP, BF16))
        found = found[:GROUP] + found[GROUP:]
        line = lax.broadcasted_iota(jnp.int32, found.shape, 0)
        lines.append(jnp.sum(jnp.where(line == column, found, 0.0), axis=0, keepdims=True))
        lines.append(flat.astype(F32))
    at = pl.multiple_of(8 * jnp.bitwise_xor(g, mine), 8)
    out[pl.ds(at, 8), :] = jnp.concatenate(lines, axis=0)


def extract(momentum, grad, positions, basis):
    column = lambda g: (0, g)
    whole = lambda *shape: pl.BlockSpec(shape, lambda g: (0,) * len(shape))
    return pl.pallas_call(
        extract_kernel,
        grid=(4,),
        in_specs=[
            pl.BlockSpec((256, 256), column),
            pl.BlockSpec((256, 256), column),
            whole(4, 16, 32),
            whole(256, 256),
            whole(256, 256),
        ],
        out_specs=whole(32, 128),
        out_shape=jax.ShapeDtypeStruct((32, 128), F32),
        scratch_shapes=[pltpu.VMEM((16, 128), jnp.int32)],
        cost_estimate=pl.CostEstimate(flops=10**9, bytes_accessed=2 * 2**20, transcendentals=0),
        name="extract",
    )(momentum, grad, positions, basis[0], basis[1])


def kept_kernel(momentum, grad, sent, bh, bl, th, tl, out):
    g = pl.program_id(0)
    mine = lax.axis_index("y")
    at = pl.multiple_of(8 * jnp.bitwise_xor(g, mine), 8)
    tile = sent[pl.ds(at, 8), :]
    blocks = []
    for q in range(4):
        row, column = split_place(tile[2 * q + 1 : 2 * q + 2].astype(jnp.int32))
        high, low = spread(tile[2 * q : 2 * q + 1], column)
        hot = one_hot_rows(row, 4 * GROUP, BF16)
        blocks.append(rows_by_rows(high, hot) + rows_by_rows(low, hot))
    grid = two_parts(jnp.concatenate(blocks, axis=0))
    half = product(rows_by_rows, (th[...], tl[...]), grid)
    dense = product(rows_by_cols, two_parts(half), (bh[...], bl[...]))
    moved = beta_decay * momentum[...] + grad[...].astype(F32)
    out[...] = moved - dense


def kept(momentum, grad, sent, basis):
    column = lambda g: (0, g)
    whole = lambda *shape: pl.BlockSpec(shape, lambda g: (0,) * len(shape))
    return pl.pallas_call(
        kept_kernel,
        grid=(4,),
        in_specs=[pl.BlockSpec((256, 256), column)] * 2 + [whole(32, 128)] + [whole(256, 256)] * 4,
        out_specs=pl.BlockSpec((256, 256), column),
        out_shape=jax.ShapeDtypeStruct((256, 1024), F32),
        cost_estimate=pl.CostEstimate(flops=2 * 10**9, bytes_accessed=3 * 2**20, transcendentals=0),
        name="kept",
    )(momentum, grad, sent, *basis)


def regroup_kernel(a, b, c, d, *outs):
    for k, out in enumerate(outs):
        for z, ref in enumerate((a, b, c, d)):
            out[8 * z : 8 * z + 8, :] = ref[8 * k : 8 * k + 8, :]


def regroup(arrays):
    return pl.pallas_call(
        regroup_kernel,
        in_specs=[VMEM] * 4,
        out_specs=[VMEM] * 4,
        out_shape=[jax.ShapeDtypeStruct((32, 128), F32)] * 4,
        name="regroup",
    )(*arrays)


def decode_kernel(*refs):
    entries, (weight, bh, bl, th, tl), (fresh, smooth_out, staged, sem) = refs[:8], refs[8:13], refs[13:]
    core = lax.axis_index("c")
    place = pl.multiple_of((lax.axis_index("y") * 2 + core) * 128, 128)
    copy = pltpu.make_async_copy(weight.at[:, pl.ds(place, 128)], staged, sem)
    copy.start()
    tiles = []
    for ref in entries:
        for z in range(4):
            tiles.append(jnp.where(core == 0, ref[8 * z : 8 * z + 4, :], ref[8 * z + 4 : 8 * z + 8, :]))
    blocks = []
    for j in range(2):
        total = jnp.zeros((2 * GROUP, 4 * GROUP), F32)
        for pair in range(0, len(tiles), 2):
            lefts, hots = [], []
            for tile in tiles[pair : pair + 2]:
                row, column = split_place(tile[2 * j + 1 : 2 * j + 2].astype(jnp.int32))
                lefts.append(jnp.concatenate(spread(tile[2 * j : 2 * j + 1], column), axis=0))
                hots.append(one_hot_rows(row, 4 * GROUP, BF16))
            total = total + rows_by_rows(jnp.concatenate(lefts, axis=1), jnp.concatenate(hots, axis=1))
        blocks.append(total[:GROUP] + total[GROUP:])
    grid = two_parts(jnp.concatenate(blocks, axis=0))
    half = product(rows_by_rows, (th[...], tl[...]), grid)
    dense = product(rows_by_cols, two_parts(half), (bh[:128, :128], bl[:128, :128]))
    smooth = jnp.tanh(dense)
    smooth_out[...] = smooth.astype(BF16)
    copy.wait()
    fresh[...] = (staged[...].astype(F32) - step_rate * smooth).astype(BF16)


def decode(entries, weight, basis):
    return pl.pallas_call(
        decode_kernel,
        in_specs=[VMEM] * 8 + [ANY] + [VMEM] * 4,
        out_specs=[VMEM] * 2,
        out_shape=[jax.ShapeDtypeStruct((256, 128), BF16)] * 2,
        scratch_shapes=[pltpu.VMEM((256, 128), BF16), pltpu.SemaphoreType.DMA],
        cost_estimate=pl.CostEstimate(flops=10**9, bytes_accessed=2**20, transcendentals=32768),
        name="decode",
    )(*entries, weight, *basis)


def join_kernel(*refs):
    out = refs[-1]
    at = 0
    for ref in refs[:-1]:
        size = ref.shape[0]
        out[at : at + size] = ref[...]
        at += size


def join(arrays, name):
    total = sum(array.shape[0] for array in arrays)
    return pl.pallas_call(
        join_kernel,
        in_specs=[VMEM] * len(arrays),
        out_specs=VMEM,
        out_shape=jax.ShapeDtypeStruct((total, *arrays[0].shape[1:]), arrays[0].dtype),
        name=name,
    )(*arrays)


def assemble_kernel(*refs):
    pieces, out, sem = refs[:8], refs[8], refs[9]
    core, x, y, zl = (lax.axis_index(name) for name in ("c", "x", "y", "zl"))
    copies = []
    for other in range(2):
        at_core = jnp.bitwise_xor(core, other)
        for k2 in range(4):
            for k1 in range(4):
                dx = jnp.where(at_core == 0, k1, k2)
                dy = jnp.where(at_core == 0, k2, k1)
                for dz in range(2):
                    shard = jnp.bitwise_xor(x, dx) * 2 + jnp.bitwise_xor(zl, dz)
                    tile = shard * 8 + jnp.bitwise_xor(y, dy) * 2 + at_core
                    columns = pl.ds(pl.multiple_of(tile * 128, 128), 128)
                    copy = pltpu.make_async_copy(
                        pieces[4 * other + k2].at[2 * k1 + dz], out.at[:, columns], sem.at[len(copies)]
                    )
                    copy.start()
                    copies.append(copy)
    for copy in copies:
        copy.wait()


def assemble(pieces):
    return pl.pallas_call(
        assemble_kernel,
        in_specs=[ANY] * 8,
        out_specs=ANY,
        out_shape=jax.ShapeDtypeStruct((256, 8192), BF16),
        scratch_shapes=[pltpu.SemaphoreType.DMA((64,))],
        name="assemble",
    )(*pieces)


def lay_kernel(*refs):
    pieces, out = refs[:8], refs[8]
    core, y = lax.axis_index("c"), lax.axis_index("y")
    for other in range(2):
        for k in range(4):
            tile = jnp.bitwise_xor(y, k) * 2 + jnp.bitwise_xor(core, other)
            out[:, pl.ds(pl.multiple_of(tile * 128, 128), 128)] = pieces[4 * other + k][...]


def lay(pieces):
    return pl.pallas_call(
        lay_kernel,
        in_specs=[VMEM] * 8,
        out_specs=VMEM,
        out_shape=jax.ShapeDtypeStruct((256, 1024), BF16),
        name="lay",
    )(*pieces)


def swapped(array, axis, size, k):
    return lax.ppermute(array, axis, [(i, i ^ k) for i in range(size)])


def crossed(array, first, k):
    perm = []
    for i in range(32):
        y, c, x = i >> 3, (i >> 2) & 1, i & 3
        to = (y, c, x ^ k) if c == first else (y ^ k, c, x)
        perm.append((i, (to[0] << 3) | (to[1] << 2) | to[2]))
    return lax.ppermute(array, ("y", "c", "x"), perm)


def per_device(weight, momentum, grad, positions):
    basis = [jnp.asarray(part) for part in basis_parts()]
    sent = extract(momentum[0], grad[0], positions[0], basis)
    mine = regroup([sent] + [swapped(sent, "zh", 4, k) for k in (1, 2, 3)])
    mine = [mine[0]] + [swapped(mine[k], "y", 4, k) for k in (1, 2, 3)]
    entries = mine + [swapped(part, "c", 2, 1) for part in mine]
    fresh, smooth = decode(entries, weight, basis)
    fresh = fresh[None]
    held = join([fresh, swapped(fresh, "zl", 2, 1)], "join_near")
    held = join([held] + [crossed(held, 0, k) for k in (1, 2, 3)], "join_far")
    parts = [held] + [crossed(held, 1, k) for k in (1, 2, 3)]
    new_weight = assemble(parts + [swapped(part, "c", 2, 1) for part in parts])
    smooths = [smooth] + [swapped(smooth, "y", 4, k) for k in (1, 2, 3)]
    direction = lay(smooths + [swapped(part, "c", 2, 1) for part in smooths])
    kept_state = kept(momentum[0], grad[0], sent, basis)
    return (kept_state[None], direction, new_weight)


def solution(mesh):
    split = Mesh(mesh.devices.reshape(4, 4, 2, 4, 2), ("zh", "y", "c", "x", "zl"))
    in_specs = (
        P(None, SHARD),
        P(REPLICA, None, SHARD),
        P(REPLICA, None, SHARD),
        P(REPLICA, None, SHARD, None),
    )
    out_specs = (P(REPLICA, None, SHARD), P(None, SHARD), P())
    return jax.shard_map(
        per_device, mesh=split, in_specs=in_specs, out_specs=out_specs, check_vma=False
    )
```

time: 220 us -> 232 us (1.055)
  Pallas kernels: 0 us -> 151 us
  blocking collectives: 60.4 us -> 0 us
  waiting for transfers between devices: 77 us -> 23.3 us
  starting transfers between devices: 0.04 us -> 52.7 us
  local copies, waits for them, and re-layouts: 27.2 us -> 3.66 us
  other arithmetic: 23.1 us -> 0 us
  matrix products: 17.4 us -> 0 us
  between operations: 14.2 us -> 1 us
    pallas_call x0 -> x8, Pallas kernels: none -> 151 us  [the longest x1 129 us: assemble(): pl.pallas_call(assemble_kernel, in_specs=[ANY] * 8, out_specs=ANY, out_sh...]
    all_gather x1 -> x0, waiting for transfers between devices: 77 us -> none  [per_device(): new_weight = lax.all_gather(updated, 'shard', axis=1, tiled=True)]
    all_to_all x4 -> x0, blocking collectives: 60.4 us -> none  [the longest x2 27.6 us: copy_for_each(): return lax.all_to_all(copies, axis, split_axis=0, concat_axis=0, tiled=True)]
    ppermute x0 -> x28, starting transfers between devices: none -> 52.7 us  [the longest x22 44.9 us: swapped(): return lax.ppermute(array, axis, [(i, i ^ k) for i in range(size)])]
    ppermute x0 -> x28, waiting for transfers between devices: none -> 23.3 us  [the longest x22 18.1 us: swapped(): return lax.ppermute(array, axis, [(i, i ^ k) for i in range(size)])]
    dot_general x6 -> x0, matrix products: 17.4 us -> none  [the longest x2 6.6 us: decode(): jnp.einsum('ai,xyab,bj->xiyj', basis_table, square, basis_table, precisio...]
    unnamed x4 -> x0, other arithmetic: 12.4 us -> none
    another operation x2 -> x0, local copies, waits for them, and re-layouts: 5.93 us -> none  [the longest x1 3.18 us: decode(): square = grid.reshape(row_blocks, col_blocks, GROUP, GROUP)]
  transfers between devices with their start and end apart: 1 -> 28, of which waited for: 1 -> 13; matrix products, arithmetic and copies ran while one was open for 6% -> 0% of each run, Pallas kernels for 0% -> 3%
where the time goes in v1:
time: 232 us
  Pallas kernels  151 us (65%)
  starting transfers between devices  52.7 us (23%)
  waiting for transfers between devices  23.3 us (10%)
  local copies, waits for them, and re-layouts  3.66 us (2%)
    pallas_call x1, Pallas kernels, assemble(): pl.pallas_call(assemble_kernel, in_specs=[ANY] * 8, out_specs=ANY, out_sh...  129 us
    ppermute x22, starting transfers between devices, swapped(): return lax.ppermute(array, axis, [(i, i ^ k) for i in range(size)])  44.9 us
    ppermute x22, waiting for transfers between devices, swapped(): return lax.ppermute(array, axis, [(i, i ^ k) for i in range(size)])  18.1 us
    ppermute x6, starting transfers between devices, crossed(): return lax.ppermute(array, ('y', 'c', 'x'), perm)  7.81 us
    pallas_call x1, Pallas kernels, kept(): pl.pallas_call(kept_kernel, grid=(4,), in_specs=[pl.BlockSpec((256, 256),...  5.9 us
    pallas_call x1, Pallas kernels, extract(): pl.pallas_call(extract_kernel, grid=(4,), in_specs=[pl.BlockSpec((256, 25...  5.31 us
    ppermute x6, waiting for transfers between devices, crossed(): return lax.ppermute(array, ('y', 'c', 'x'), perm)  5.2 us
  transfers between devices with their start and end apart: 28, of which 13 were waited for; matrix products, arithmetic and copies ran while one was open for 0% of the time, Pallas kernels for 3%

profile of v1, /device:TPU:1, one launch (start us, length us, event | category | flops | bytes accessed | tf_op | source)
XLA Modules:
  0.0 231.7 jit_solution(7280651255527999363)
XLA Ops:
  0.6 5.3 %extract.1.sent.a = f32[32,128]{1,0:T(8,128)} custom-call(f32[256,1024]{1,0:T(8,128)} %bitcast.7, bf16[256,1024]{1,0:T(8,128)(2,1)} %bitcast.9, s32[4,16,32]{2,1,0:T(8,128)} %bitcast.11, bf16[256,256]{1,0:T(8,128)(2,1)} %constant.8.clone.bh.refs_9_, bf16[256,256]{1,0:T(8,128)(2,1)} %constant.9.clone.bl.refs_10_), custom_call_target="tpu_custom_call" | custom-call | flops 1000000000 | bytes 2097152 | tf_op jit(solution)/shard_map/extract/pallas_call | solution.py:95
  5.9 3.8 %collective-permute-start = (f32[32,128]{1,0:T(8,128)}, f32[32,128]{1,0:T(8,128)S(1)}, u32[]{:S(2)}, u32[]{:S(2)}) collective-permute-start(f32[32,128]{1,0:T(8,128)} %extract.1.sent.a), channel_id=1, source_target_pairs={{0,64},{64,0},{128,192},{192,128},{1,65},{65,1},{129,193},{193,129... | collective-permute-start | bytes 49160 | tf_op jit(solution)/shard_map/ppermute | solution.py:277
  9.8 5.1 %collective-permute-start.1 = (f32[32,128]{1,0:T(8,128)}, f32[32,128]{1,0:T(8,128)S(1)}, u32[]{:S(2)}, u32[]{:S(2)}) collective-permute-start(f32[32,128]{1,0:T(8,128)} %extract.1.sent.a), channel_id=1, source_target_pairs={{0,128},{64,192},{128,0},{192,64},{1,129},{65,193},{129,1},{193,65... | collective-permute-start | bytes 49160 | tf_op jit(solution)/shard_map/ppermute | solution.py:277
  14.9 0.0 collective-permute-done.b
  14.9 1.6 collective-permute-done.1.c
  16.5 3.3 %collective-permute-done.2.d = f32[32,128]{1,0:T(8,128)S(1)} collective-permute-done((f32[32,128]{1,0:T(8,128)}, f32[32,128]{1,0:T(8,128)S(1)}, u32[]{:S(2)}, u32[]{:S(2)}) %collective-permute-start.2) | collective-permute-done | bytes 16416 | tf_op jit(solution)/shard_map/ppermute | solution.py:277
  19.8 0.6 copy-done.18
  20.4 1.4 regroup.1
  21.8 1.3 collective-permute-start.3
  23.1 2.6 %collective-permute-start.4 = (f32[32,128]{1,0:T(8,128)}, f32[32,128]{1,0:T(8,128)S(1)}, u32[]{:S(2)}, u32[]{:S(2)}) collective-permute-start(f32[32,128]{1,0:T(8,128)} %get-tuple-element.11), channel_id=1, source_target_pairs={{0,32},{16,48},{32,0},{48,16},{1,33},{17,49},{33,1},{49,17},{2,34}... | collective-permute-start | bytes 49160 | tf_op jit(solution)/shard_map/ppermute | solution.py:277
  25.7 3.2 %collective-permute-start.6 = (f32[32,128]{1,0:T(8,128)}, f32[32,128]{1,0:T(8,128)S(1)}, u32[]{:S(2)}, u32[]{:S(2)}) collective-permute-start(f32[32,128]{1,0:T(8,128)} %get-tuple-element.9.refs_0_), channel_id=1, source_target_pairs={{0,8},{8,0},{1,9},{9,1},{2,10},{10,2},{3,11},{11,3},{4,12},{12,4},... | collective-permute-start | bytes 49160 | tf_op jit(solution)/shard_map/ppermute | solution.py:277
  28.9 0.0 collective-permute-done.3.refs_1_
  28.9 0.1 collective-permute-start.7
  29.0 0.0 collective-permute-done.4.refs_2_
  29.0 2.2 collective-permute-start.8
  31.2 0.0 collective-permute-done.5.refs_3_
  31.2 2.6 %collective-permute-start.9 = (f32[32,128]{1,0:T(8,128)S(1)}, f32[32,128]{1,0:T(8,128)S(1)}, u32[]{:S(2)}, u32[]{:S(2)}) collective-permute-start(f32[32,128]{1,0:T(8,128)S(1)} %collective-permute-done.5.refs_3_), channel_id=1, source_target_pairs={{0,8},{8,0},{1,9},{9,1},{2,10},{10,2},{3,11},{11,3},{4,12},{12,4},... | collective-permute-start | bytes 49160 | tf_op jit(solution)/shard_map/ppermute | solution.py:277
  33.8 0.0 collective-permute-done.7.refs_5_
  33.8 0.0 collective-permute-done.8.refs_6_
  33.9 0.8 collective-permute-done.9.refs_7_
  34.7 0.6 copy-done.25
  35.3 4.2 %decode.1 = (bf16[256,128]{1,0:T(8,128)(2,1)}, bf16[256,128]{1,0:T(8,128)(2,1)}) custom-call(f32[32,128]{1,0:T(8,128)} %get-tuple-element.9.refs_0_, f32[32,128]{1,0:T(8,128)} %copy-done.19, f32[32,128]{1,0:T(8,128)} %copy-done.20, f32[32,128]{1,0:T(8,128)} %copy-done.21, f32[32,128]{1,0:T(8,128)} %copy-done.22, f32[32,128]{1,0:T(8,128)} %copy-done.23, ...), custom_call_target="tpu_custom_call" | custom-call | flops 1000000000 | bytes 1048576 | tf_op jit(solution)/shard_map/decode/pallas_call | solution.py:192
  39.5 0.8 collective-permute-start.17
  40.4 2.6 %collective-permute-done.17.refs_1_ = bf16[1,256,128]{2,1,0:T(8,128)(2,1)S(1)} collective-permute-done((bf16[1,256,128]{2,1,0:T(8,128)(2,1)}, bf16[1,256,128]{2,1,0:T(8,128)(2,1)S(1)}, u32[]{:S(2)}, u32[]{:S(2)}) %collective-permute-start.17) | collective-permute-done | bytes 65568 | tf_op jit(solution)/shard_map/ppermute | solution.py:277
  43.0 0.6 copy-done.15
  43.6 1.5 join_near.1.refs_0_
  45.1 0.0 collective-permute-start.18
  45.1 1.1 collective-permute-start.19
  46.3 2.7 %collective-permute-start.20 = (bf16[2,256,128]{2,1,0:T(8,128)(2,1)}, bf16[2,256,128]{2,1,0:T(8,128)(2,1)S(1)}, u32[]{:S(2)}, u32[]{:S(2)}) collective-permute-start(bf16[2,256,128]{2,1,0:T(8,128)(2,1)} %join_near.1.refs_0_), channel_id=1, source_target_pairs={{0,6},{2,4},{4,2},{6,0},{8,56},{10,58},{12,60},{14,62},{16,22},{18... | collective-permute-start | bytes 393224 | tf_op jit(solution)/shard_map/ppermute | solution.py:286
  49.0 0.2 collective-permute-done.18.refs_1_
  49.2 1.6 collective-permute-done.19.refs_2_
  50.7 1.4 collective-permute-done.20.refs_3_
  52.1 0.7 copy-done.8
  52.7 1.9 join_far.1.refs_0_
  54.6 1.2 collective-permute-start.21
  55.9 2.7 %collective-permute-start.22 = (bf16[8,256,128]{2,1,0:T(8,128)(2,1)}, bf16[8,256,128]{2,1,0:T(8,128)(2,1)S(1)}, u32[]{:S(2)}, u32[]{:S(2)}) collective-permute-start(bf16[8,256,128]{2,1,0:T(8,128)(2,1)} %join_far.1.refs_0_), channel_id=1, source_target_pairs={{0,32},{2,34},{4,36},{6,38},{8,12},{10,14},{12,8},{14,10},{16,48},... | collective-permute-start | bytes 1572872 | tf_op jit(solution)/shard_map/ppermute | solution.py:286
  58.6 0.9 collective-permute-start.10
  59.5 5.0 %collective-permute-start.24 = (bf16[8,256,128]{2,1,0:T(8,128)(2,1)}, bf16[8,256,128]{2,1,0:T(8,128)(2,1)S(1)}, u32[]{:S(2)}, u32[]{:S(2)}) collective-permute-start(bf16[8,256,128]{2,1,0:T(8,128)(2,1)} %join_far.1.refs_0_), channel_id=1, source_target_pairs={{0,8},{8,0},{1,9},{9,1},{2,10},{10,2},{3,11},{11,3},{4,12},{12,4},... | collective-permute-start | bytes 1572872 | tf_op jit(solution)/shard_map/ppermute | solution.py:277
  64.5 0.0 collective-permute-done.21.refs_1_
  64.5 4.7 %collective-permute-start.25 = (bf16[8,256,128]{2,1,0:T(8,128)(2,1)S(1)}, bf16[8,256,128]{2,1,0:T(8,128)(2,1)S(1)}, u32[]{:S(2)}, u32[]{:S(2)}) collective-permute-start(bf16[8,256,128]{2,1,0:T(8,128)(2,1)S(1)} %collective-permute-done.21.refs_1_), channel_id=1, source_target_pairs={{0,8},{8,0},{1,9},{9,1},{2,10},{10,2},{3,11},{11,3},{4,12},{12,4},... | collective-permute-start | bytes 1572872 | tf_op jit(solution)/shard_map/ppermute | solution.py:277
  69.2 2.1 collective-permute-done.22.refs_2_
  71.3 4.0 %collective-permute-start.26 = (bf16[8,256,128]{2,1,0:T(8,128)(2,1)S(1)}, bf16[8,256,128]{2,1,0:T(8,128)(2,1)S(1)}, u32[]{:S(2)}, u32[]{:S(2)}) collective-permute-start(bf16[8,256,128]{2,1,0:T(8,128)(2,1)S(1)} %collective-permute-done.22.refs_2_), channel_id=1, source_target_pairs={{0,8},{8,0},{1,9},{9,1},{2,10},{10,2},{3,11},{11,3},{4,12},{12,4},... | collective-permute-start | bytes 1572872 | tf_op jit(solution)/shard_map/ppermute | solution.py:277
  75.3 0.0 collective-permute-done.23.refs_3_
  75.3 2.4 %collective-permute-start.27 = (bf16[8,256,128]{2,1,0:T(8,128)(2,1)S(1)}, bf16[8,256,128]{2,1,0:T(8,128)(2,1)}, u32[]{:S(2)}, u32[]{:S(2)}) collective-permute-start(bf16[8,256,128]{2,1,0:T(8,128)(2,1)S(1)} %collective-permute-done.23.refs_3_), channel_id=1, source_target_pairs={{0,8},{8,0},{1,9},{9,1},{2,10},{10,2},{3,11},{11,3},{4,12},{12,4},... | collective-permute-start | bytes 1572872 | tf_op jit(solution)/shard_map/ppermute | solution.py:277
  77.7 0.0 collective-permute-done.10.refs_1_
  77.7 0.4 collective-permute-start.11
  78.1 5.0 %collective-permute-done.11.refs_2_ = bf16[256,128]{1,0:T(8,128)(2,1)S(1)} collective-permute-done((bf16[256,128]{1,0:T(8,128)(2,1)}, bf16[256,128]{1,0:T(8,128)(2,1)S(1)}, u32[]{:S(2)}, u32[]{:S(2)}) %collective-permute-start.11) | collective-permute-done | bytes 65568 | tf_op jit(solution)/shard_map/ppermute | solution.py:277
  83.1 2.7 %collective-permute-start.12 = (bf16[256,128]{1,0:T(8,128)(2,1)}, bf16[256,128]{1,0:T(8,128)(2,1)S(1)}, u32[]{:S(2)}, u32[]{:S(2)}) collective-permute-start(bf16[256,128]{1,0:T(8,128)(2,1)} %get-tuple-element.13.refs_0_), channel_id=1, source_target_pairs={{0,48},{16,32},{32,16},{48,0},{1,49},{17,33},{33,17},{49,1},{2,50}... | collective-permute-start | bytes 196616 | tf_op jit(solution)/shard_map/ppermute | solution.py:277
  85.8 1.9 collective-permute-done.12.refs_3_
  87.7 2.0 collective-permute-start.13
  89.7 1.1 collective-permute-done.13.refs_4_
  90.8 0.4 collective-permute-start.14
  91.1 0.9 collective-permute-done.14.refs_5_
  92.0 0.4 collective-permute-start.15
  92.4 0.9 collective-permute-done.15.refs_6_
  93.3 0.4 collective-permute-start.16
  93.6 5.9 %kept.1 = f32[256,1024]{1,0:T(8,128)} custom-call(f32[256,1024]{1,0:T(8,128)} %bitcast.8, bf16[256,1024]{1,0:T(8,128)(2,1)} %bitcast.10, f32[32,128]{1,0:T(8,128)} %extract.1.sent.a, bf16[256,256]{1,0:T(8,128)(2,1)} %constant.8.clone.bh.refs_9_, bf16[256,256]{1,0:T(8,128)(2,1)} %constant.9.clone.bl.refs_10_, bf16[256,256]{1,0:T(8,128)(2,1)} %constant.10.clone.th.refs_11_, ...), custom_call_target="tpu_custom_call" | custom-call | flops 2000000000 | bytes 3145728 | tf_op jit(solution)/shard_map/kept/pallas_call | solution.py:134
  99.6 0.0 collective-permute-done.16.refs_7_
  99.6 2.0 lay.1
  101.6 0.0 collective-permute-done.24.refs_4_
  101.7 0.7 copy-done.3
  102.4 0.2 copy-done.4
  102.6 0.2 copy-done.5
  102.8 128.7 %assemble.1 = bf16[256,8192]{1,0:T(8,128)(2,1)} custom-call(bf16[8,256,128]{2,1,0:T(8,128)(2,1)} %join_far.1.refs_0_, bf16[8,256,128]{2,1,0:T(8,128)(2,1)} %copy-done, bf16[8,256,128]{2,1,0:T(8,128)(2,1)} %copy-done.1, bf16[8,256,128]{2,1,0:T(8,128)(2,1)} %copy-done.2, bf16[8,256,128]{2,1,0:T(8,128)(2,1)} %copy-done.3, bf16[8,256,128]{2,1,0:T(8,128)(2,1)} %copy-done.4, ...), custom_call_target="tpu_custom_call" | custom-call | tf_op jit(solution)/shard_map/assemble/pallas_call | solution.py:247
  (52 shorter events, 0.1 us)
Async XLA Ops:
  5.9 8.9 %collective-permute-start = (f32[32,128]{1,0:T(8,128)}, f32[32,128]{1,0:T(8,128)S(1)}, u32[]{:S(2)}, u32[]{:S(2)}) collective-permute-start(f32[32,128]{1,0:T(8,128)} %extract.1.sent.a), channel_id=1, source_target_pairs={{0,64},{64,0},{128,192},{192,128},{1,65},{65,1},{129,193},{193,129... | collective-permute-start | bytes 49160 | tf_op jit(solution)/shard_map/ppermute | solution.py:277
  9.8 6.7 %collective-permute-start.1 = (f32[32,128]{1,0:T(8,128)}, f32[32,128]{1,0:T(8,128)S(1)}, u32[]{:S(2)}, u32[]{:S(2)}) collective-permute-start(f32[32,128]{1,0:T(8,128)} %extract.1.sent.a), channel_id=1, source_target_pairs={{0,128},{64,192},{128,0},{192,64},{1,129},{65,193},{129,1},{193,65... | collective-permute-start | bytes 49160 | tf_op jit(solution)/shard_map/ppermute | solution.py:277
  14.9 4.9 %collective-permute-start.2 = (f32[32,128]{1,0:T(8,128)}, f32[32,128]{1,0:T(8,128)S(1)}, u32[]{:S(2)}, u32[]{:S(2)}) collective-permute-start(f32[32,128]{1,0:T(8,128)} %extract.1.sent.a), channel_id=1, source_target_pairs={{0,192},{64,128},{128,64},{192,0},{1,193},{65,129},{129,65},{193,1... | collective-permute-start | bytes 49160 | tf_op jit(solution)/shard_map/ppermute | solution.py:277
  14.9 4.9 %copy-start.16 = (f32[32,128]{1,0:T(8,128)}, f32[32,128]{1,0:T(8,128)S(1)}, u32[]{:S(2)}) copy-start(f32[32,128]{1,0:T(8,128)S(1)} %collective-permute-done.b) | copy-start | bytes 49156
  16.5 3.3 %copy-start.17 = (f32[32,128]{1,0:T(8,128)}, f32[32,128]{1,0:T(8,128)S(1)}, u32[]{:S(2)}) copy-start(f32[32,128]{1,0:T(8,128)S(1)} %collective-permute-done.1.c) | copy-start | bytes 49156
  19.8 0.6 copy-start.18
  21.8 7.1 %collective-permute-start.3 = (f32[32,128]{1,0:T(8,128)}, f32[32,128]{1,0:T(8,128)S(1)}, u32[]{:S(2)}, u32[]{:S(2)}) collective-permute-start(f32[32,128]{1,0:T(8,128)} %get-tuple-element.10), channel_id=1, source_target_pairs={{0,16},{16,0},{32,48},{48,32},{1,17},{17,1},{33,49},{49,33},{2,18}... | collective-permute-start | bytes 49160 | tf_op jit(solution)/shard_map/ppermute | solution.py:277
  23.1 5.9 %collective-permute-start.4 = (f32[32,128]{1,0:T(8,128)}, f32[32,128]{1,0:T(8,128)S(1)}, u32[]{:S(2)}, u32[]{:S(2)}) collective-permute-start(f32[32,128]{1,0:T(8,128)} %get-tuple-element.11), channel_id=1, source_target_pairs={{0,32},{16,48},{32,0},{48,16},{1,33},{17,49},{33,1},{49,17},{2,34}... | collective-permute-start | bytes 49160 | tf_op jit(solution)/shard_map/ppermute | solution.py:277
  25.7 5.5 %collective-permute-start.5 = (f32[32,128]{1,0:T(8,128)}, f32[32,128]{1,0:T(8,128)S(1)}, u32[]{:S(2)}, u32[]{:S(2)}) collective-permute-start(f32[32,128]{1,0:T(8,128)} %get-tuple-element.12), channel_id=1, source_target_pairs={{0,48},{16,32},{32,16},{48,0},{1,49},{17,33},{33,17},{49,1},{2,50}... | collective-permute-start | bytes 49160 | tf_op jit(solution)/shard_map/ppermute | solution.py:277
  25.7 8.1 %collective-permute-start.6 = (f32[32,128]{1,0:T(8,128)}, f32[32,128]{1,0:T(8,128)S(1)}, u32[]{:S(2)}, u32[]{:S(2)}) collective-permute-start(f32[32,128]{1,0:T(8,128)} %get-tuple-element.9.refs_0_), channel_id=1, source_target_pairs={{0,8},{8,0},{1,9},{9,1},{2,10},{10,2},{3,11},{11,3},{4,12},{12,4},... | collective-permute-start | bytes 49160 | tf_op jit(solution)/shard_map/ppermute | solution.py:277
  28.9 5.8 %copy-start.19 = (f32[32,128]{1,0:T(8,128)}, f32[32,128]{1,0:T(8,128)S(1)}, u32[]{:S(2)}) copy-start(f32[32,128]{1,0:T(8,128)S(1)} %collective-permute-done.3.refs_1_) | copy-start | bytes 49156
  28.9 4.9 %collective-permute-start.7 = (f32[32,128]{1,0:T(8,128)S(1)}, f32[32,128]{1,0:T(8,128)S(1)}, u32[]{:S(2)}, u32[]{:S(2)}) collective-permute-start(f32[32,128]{1,0:T(8,128)S(1)} %collective-permute-done.3.refs_1_), channel_id=1, source_target_pairs={{0,8},{8,0},{1,9},{9,1},{2,10},{10,2},{3,11},{11,3},{4,12},{12,4},... | collective-permute-start | bytes 49160 | tf_op jit(solution)/shard_map/ppermute | solution.py:277
  29.0 5.7 %copy-start.20 = (f32[32,128]{1,0:T(8,128)}, f32[32,128]{1,0:T(8,128)S(1)}, u32[]{:S(2)}) copy-start(f32[32,128]{1,0:T(8,128)S(1)} %collective-permute-done.4.refs_2_) | copy-start | bytes 49156
  29.0 4.9 %collective-permute-start.8 = (f32[32,128]{1,0:T(8,128)S(1)}, f32[32,128]{1,0:T(8,128)S(1)}, u32[]{:S(2)}, u32[]{:S(2)}) collective-permute-start(f32[32,128]{1,0:T(8,128)S(1)} %collective-permute-done.4.refs_2_), channel_id=1, source_target_pairs={{0,8},{8,0},{1,9},{9,1},{2,10},{10,2},{3,11},{11,3},{4,12},{12,4},... | collective-permute-start | bytes 49160 | tf_op jit(solution)/shard_map/ppermute | solution.py:277
  31.2 3.5 %copy-start.21 = (f32[32,128]{1,0:T(8,128)}, f32[32,128]{1,0:T(8,128)S(1)}, u32[]{:S(2)}) copy-start(f32[32,128]{1,0:T(8,128)S(1)} %collective-permute-done.5.refs_3_) | copy-start | bytes 49156
  31.2 3.4 %collective-permute-start.9 = (f32[32,128]{1,0:T(8,128)S(1)}, f32[32,128]{1,0:T(8,128)S(1)}, u32[]{:S(2)}, u32[]{:S(2)}) collective-permute-start(f32[32,128]{1,0:T(8,128)S(1)} %collective-permute-done.5.refs_3_), channel_id=1, source_target_pairs={{0,8},{8,0},{1,9},{9,1},{2,10},{10,2},{3,11},{11,3},{4,12},{12,4},... | collective-permute-start | bytes 49160 | tf_op jit(solution)/shard_map/ppermute | solution.py:277
  33.8 0.8 copy-start.22
  33.8 0.8 copy-start.23
  33.9 0.8 copy-start.24
  34.7 0.6 copy-start.25
  39.5 3.4 %collective-permute-start.17 = (bf16[1,256,128]{2,1,0:T(8,128)(2,1)}, bf16[1,256,128]{2,1,0:T(8,128)(2,1)S(1)}, u32[]{:S(2)}, u32[]{:S(2)}) collective-permute-start(bf16[1,256,128]{2,1,0:T(8,128)(2,1)} %bitcast.5), channel_id=1, source_target_pairs={{0,1},{1,0},{2,3},{3,2},{4,5},{5,4},{6,7},{7,6},{8,9},{9,8},{10,11... | collective-permute-start | bytes 196616 | tf_op jit(solution)/shard_map/ppermute | solution.py:277
  43.0 0.6 copy-start.15
  45.1 4.0 %collective-permute-start.18 = (bf16[2,256,128]{2,1,0:T(8,128)(2,1)}, bf16[2,256,128]{2,1,0:T(8,128)(2,1)S(1)}, u32[]{:S(2)}, u32[]{:S(2)}) collective-permute-start(bf16[2,256,128]{2,1,0:T(8,128)(2,1)} %join_near.1.refs_0_), channel_id=1, source_target_pairs={{0,2},{2,0},{4,6},{6,4},{8,24},{10,26},{12,28},{14,30},{16,18},{18... | collective-permute-start | bytes 393224 | tf_op jit(solution)/shard_map/ppermute | solution.py:286
  45.1 5.6 %collective-permute-start.19 = (bf16[2,256,128]{2,1,0:T(8,128)(2,1)}, bf16[2,256,128]{2,1,0:T(8,128)(2,1)S(1)}, u32[]{:S(2)}, u32[]{:S(2)}) collective-permute-start(bf16[2,256,128]{2,1,0:T(8,128)(2,1)} %join_near.1.refs_0_), channel_id=1, source_target_pairs={{0,4},{2,6},{4,0},{6,2},{8,40},{10,42},{12,44},{14,46},{16,20},{18... | collective-permute-start | bytes 393224 | tf_op jit(solution)/shard_map/ppermute | solution.py:286
  46.3 5.8 %collective-permute-start.20 = (bf16[2,256,128]{2,1,0:T(8,128)(2,1)}, bf16[2,256,128]{2,1,0:T(8,128)(2,1)S(1)}, u32[]{:S(2)}, u32[]{:S(2)}) collective-permute-start(bf16[2,256,128]{2,1,0:T(8,128)(2,1)} %join_near.1.refs_0_), channel_id=1, source_target_pairs={{0,6},{2,4},{4,2},{6,0},{8,56},{10,58},{12,60},{14,62},{16,22},{18... | collective-permute-start | bytes 393224 | tf_op jit(solution)/shard_map/ppermute | solution.py:286
  49.2 2.9 %copy-start.6 = (bf16[2,256,128]{2,1,0:T(8,128)(2,1)}, bf16[2,256,128]{2,1,0:T(8,128)(2,1)S(1)}, u32[]{:S(2)}) copy-start(bf16[2,256,128]{2,1,0:T(8,128)(2,1)S(1)} %collective-permute-done.18.refs_1_) | copy-start | bytes 393220
  50.7 1.4 copy-start.7
  52.1 0.7 copy-start.8
  54.6 9.9 %collective-permute-start.21 = (bf16[8,256,128]{2,1,0:T(8,128)(2,1)}, bf16[8,256,128]{2,1,0:T(8,128)(2,1)S(1)}, u32[]{:S(2)}, u32[]{:S(2)}) collective-permute-start(bf16[8,256,128]{2,1,0:T(8,128)(2,1)} %join_far.1.refs_0_), channel_id=1, source_target_pairs={{0,16},{2,18},{4,20},{6,22},{8,10},{10,8},{12,14},{14,12},{16,0},{... | collective-permute-start | bytes 1572872 | tf_op jit(solution)/shard_map/ppermute | solution.py:286
  55.9 15.5 %collective-permute-start.22 = (bf16[8,256,128]{2,1,0:T(8,128)(2,1)}, bf16[8,256,128]{2,1,0:T(8,128)(2,1)S(1)}, u32[]{:S(2)}, u32[]{:S(2)}) collective-permute-start(bf16[8,256,128]{2,1,0:T(8,128)(2,1)} %join_far.1.refs_0_), channel_id=1, source_target_pairs={{0,32},{2,34},{4,36},{6,38},{8,12},{10,14},{12,8},{14,10},{16,48},... | collective-permute-start | bytes 1572872 | tf_op jit(solution)/shard_map/ppermute | solution.py:286
  58.6 16.7 %collective-permute-start.23 = (bf16[8,256,128]{2,1,0:T(8,128)(2,1)}, bf16[8,256,128]{2,1,0:T(8,128)(2,1)S(1)}, u32[]{:S(2)}, u32[]{:S(2)}) collective-permute-start(bf16[8,256,128]{2,1,0:T(8,128)(2,1)} %join_far.1.refs_0_), channel_id=1, source_target_pairs={{0,48},{2,50},{4,52},{6,54},{8,14},{10,12},{12,10},{14,8},{16,32},... | collective-permute-start | bytes 1572872 | tf_op jit(solution)/shard_map/ppermute | solution.py:286
  58.6 19.1 %collective-permute-start.10 = (bf16[256,128]{1,0:T(8,128)(2,1)}, bf16[256,128]{1,0:T(8,128)(2,1)S(1)}, u32[]{:S(2)}, u32[]{:S(2)}) collective-permute-start(bf16[256,128]{1,0:T(8,128)(2,1)} %get-tuple-element.13.refs_0_), channel_id=1, source_target_pairs={{0,16},{16,0},{32,48},{48,32},{1,17},{17,1},{33,49},{49,33},{2,18}... | collective-permute-start | bytes 196616 | tf_op jit(solution)/shard_map/ppermute | solution.py:277
  59.5 42.1 %collective-permute-start.24 = (bf16[8,256,128]{2,1,0:T(8,128)(2,1)}, bf16[8,256,128]{2,1,0:T(8,128)(2,1)S(1)}, u32[]{:S(2)}, u32[]{:S(2)}) collective-permute-start(bf16[8,256,128]{2,1,0:T(8,128)(2,1)} %join_far.1.refs_0_), channel_id=1, source_target_pairs={{0,8},{8,0},{1,9},{9,1},{2,10},{10,2},{3,11},{11,3},{4,12},{12,4},... | collective-permute-start | bytes 1572872 | tf_op jit(solution)/shard_map/ppermute | solution.py:277
  64.5 37.1 %copy-start = (bf16[8,256,128]{2,1,0:T(8,128)(2,1)}, bf16[8,256,128]{2,1,0:T(8,128)(2,1)S(1)}, u32[]{:S(2)}) copy-start(bf16[8,256,128]{2,1,0:T(8,128)(2,1)S(1)} %collective-permute-done.21.refs_1_) | copy-start | bytes 1572868
  64.5 37.1 %collective-permute-start.25 = (bf16[8,256,128]{2,1,0:T(8,128)(2,1)S(1)}, bf16[8,256,128]{2,1,0:T(8,128)(2,1)S(1)}, u32[]{:S(2)}, u32[]{:S(2)}) collective-permute-start(bf16[8,256,128]{2,1,0:T(8,128)(2,1)S(1)} %collective-permute-done.21.refs_1_), channel_id=1, source_target_pairs={{0,8},{8,0},{1,9},{9,1},{2,10},{10,2},{3,11},{11,3},{4,12},{12,4},... | collective-permute-start | bytes 1572872 | tf_op jit(solution)/shard_map/ppermute | solution.py:277
  71.3 30.3 %copy-start.1 = (bf16[8,256,128]{2,1,0:T(8,128)(2,1)}, bf16[8,256,128]{2,1,0:T(8,128)(2,1)S(1)}, u32[]{:S(2)}) copy-start(bf16[8,256,128]{2,1,0:T(8,128)(2,1)S(1)} %collective-permute-done.22.refs_2_) | copy-start | bytes 1572868
  71.3 30.3 %collective-permute-start.26 = (bf16[8,256,128]{2,1,0:T(8,128)(2,1)S(1)}, bf16[8,256,128]{2,1,0:T(8,128)(2,1)S(1)}, u32[]{:S(2)}, u32[]{:S(2)}) collective-permute-start(bf16[8,256,128]{2,1,0:T(8,128)(2,1)S(1)} %collective-permute-done.22.refs_2_), channel_id=1, source_target_pairs={{0,8},{8,0},{1,9},{9,1},{2,10},{10,2},{3,11},{11,3},{4,12},{12,4},... | collective-permute-start | bytes 1572872 | tf_op jit(solution)/shard_map/ppermute | solution.py:277
  75.3 26.3 %copy-start.2 = (bf16[8,256,128]{2,1,0:T(8,128)(2,1)}, bf16[8,256,128]{2,1,0:T(8,128)(2,1)S(1)}, u32[]{:S(2)}) copy-start(bf16[8,256,128]{2,1,0:T(8,128)(2,1)S(1)} %collective-permute-done.23.refs_3_) | copy-start | bytes 1572868
  75.3 26.4 %collective-permute-start.27 = (bf16[8,256,128]{2,1,0:T(8,128)(2,1)S(1)}, bf16[8,256,128]{2,1,0:T(8,128)(2,1)}, u32[]{:S(2)}, u32[]{:S(2)}) collective-permute-start(bf16[8,256,128]{2,1,0:T(8,128)(2,1)S(1)} %collective-permute-done.23.refs_3_), channel_id=1, source_target_pairs={{0,8},{8,0},{1,9},{9,1},{2,10},{10,2},{3,11},{11,3},{4,12},{12,4},... | collective-permute-start | bytes 1572872 | tf_op jit(solution)/shard_map/ppermute | solution.py:277
  77.7 21.8 %copy-start.9 = (bf16[256,128]{1,0:T(8,128)(2,1)}, bf16[256,128]{1,0:T(8,128)(2,1)S(1)}, u32[]{:S(2)}) copy-start(bf16[256,128]{1,0:T(8,128)(2,1)S(1)} %collective-permute-done.10.refs_1_) | copy-start | bytes 196612
  77.7 5.4 %collective-permute-start.11 = (bf16[256,128]{1,0:T(8,128)(2,1)}, bf16[256,128]{1,0:T(8,128)(2,1)S(1)}, u32[]{:S(2)}, u32[]{:S(2)}) collective-permute-start(bf16[256,128]{1,0:T(8,128)(2,1)} %get-tuple-element.13.refs_0_), channel_id=1, source_target_pairs={{0,32},{16,48},{32,0},{48,16},{1,33},{17,49},{33,1},{49,17},{2,34}... | collective-permute-start | bytes 196616 | tf_op jit(solution)/shard_map/ppermute | solution.py:277
  83.1 16.5 %copy-start.10 = (bf16[256,128]{1,0:T(8,128)(2,1)}, bf16[256,128]{1,0:T(8,128)(2,1)S(1)}, u32[]{:S(2)}) copy-start(bf16[256,128]{1,0:T(8,128)(2,1)S(1)} %collective-permute-done.11.refs_2_) | copy-start | bytes 196612
  83.1 4.6 %collective-permute-start.12 = (bf16[256,128]{1,0:T(8,128)(2,1)}, bf16[256,128]{1,0:T(8,128)(2,1)S(1)}, u32[]{:S(2)}, u32[]{:S(2)}) collective-permute-start(bf16[256,128]{1,0:T(8,128)(2,1)} %get-tuple-element.13.refs_0_), channel_id=1, source_target_pairs={{0,48},{16,32},{32,16},{48,0},{1,49},{17,33},{33,17},{49,1},{2,50}... | collective-permute-start | bytes 196616 | tf_op jit(solution)/shard_map/ppermute | solution.py:277
  87.7 11.9 %copy-start.11 = (bf16[256,128]{1,0:T(8,128)(2,1)}, bf16[256,128]{1,0:T(8,128)(2,1)S(1)}, u32[]{:S(2)}) copy-start(bf16[256,128]{1,0:T(8,128)(2,1)S(1)} %collective-permute-done.12.refs_3_) | copy-start | bytes 196612
  87.7 3.1 %collective-permute-start.13 = (bf16[256,128]{1,0:T(8,128)(2,1)}, bf16[256,128]{1,0:T(8,128)(2,1)S(1)}, u32[]{:S(2)}, u32[]{:S(2)}) collective-permute-start(bf16[256,128]{1,0:T(8,128)(2,1)} %get-tuple-element.13.refs_0_), channel_id=1, source_target_pairs={{0,8},{8,0},{1,9},{9,1},{2,10},{10,2},{3,11},{11,3},{4,12},{12,4},... | collective-permute-start | bytes 196616 | tf_op jit(solution)/shard_map/ppermute | solution.py:277
  90.8 8.8 %copy-start.12 = (bf16[256,128]{1,0:T(8,128)(2,1)}, bf16[256,128]{1,0:T(8,128)(2,1)S(1)}, u32[]{:S(2)}) copy-start(bf16[256,128]{1,0:T(8,128)(2,1)S(1)} %collective-permute-done.13.refs_4_) | copy-start | bytes 196612
  90.8 1.3 collective-permute-start.14
  92.0 7.6 %copy-start.13 = (bf16[256,128]{1,0:T(8,128)(2,1)}, bf16[256,128]{1,0:T(8,128)(2,1)S(1)}, u32[]{:S(2)}) copy-start(bf16[256,128]{1,0:T(8,128)(2,1)S(1)} %collective-permute-done.14.refs_5_) | copy-start | bytes 196612
  92.0 1.3 collective-permute-start.15
  93.3 6.3 %copy-start.14 = (bf16[256,128]{1,0:T(8,128)(2,1)}, bf16[256,128]{1,0:T(8,128)(2,1)S(1)}, u32[]{:S(2)}) copy-start(bf16[256,128]{1,0:T(8,128)(2,1)S(1)} %collective-permute-done.15.refs_6_) | copy-start | bytes 196612
  93.3 6.3 %collective-permute-start.16 = (bf16[256,128]{1,0:T(8,128)(2,1)S(1)}, bf16[256,128]{1,0:T(8,128)(2,1)}, u32[]{:S(2)}, u32[]{:S(2)}) collective-permute-start(bf16[256,128]{1,0:T(8,128)(2,1)S(1)} %collective-permute-done.12.refs_3_), channel_id=1, source_target_pairs={{0,8},{8,0},{1,9},{9,1},{2,10},{10,2},{3,11},{11,3},{4,12},{12,4},... | collective-permute-start | bytes 196616 | tf_op jit(solution)/shard_map/ppermute | solution.py:277
  101.6 0.8 copy-start.3
  101.7 0.9 copy-start.4
  101.7 1.1 copy-start.5

commit v2 on v1

--- a/solution.py
+++ b/solution.py
@@ -20,6 +20,10 @@
 ANY = pl.BlockSpec(memory_space=pl.ANY)
 
 
+def limit(mib):
+    return pltpu.CompilerParams(vmem_limit_bytes=mib * 2**20)
+
+
 def basis_parts():
     freq, cells = np.arange(GROUP)[:, None], np.arange(GROUP)[None, :]
     scales = np.where(freq == 0, math.sqrt(1.0 / GROUP), math.sqrt(2.0 / GROUP))
@@ -64,7 +68,6 @@
 
 def extract_kernel(momentum, grad, positions, bh, bl, out, places):
     g = pl.program_id(0)
-    mine = lax.axis_index("y")
 
     @pl.when(g == 0)
     def _():
@@ -85,8 +88,9 @@
         line = lax.broadcasted_iota(jnp.int32, found.shape, 0)
         lines.append(jnp.sum(jnp.where(line == column, found, 0.0), axis=0, keepdims=True))
         lines.append(flat.astype(F32))
-    at = pl.multiple_of(8 * jnp.bitwise_xor(g, mine), 8)
-    out[pl.ds(at, 8), :] = jnp.concatenate(lines, axis=0)
+    tile = jnp.concatenate(lines, axis=0)
+    for z in range(4):
+        out[4 * z + g] = tile
 
 
 def extract(momentum, grad, positions, basis):
@@ -102,19 +106,17 @@
             whole(256, 256),
             whole(256, 256),
         ],
-        out_specs=whole(32, 128),
-        out_shape=jax.ShapeDtypeStruct((32, 128), F32),
+        out_specs=whole(16, 8, 128),
+        out_shape=jax.ShapeDtypeStruct((16, 8, 128), F32),
         scratch_shapes=[pltpu.VMEM((16, 128), jnp.int32)],
         cost_estimate=pl.CostEstimate(flops=10**9, bytes_accessed=2 * 2**20, transcendentals=0),
+        compiler_params=limit(12),
         name="extract",
     )(momentum, grad, positions, basis[0], basis[1])
 
 
 def kept_kernel(momentum, grad, sent, bh, bl, th, tl, out):
-    g = pl.program_id(0)
-    mine = lax.axis_index("y")
-    at = pl.multiple_of(8 * jnp.bitwise_xor(g, mine), 8)
-    tile = sent[pl.ds(at, 8), :]
+    tile = sent[0]
     blocks = []
     for q in range(4):
         row, column = split_place(tile[2 * q + 1 : 2 * q + 2].astype(jnp.int32))
@@ -134,40 +136,26 @@
     return pl.pallas_call(
         kept_kernel,
         grid=(4,),
-        in_specs=[pl.BlockSpec((256, 256), column)] * 2 + [whole(32, 128)] + [whole(256, 256)] * 4,
+        in_specs=[pl.BlockSpec((256, 256), column)] * 2 + [pl.BlockSpec((1, 8, 128), lambda g: (g, 0, 0))] + [whole(256, 256)] * 4,
         out_specs=pl.BlockSpec((256, 256), column),
         out_shape=jax.ShapeDtypeStruct((256, 1024), F32),
         cost_estimate=pl.CostEstimate(flops=2 * 10**9, bytes_accessed=3 * 2**20, transcendentals=0),
+        compiler_params=limit(12),
         name="kept",
     )(momentum, grad, sent, *basis)
 
 
-def regroup_kernel(a, b, c, d, *outs):
-    for k, out in enumerate(outs):
-        for z, ref in enumerate((a, b, c, d)):
-            out[8 * z : 8 * z + 8, :] = ref[8 * k : 8 * k + 8, :]
-
-
-def regroup(arrays):
-    return pl.pallas_call(
-        regroup_kernel,
-        in_specs=[VMEM] * 4,
-        out_specs=[VMEM] * 4,
-        out_shape=[jax.ShapeDtypeStruct((32, 128), F32)] * 4,
-        name="regroup",
-    )(*arrays)
-
-
 def decode_kernel(*refs):
-    entries, (weight, bh, bl, th, tl), (fresh, smooth_out, staged, sem) = refs[:8], refs[8:13], refs[13:]
+    entries, (weight, bh, bl, th, tl), (fresh, smooth_out, staged, sem) = refs[:2], refs[2:7], refs[7:]
     core = lax.axis_index("c")
     place = pl.multiple_of((lax.axis_index("y") * 2 + core) * 128, 128)
     copy = pltpu.make_async_copy(weight.at[:, pl.ds(place, 128)], staged, sem)
     copy.start()
     tiles = []
     for ref in entries:
-        for z in range(4):
-            tiles.append(jnp.where(core == 0, ref[8 * z : 8 * z + 4, :], ref[8 * z + 4 : 8 * z + 8, :]))
+        for source in range(16):
+            tile = ref[source]
+            tiles.append(jnp.where(core == 0, tile[:4], tile[4:]))
     blocks = []
     for j in range(2):
         total = jnp.zeros((2 * GROUP, 4 * GROUP), F32)
@@ -183,50 +171,48 @@
     half = product(rows_by_rows, (th[...], tl[...]), grid)
     dense = product(rows_by_cols, two_parts(half), (bh[:128, :128], bl[:128, :128]))
     smooth = jnp.tanh(dense)
-    smooth_out[...] = smooth.astype(BF16)
+    smooth_out[0] = smooth.astype(BF16)
     copy.wait()
-    fresh[...] = (staged[...].astype(F32) - step_rate * smooth).astype(BF16)
+    fresh[0] = (staged[...].astype(F32) - step_rate * smooth).astype(BF16)
 
 
 def decode(entries, weight, basis):
     return pl.pallas_call(
         decode_kernel,
-        in_specs=[VMEM] * 8 + [ANY] + [VMEM] * 4,
+        in_specs=[VMEM] * 2 + [ANY] + [VMEM] * 4,
         out_specs=[VMEM] * 2,
-        out_shape=[jax.ShapeDtypeStruct((256, 128), BF16)] * 2,
+        out_shape=[jax.ShapeDtypeStruct((1, 256, 128), BF16)] * 2,
         scratch_shapes=[pltpu.VMEM((256, 128), BF16), pltpu.SemaphoreType.DMA],
         cost_estimate=pl.CostEstimate(flops=10**9, bytes_accessed=2**20, transcendentals=32768),
+        compiler_params=limit(12),
         name="decode",
     )(*entries, weight, *basis)
 
 
-def join_kernel(*refs):
+def join_kernel(size, *refs):
     out = refs[-1]
-    at = 0
-    for ref in refs[:-1]:
-        size = ref.shape[0]
-        out[at : at + size] = ref[...]
-        at += size
-
-
-def join(arrays, name):
-    total = sum(array.shape[0] for array in arrays)
-    return pl.pallas_call(
-        join_kernel,
+    for k, ref in enumerate(refs[:-1]):
+        out[size * k : size * (k + 1)] = ref[:size]
+
+
+def join(arrays, size, name):
+    return pl.pallas_call(
+        functools.partial(join_kernel, size),
         in_specs=[VMEM] * len(arrays),
         out_specs=VMEM,
-        out_shape=jax.ShapeDtypeStruct((total, *arrays[0].shape[1:]), arrays[0].dtype),
+        out_shape=jax.ShapeDtypeStruct((size * len(arrays), 256, 128), BF16),
+        compiler_params=limit(4),
         name=name,
     )(*arrays)
 
 
-def assemble_kernel(*refs):
-    pieces, out, sem = refs[:8], refs[8], refs[9]
+def assemble_kernel(steps, *refs):
+    pieces, out, sems = refs[: 2 * len(steps)], refs[-2], refs[-1]
     core, x, y, zl = (lax.axis_index(name) for name in ("c", "x", "y", "zl"))
     copies = []
-    for other in range(2):
-        at_core = jnp.bitwise_xor(core, other)
-        for k2 in range(4):
+    for n, k2 in enumerate(steps):
+        for other in range(2):
+            at_core = jnp.bitwise_xor(core, other)
             for k1 in range(4):
                 dx = jnp.where(at_core == 0, k1, k2)
                 dy = jnp.where(at_core == 0, k2, k1)
@@ -235,7 +221,7 @@
                     tile = shard * 8 + jnp.bitwise_xor(y, dy) * 2 + at_core
                     columns = pl.ds(pl.multiple_of(tile * 128, 128), 128)
                     copy = pltpu.make_async_copy(
-                        pieces[4 * other + k2].at[2 * k1 + dz], out.at[:, columns], sem.at[len(copies)]
+                        pieces[2 * n + other].at[2 * k1 + dz], out.at[:, columns], sems.at[len(copies)]
                     )
                     copy.start()
                     copies.append(copy)
@@ -243,34 +229,61 @@
         copy.wait()
 
 
-def assemble(pieces):
-    return pl.pallas_call(
-        assemble_kernel,
-        in_specs=[ANY] * 8,
+def assemble(steps, pieces, done, name):
+    before = [] if done is None else [done]
+    return pl.pallas_call(
+        functools.partial(assemble_kernel, steps),
+        in_specs=[ANY] * (len(pieces) + len(before)),
         out_specs=ANY,
         out_shape=jax.ShapeDtypeStruct((256, 8192), BF16),
-        scratch_shapes=[pltpu.SemaphoreType.DMA((64,))],
-        name="assemble",
-    )(*pieces)
+        scratch_shapes=[pltpu.SemaphoreType.DMA((16 * len(steps),))],
+        input_output_aliases={} if done is None else {len(pieces): 0},
+        compiler_params=limit(1),
+        cost_estimate=pl.CostEstimate(flops=0, bytes_accessed=2**20 * len(steps), transcendentals=0),
+        name=name,
+    )(*pieces, *before)
 
 
 def lay_kernel(*refs):
-    pieces, out = refs[:8], refs[8]
+    pieces, out = refs[:4], refs[4]
     core, y = lax.axis_index("c"), lax.axis_index("y")
     for other in range(2):
         for k in range(4):
             tile = jnp.bitwise_xor(y, k) * 2 + jnp.bitwise_xor(core, other)
-            out[:, pl.ds(pl.multiple_of(tile * 128, 128), 128)] = pieces[4 * other + k][...]
+            out[:, pl.ds(pl.multiple_of(tile * 128, 128), 128)] = pieces[k][2 + other]
 
 
 def lay(pieces):
     return pl.pallas_call(
         lay_kernel,
-        in_specs=[VMEM] * 8,
+        in_specs=[VMEM] * 4,
         out_specs=VMEM,
         out_shape=jax.ShapeDtypeStruct((256, 1024), BF16),
+        compiler_params=limit(4),
         name="lay",
     )(*pieces)
+
+
+def choose_kernel(mine, theirs, out, sem):
+    for core, source in enumerate((theirs, mine)):
+
+        @pl.when(lax.axis_index("c") == core)
+        def _():
+            copy = pltpu.make_async_copy(source, out, sem)
+            copy.start()
+            copy.wait()
+
+
+def choose(mine, theirs):
+    return pl.pallas_call(
+        choose_kernel,
+        in_specs=[ANY] * 2,
+        out_specs=ANY,
+        out_shape=jax.ShapeDtypeStruct((256, 1024), BF16),
+        scratch_shapes=[pltpu.SemaphoreType.DMA],
+        compiler_params=limit(1),
+        name="choose",
+    )(mine, theirs)
 
 
 def swapped(array, axis, size, k):
@@ -289,17 +302,18 @@
 def per_device(weight, momentum, grad, positions):
     basis = [jnp.asarray(part) for part in basis_parts()]
     sent = extract(momentum[0], grad[0], positions[0], basis)
-    mine = regroup([sent] + [swapped(sent, "zh", 4, k) for k in (1, 2, 3)])
-    mine = [mine[0]] + [swapped(mine[k], "y", 4, k) for k in (1, 2, 3)]
-    entries = mine + [swapped(part, "c", 2, 1) for part in mine]
-    fresh, smooth = decode(entries, weight, basis)
-    fresh = fresh[None]
-    held = join([fresh, swapped(fresh, "zl", 2, 1)], "join_near")
-    held = join([held] + [crossed(held, 0, k) for k in (1, 2, 3)], "join_far")
-    parts = [held] + [crossed(held, 1, k) for k in (1, 2, 3)]
-    new_weight = assemble(parts + [swapped(part, "c", 2, 1) for part in parts])
-    smooths = [smooth] + [swapped(smooth, "y", 4, k) for k in (1, 2, 3)]
-    direction = lay(smooths + [swapped(part, "c", 2, 1) for part in smooths])
+    arrived = lax.all_to_all(sent, ("zh", "y"), 0, 0, tiled=True)
+    fresh, smooth = decode([arrived, swapped(arrived, "c", 2, 1)], weight, basis)
+    near = [fresh, swapped(fresh, "zl", 2, 1), smooth, swapped(smooth, "c", 2, 1)]
+    held = join(near, 1, "join_near")
+    firsts = [held] + [crossed(held, 0, k) for k in (1, 2, 3)]
+    far = join(firsts, 2, "join_far")
+    parts = [far] + [crossed(far, 1, k) for k in (1, 2, 3)]
+    others = [swapped(part, "c", 2, 1) for part in parts]
+    laid = lay(firsts)
+    direction = choose(laid, swapped(laid, "c", 2, 1))
+    new_weight = assemble([0, 1], [parts[0], others[0], parts[1], others[1]], None, "assemble_a")
+    new_weight = assemble([2, 3], [parts[2], others[2], parts[3], others[3]], new_weight, "assemble_b")
     kept_state = kept(momentum[0], grad[0], sent, basis)
     return (kept_state[None], direction, new_weight)
 

time: 232 us -> 83.7 us (0.36)
  Pallas kernels: 151 us -> 14.8 us
  starting transfers between devices: 52.7 us -> 26.6 us
  blocking collectives: 0 us -> 20.6 us
  waiting for transfers between devices: 23.3 us -> 11.9 us
  local copies, waits for them, and re-layouts: 3.66 us -> 8.59 us
    pallas_call x6 -> x7, Pallas kernels: 140 us -> 6.59 us  [the longest x2 3.18 us: assemble(): pl.pallas_call(functools.partial(assemble_kernel, steps), in_specs=[ANY]...]
    ppermute x22 -> x8, starting transfers between devices: 44.9 us -> 18.8 us  [swapped(): return lax.ppermute(array, axis, [(i, i ^ k) for i in range(size)])]
    all_to_all x0 -> x1, blocking collectives: none -> 20.6 us  [per_device(): arrived = lax.all_to_all(sent, ('zh', 'y'), 0, 0, tiled=True)]
    ppermute x22 -> x8, waiting for transfers between devices: 18.1 us -> 2.69 us  [swapped(): return lax.ppermute(array, axis, [(i, i ^ k) for i in range(size)])]
    unnamed x52 -> x24, local copies, waits for them, and re-layouts: 3.66 us -> 8.59 us
    ppermute x6, waiting for transfers between devices: 5.2 us -> 9.22 us  [crossed(): return lax.ppermute(array, ('y', 'c', 'x'), perm)]
  transfers between devices with their start and end apart: 28 -> 14, of which waited for: 13 -> 6; matrix products, arithmetic and copies ran while one was open for 0% -> 0% of each run, Pallas kernels for 3% -> 9%
where the time goes in v2:
time: 83.7 us; the launch traced here: 83.3 us
  starting transfers between devices  26.6 us (32%)
  blocking collectives  20.6 us (25%)
  Pallas kernels  14.8 us (18%)
  waiting for transfers between devices  11.9 us (14%)
  local copies, waits for them, and re-layouts  8.59 us (10%)
    all_to_all x1, blocking collectives, per_device(): arrived = lax.all_to_all(sent, ('zh', 'y'), 0, 0, tiled=True)  20.6 us
    ppermute x8, starting transfers between devices, swapped(): return lax.ppermute(array, axis, [(i, i ^ k) for i in range(size)])  18.8 us
    ppermute x6, waiting for transfers between devices, crossed(): return lax.ppermute(array, ('y', 'c', 'x'), perm)  9.22 us
    unnamed x24, local copies, waits for them, and re-layouts  8.59 us
    ppermute x6, starting transfers between devices, crossed(): return lax.ppermute(array, ('y', 'c', 'x'), perm)  7.77 us
    pallas_call x1, Pallas kernels, kept(): pl.pallas_call(kept_kernel, grid=(4,), in_specs=[pl.BlockSpec((256, 256),...  4.68 us
    pallas_call x1, Pallas kernels, extract(): pl.pallas_call(extract_kernel, grid=(4,), in_specs=[pl.BlockSpec((256, 25...  3.51 us
    pallas_call x2, Pallas kernels, assemble(): pl.pallas_call(functools.partial(assemble_kernel, steps), in_specs=[ANY]...  3.18 us
  transfers between devices with their start and end apart: 14, of which 6 were waited for; matrix products, arithmetic and copies ran while one was open for 0% of the time, Pallas kernels for 9%

profile of v2, /device:TPU:1, one launch (start us, length us, event | category | flops | bytes accessed | tf_op | source)
XLA Modules:
  0.0 83.3 jit_solution(4812408801478606944)
XLA Ops:
  0.6 0.0 copy-start
  0.6 1.2 %copy-done = f32[1,256,1024]{2,1,0:T(8,128)S(1)} copy-done((f32[1,256,1024]{2,1,0:T(8,128)S(1)}, f32[1,256,1024]{2,1,0:T(8,128)}, u32[]{:S(2)}) %copy-start) | copy-done | bytes 1048600
  1.9 0.0 copy-start.3
  1.9 1.0 %copy-done.3 = bf16[1,256,1024]{2,1,0:T(8,128)(2,1)S(1)} copy-done((bf16[1,256,1024]{2,1,0:T(8,128)(2,1)S(1)}, bf16[1,256,1024]{2,1,0:T(8,128)(2,1)}, u32[]{:S(2)}) %copy-start.3) | copy-done | bytes 524312
  2.9 0.0 copy-start.5
  2.9 0.8 copy-done.5
  3.7 0.0 copy-start.6
  3.7 0.9 %copy-done.6 = bf16[256,256]{1,0:T(8,128)(2,1)S(1)} copy-done((bf16[256,256]{1,0:T(8,128)(2,1)S(1)}, bf16[256,256]{1,0:T(8,128)(2,1)}, u32[]{:S(2)}) %copy-start.6) | copy-done | bytes 131096
  4.6 0.0 copy-start.8
  4.6 0.9 %copy-done.8 = bf16[256,256]{1,0:T(8,128)(2,1)S(1)} copy-done((bf16[256,256]{1,0:T(8,128)(2,1)S(1)}, bf16[256,256]{1,0:T(8,128)(2,1)}, u32[]{:S(2)}) %copy-start.8) | copy-done | bytes 131096
  5.5 0.0 copy-start.4
  5.5 0.0 copy-start.7
  5.5 3.5 %extract.1.sent = f32[16,8,128]{2,1,0:T(8,128)S(1)} custom-call(f32[256,1024]{1,0:T(8,128)S(1)} %bitcast.4, bf16[256,1024]{1,0:T(8,128)(2,1)S(1)} %bitcast.6, s32[4,16,32]{2,1,0:T(8,128)S(1)} %bitcast.8, bf16[256,256]{1,0:T(8,128)(2,1)S(1)} %copy-done.6, bf16[256,256]{1,0:T(8,128)(2,1)S(1)} %copy-done.8), custom_call_target="tpu_custom_call" | custom-call | flops 1000000000 | bytes 2097152 | tf_op jit(solution)/shard_map/extract/pallas_call | solution.py:99
  9.0 0.0 copy-start.1
  9.0 20.6 %all_to_all.5.refs_0_ = f32[16,8,128]{2,1,0:T(8,128)S(1)} all-to-all(f32[16,8,128]{2,1,0:T(8,128)S(1)} %extract.1.sent), channel_id=1, replica_groups=mesh['zh'=4,'y'=4,'c'=2,'x'=4,'zl'=2] {'zh','y'}, dimensions={0} | all-to-all | bytes 131072 | tf_op jit(solution)/shard_map/all_to_all | solution.py:305
  29.6 2.1 %collective-permute-start = (f32[16,8,128]{2,1,0:T(8,128)S(1)}, f32[16,8,128]{2,1,0:T(8,128)S(1)}, u32[]{:S(2)}, u32[]{:S(2)}) collective-permute-start(f32[16,8,128]{2,1,0:T(8,128)S(1)} %all_to_all.5.refs_0_), channel_id=1, source_target_pairs={{0,8},{8,0},{1,9},{9,1},{2,10},{10,2},{3,11},{11,3},{4,12},{12,4},... | collective-permute-start | bytes 196616 | tf_op jit(solution)/shard_map/ppermute | solution.py:290
  31.7 0.9 %collective-permute-done.refs_1_ = f32[16,8,128]{2,1,0:T(8,128)S(1)} collective-permute-done((f32[16,8,128]{2,1,0:T(8,128)S(1)}, f32[16,8,128]{2,1,0:T(8,128)S(1)}, u32[]{:S(2)}, u32[]{:S(2)}) %collective-permute-start) | collective-permute-done | bytes 65568 | tf_op jit(solution)/shard_map/ppermute | solution.py:290
  32.6 0.0 copy-start.2
  32.6 1.0 %copy-done.2 = bf16[256,1024]{1,0:T(8,128)(2,1)S(1)} copy-done((bf16[256,1024]{1,0:T(8,128)(2,1)S(1)}, bf16[256,1024]{1,0:T(8,128)(2,1)}, u32[]{:S(2)}) %copy-start.2) | copy-done | bytes 524312
  33.7 0.0 copy-start.9
  33.7 0.9 %copy-done.9 = bf16[256,256]{1,0:T(8,128)(2,1)S(1)} copy-done((bf16[256,256]{1,0:T(8,128)(2,1)S(1)}, bf16[256,256]{1,0:T(8,128)(2,1)}, u32[]{:S(2)}) %copy-start.9) | copy-done | bytes 131096
  34.6 0.0 copy-start.10
  34.6 0.9 %copy-done.10 = bf16[256,256]{1,0:T(8,128)(2,1)S(1)} copy-done((bf16[256,256]{1,0:T(8,128)(2,1)S(1)}, bf16[256,256]{1,0:T(8,128)(2,1)}, u32[]{:S(2)}) %copy-start.10) | copy-done | bytes 131096
  35.5 0.0 copy-start.11
  35.5 0.9 %copy-done.11 = bf16[256,256]{1,0:T(8,128)(2,1)S(1)} copy-done((bf16[256,256]{1,0:T(8,128)(2,1)S(1)}, bf16[256,256]{1,0:T(8,128)(2,1)}, u32[]{:S(2)}) %copy-start.11) | copy-done | bytes 131096
  36.4 2.4 %decode.1 = (bf16[1,256,128]{2,1,0:T(8,128)(2,1)S(1)}, bf16[1,256,128]{2,1,0:T(8,128)(2,1)S(1)}) custom-call(f32[16,8,128]{2,1,0:T(8,128)S(1)} %all_to_all.5.refs_0_, f32[16,8,128]{2,1,0:T(8,128)S(1)} %collective-permute-done.refs_1_, bf16[256,1024]{1,0:T(8,128)(2,1)S(1)} %copy-done.2, bf16[256,256]{1,0:T(8,128)(2,1)S(1)} %copy-done.6, ...), custom_call_target="tpu_custom_call" | custom-call | flops 1000000000 | bytes 1048576 | tf_op jit(solution)/shard_map/decode/pallas_call | solution.py:180
  38.8 0.8 collective-permute-start.1
  39.6 0.6 collective-permute-start.2
  40.2 1.8 %collective-permute-done.1.refs_1_ = bf16[1,256,128]{2,1,0:T(8,128)(2,1)S(1)} collective-permute-done((bf16[1,256,128]{2,1,0:T(8,128)(2,1)S(1)}, bf16[1,256,128]{2,1,0:T(8,128)(2,1)S(1)}, u32[]{:S(2)}, u32[]{:S(2)}) %collective-permute-start.1) | collective-permute-done | bytes 65568 | tf_op jit(solution)/shard_map/ppermute | solution.py:290
  42.0 0.0 collective-permute-done.2.refs_3_
  42.0 0.4 collective-permute-start.3
  42.4 1.9 %collective-permute-start.4 = (bf16[4,256,128]{2,1,0:T(8,128)(2,1)S(1)}, bf16[4,256,128]{2,1,0:T(8,128)(2,1)S(1)}, u32[]{:S(2)}, u32[]{:S(2)}) collective-permute-start(bf16[4,256,128]{2,1,0:T(8,128)(2,1)S(1)} %join_near.1.refs_0_), channel_id=1, source_target_pairs={{0,4},{2,6},{4,0},{6,2},{8,40},{10,42},{12,44},{14,46},{16,20},{18... | collective-permute-start | bytes 786440 | tf_op jit(solution)/shard_map/ppermute | solution.py:299
  44.3 1.7 %collective-permute-start.5 = (bf16[4,256,128]{2,1,0:T(8,128)(2,1)S(1)}, bf16[4,256,128]{2,1,0:T(8,128)(2,1)S(1)}, u32[]{:S(2)}, u32[]{:S(2)}) collective-permute-start(bf16[4,256,128]{2,1,0:T(8,128)(2,1)S(1)} %join_near.1.refs_0_), channel_id=1, source_target_pairs={{0,6},{2,4},{4,2},{6,0},{8,56},{10,58},{12,60},{14,62},{16,22},{18... | collective-permute-start | bytes 786440 | tf_op jit(solution)/shard_map/ppermute | solution.py:299
  46.0 1.7 %collective-permute-done.3.refs_1_ = bf16[4,256,128]{2,1,0:T(8,128)(2,1)S(1)} collective-permute-done((bf16[4,256,128]{2,1,0:T(8,128)(2,1)S(1)}, bf16[4,256,128]{2,1,0:T(8,128)(2,1)S(1)}, u32[]{:S(2)}, u32[]{:S(2)}) %collective-permute-start.3) | collective-permute-done | bytes 262176 | tf_op jit(solution)/shard_map/ppermute | solution.py:299
  47.6 3.3 %collective-permute-done.4.refs_2_ = bf16[4,256,128]{2,1,0:T(8,128)(2,1)S(1)} collective-permute-done((bf16[4,256,128]{2,1,0:T(8,128)(2,1)S(1)}, bf16[4,256,128]{2,1,0:T(8,128)(2,1)S(1)}, u32[]{:S(2)}, u32[]{:S(2)}) %collective-permute-start.4) | collective-permute-done | bytes 262176 | tf_op jit(solution)/shard_map/ppermute | solution.py:299
  51.0 2.9 %collective-permute-done.5.refs_3_ = bf16[4,256,128]{2,1,0:T(8,128)(2,1)S(1)} collective-permute-done((bf16[4,256,128]{2,1,0:T(8,128)(2,1)S(1)}, bf16[4,256,128]{2,1,0:T(8,128)(2,1)S(1)}, u32[]{:S(2)}, u32[]{:S(2)}) %collective-permute-start.5) | collective-permute-done | bytes 262176 | tf_op jit(solution)/shard_map/ppermute | solution.py:299
  53.9 1.1 %collective-permute-start.12 = (bf16[8,256,128]{2,1,0:T(8,128)(2,1)S(1)}, bf16[8,256,128]{2,1,0:T(8,128)(2,1)S(1)}, u32[]{:S(2)}, u32[]{:S(2)}) collective-permute-start(bf16[8,256,128]{2,1,0:T(8,128)(2,1)S(1)} %join_far.1.refs_0_), channel_id=1, source_target_pairs={{0,16},{2,18},{4,20},{6,22},{8,10},{10,8},{12,14},{14,12},{16,0},{... | collective-permute-start | bytes 1572872 | tf_op jit(solution)/shard_map/ppermute | solution.py:299
  54.9 1.8 %collective-permute-start.9 = (bf16[8,256,128]{2,1,0:T(8,128)(2,1)S(1)}, bf16[8,256,128]{2,1,0:T(8,128)(2,1)S(1)}, u32[]{:S(2)}, u32[]{:S(2)}) collective-permute-start(bf16[8,256,128]{2,1,0:T(8,128)(2,1)S(1)} %join_far.1.refs_0_), channel_id=1, source_target_pairs={{0,48},{2,50},{4,52},{6,54},{8,14},{10,12},{12,10},{14,8},{16,32},... | collective-permute-start | bytes 1572872 | tf_op jit(solution)/shard_map/ppermute | solution.py:299
  56.8 0.9 %collective-permute-start.7 = (bf16[8,256,128]{2,1,0:T(8,128)(2,1)S(1)}, bf16[8,256,128]{2,1,0:T(8,128)(2,1)S(1)}, u32[]{:S(2)}, u32[]{:S(2)}) collective-permute-start(bf16[8,256,128]{2,1,0:T(8,128)(2,1)S(1)} %join_far.1.refs_0_), channel_id=1, source_target_pairs={{0,32},{2,34},{4,36},{6,38},{8,12},{10,14},{12,8},{14,10},{16,48},... | collective-permute-start | bytes 1572872 | tf_op jit(solution)/shard_map/ppermute | solution.py:299
  57.7 4.3 %collective-permute-start.11 = (bf16[8,256,128]{2,1,0:T(8,128)(2,1)S(1)}, bf16[8,256,128]{2,1,0:T(8,128)(2,1)S(1)}, u32[]{:S(2)}, u32[]{:S(2)}) collective-permute-start(bf16[8,256,128]{2,1,0:T(8,128)(2,1)S(1)} %join_far.1.refs_0_), channel_id=1, source_target_pairs={{0,8},{8,0},{1,9},{9,1},{2,10},{10,2},{3,11},{11,3},{4,12},{12,4},... | collective-permute-start | bytes 1572872 | tf_op jit(solution)/shard_map/ppermute | solution.py:290
  62.0 0.1 lay.1.mine
  62.2 0.1 collective-permute-start.6
  62.3 0.0 collective-permute-done.12.refs_2_
  62.3 4.8 %collective-permute-start.13 = (bf16[8,256,128]{2,1,0:T(8,128)(2,1)S(1)}, bf16[8,256,128]{2,1,0:T(8,128)(2,1)S(1)}, u32[]{:S(2)}, u32[]{:S(2)}) collective-permute-start(bf16[8,256,128]{2,1,0:T(8,128)(2,1)S(1)} %collective-permute-done.12.refs_2_), channel_id=1, source_target_pairs={{0,8},{8,0},{1,9},{9,1},{2,10},{10,2},{3,11},{11,3},{4,12},{12,4},... | collective-permute-start | bytes 1572872 | tf_op jit(solution)/shard_map/ppermute | solution.py:290
  67.1 1.4 %collective-permute-done.9.refs_2_ = bf16[8,256,128]{2,1,0:T(8,128)(2,1)S(1)} collective-permute-done((bf16[8,256,128]{2,1,0:T(8,128)(2,1)S(1)}, bf16[8,256,128]{2,1,0:T(8,128)(2,1)S(1)}, u32[]{:S(2)}, u32[]{:S(2)}) %collective-permute-start.9) | collective-permute-done | bytes 524320 | tf_op jit(solution)/shard_map/ppermute | solution.py:299
  68.5 6.0 %collective-permute-start.10 = (bf16[8,256,128]{2,1,0:T(8,128)(2,1)S(1)}, bf16[8,256,128]{2,1,0:T(8,128)(2,1)S(1)}, u32[]{:S(2)}, u32[]{:S(2)}) collective-permute-start(bf16[8,256,128]{2,1,0:T(8,128)(2,1)S(1)} %collective-permute-done.9.refs_2_), channel_id=1, source_target_pairs={{0,8},{8,0},{1,9},{9,1},{2,10},{10,2},{3,11},{11,3},{4,12},{12,4},... | collective-permute-start | bytes 1572872 | tf_op jit(solution)/shard_map/ppermute | solution.py:290
  74.5 0.0 collective-permute-done.7.refs_0_
  74.5 0.0 collective-permute-start.8
  74.5 0.0 copy-done.4
  74.5 0.0 copy-done.7
  74.5 0.0 copy-done.1
  74.5 4.7 %kept.1 = f32[256,1024]{1,0:T(8,128)} custom-call(f32[256,1024]{1,0:T(8,128)S(1)} %bitcast.5, bf16[256,1024]{1,0:T(8,128)(2,1)S(1)} %bitcast.7, f32[16,8,128]{2,1,0:T(8,128)S(1)} %extract.1.sent, bf16[256,256]{1,0:T(8,128)(2,1)S(1)} %copy-done.7, bf16[256,256]{1,0:T(8,128)(2,1)S(1)} %copy-done.9, bf16[256,256]{1,0:T(8,128)(2,1)S(1)} %copy-done.10, ...), custom_call_target="tpu_custom_call" | custom-call | flops 2000000000 | bytes 3145728 | tf_op jit(solution)/shard_map/kept/pallas_call | solution.py:136
  79.2 0.0 collective-permute-done.6.theirs
  79.2 0.8 choose.1
  80.0 0.0 collective-permute-done.11.refs_1_
  80.0 0.0 collective-permute-done.13.refs_3_
  80.1 1.6 %assemble_a.1.refs_4_ = bf16[256,8192]{1,0:T(8,128)(2,1)} custom-call(bf16[8,256,128]{2,1,0:T(8,128)(2,1)S(1)} %join_far.1.refs_0_, bf16[8,256,128]{2,1,0:T(8,128)(2,1)S(1)} %collective-permute-done.11.refs_1_, bf16[8,256,128]{2,1,0:T(8,128)(2,1)S(1)} %collective-permute-done.12.refs_2_, bf16[8,256,128]{2,1,0:T(8,128)(2,1)S(1)} %collective-permute-done.13.refs_3_), custom_call_target="tpu_custom_call" | custom-call | bytes 2097152 | tf_op jit(solution)/shard_map/assemble_a/pallas_call | solution.py:234
  81.7 0.0 collective-permute-done.10.refs_3_
  81.7 0.0 collective-permute-done.8.refs_1_
  81.7 1.6 %assemble_b.1 = bf16[256,8192]{1,0:T(8,128)(2,1)} custom-call(bf16[8,256,128]{2,1,0:T(8,128)(2,1)S(1)} %collective-permute-done.7.refs_0_, bf16[8,256,128]{2,1,0:T(8,128)(2,1)S(1)} %collective-permute-done.8.refs_1_, bf16[8,256,128]{2,1,0:T(8,128)(2,1)S(1)} %collective-permute-done.9.refs_2_, ...), custom_call_target="tpu_custom_call", output_to_operand_aliasing={{}: (4, {})} | custom-call | bytes 2097152 | tf_op jit(solution)/shard_map/assemble_b/pallas_call | solution.py:234
  (2 shorter events, 0.1 us)
Async XLA Ops:
  0.6 1.2 %copy-start = (f32[1,256,1024]{2,1,0:T(8,128)S(1)}, f32[1,256,1024]{2,1,0:T(8,128)}, u32[]{:S(2)}) copy-start(f32[1,256,1024]{2,1,0:T(8,128)} %param.9) | copy-start | bytes 3145732
  1.9 1.0 %copy-start.3 = (bf16[1,256,1024]{2,1,0:T(8,128)(2,1)S(1)}, bf16[1,256,1024]{2,1,0:T(8,128)(2,1)}, u32[]{:S(2)}) copy-start(bf16[1,256,1024]{2,1,0:T(8,128)(2,1)} %param.10) | copy-start | bytes 1572868
  2.9 0.8 copy-start.5
  3.7 0.9 %copy-start.6 = (bf16[256,256]{1,0:T(8,128)(2,1)S(1)}, bf16[256,256]{1,0:T(8,128)(2,1)}, u32[]{:S(2)}) copy-start(bf16[256,256]{1,0:T(8,128)(2,1)} %constant.8.clone.bh.refs_3_) | copy-start | bytes 393220
  4.6 0.9 %copy-start.8 = (bf16[256,256]{1,0:T(8,128)(2,1)S(1)}, bf16[256,256]{1,0:T(8,128)(2,1)}, u32[]{:S(2)}) copy-start(bf16[256,256]{1,0:T(8,128)(2,1)} %constant.9.clone.bl.refs_4_) | copy-start | bytes 393220
  5.5 69.1 %copy-start.4 = (bf16[1,256,1024]{2,1,0:T(8,128)(2,1)S(1)}, bf16[1,256,1024]{2,1,0:T(8,128)(2,1)}, u32[]{:S(2)}) copy-start(bf16[1,256,1024]{2,1,0:T(8,128)(2,1)} %param.10) | copy-start | bytes 1572868
  5.5 69.1 %copy-start.7 = (bf16[256,256]{1,0:T(8,128)(2,1)S(1)}, bf16[256,256]{1,0:T(8,128)(2,1)}, u32[]{:S(2)}) copy-start(bf16[256,256]{1,0:T(8,128)(2,1)} %constant.8.clone.bh.refs_3_) | copy-start | bytes 393220
  9.0 65.5 %copy-start.1 = (f32[1,256,1024]{2,1,0:T(8,128)S(1)}, f32[1,256,1024]{2,1,0:T(8,128)}, u32[]{:S(2)}) copy-start(f32[1,256,1024]{2,1,0:T(8,128)} %param.9) | copy-start | bytes 3145732
  29.6 3.0 %collective-permute-start = (f32[16,8,128]{2,1,0:T(8,128)S(1)}, f32[16,8,128]{2,1,0:T(8,128)S(1)}, u32[]{:S(2)}, u32[]{:S(2)}) collective-permute-start(f32[16,8,128]{2,1,0:T(8,128)S(1)} %all_to_all.5.refs_0_), channel_id=1, source_target_pairs={{0,8},{8,0},{1,9},{9,1},{2,10},{10,2},{3,11},{11,3},{4,12},{12,4},... | collective-permute-start | bytes 196616 | tf_op jit(solution)/shard_map/ppermute | solution.py:290
  32.6 1.0 %copy-start.2 = (bf16[256,1024]{1,0:T(8,128)(2,1)S(1)}, bf16[256,1024]{1,0:T(8,128)(2,1)}, u32[]{:S(2)}) copy-start(bf16[256,1024]{1,0:T(8,128)(2,1)} %refs_2_.1) | copy-start | bytes 1572868
  33.7 0.9 %copy-start.9 = (bf16[256,256]{1,0:T(8,128)(2,1)S(1)}, bf16[256,256]{1,0:T(8,128)(2,1)}, u32[]{:S(2)}) copy-start(bf16[256,256]{1,0:T(8,128)(2,1)} %constant.9.clone.bl.refs_4_) | copy-start | bytes 393220
  34.6 0.9 %copy-start.10 = (bf16[256,256]{1,0:T(8,128)(2,1)S(1)}, bf16[256,256]{1,0:T(8,128)(2,1)}, u32[]{:S(2)}) copy-start(bf16[256,256]{1,0:T(8,128)(2,1)} %constant.10.clone.th.refs_5_) | copy-start | bytes 393220
  35.5 0.9 %copy-start.11 = (bf16[256,256]{1,0:T(8,128)(2,1)S(1)}, bf16[256,256]{1,0:T(8,128)(2,1)}, u32[]{:S(2)}) copy-start(bf16[256,256]{1,0:T(8,128)(2,1)} %constant.11.clone.tl.refs_6_) | copy-start | bytes 393220
  38.8 3.2 %collective-permute-start.1 = (bf16[1,256,128]{2,1,0:T(8,128)(2,1)S(1)}, bf16[1,256,128]{2,1,0:T(8,128)(2,1)S(1)}, u32[]{:S(2)}, u32[]{:S(2)}) collective-permute-start(bf16[1,256,128]{2,1,0:T(8,128)(2,1)S(1)} %get-tuple-element.5.refs_0_), channel_id=1, source_target_pairs={{0,1},{1,0},{2,3},{3,2},{4,5},{5,4},{6,7},{7,6},{8,9},{9,8},{10,11... | collective-permute-start | bytes 196616 | tf_op jit(solution)/shard_map/ppermute | solution.py:290
  39.6 2.4 %collective-permute-start.2 = (bf16[1,256,128]{2,1,0:T(8,128)(2,1)S(1)}, bf16[1,256,128]{2,1,0:T(8,128)(2,1)S(1)}, u32[]{:S(2)}, u32[]{:S(2)}) collective-permute-start(bf16[1,256,128]{2,1,0:T(8,128)(2,1)S(1)} %get-tuple-element.6.refs_2_), channel_id=1, source_target_pairs={{0,8},{8,0},{1,9},{9,1},{2,10},{10,2},{3,11},{11,3},{4,12},{12,4},... | collective-permute-start | bytes 196616 | tf_op jit(solution)/shard_map/ppermute | solution.py:290
  42.0 5.6 %collective-permute-start.3 = (bf16[4,256,128]{2,1,0:T(8,128)(2,1)S(1)}, bf16[4,256,128]{2,1,0:T(8,128)(2,1)S(1)}, u32[]{:S(2)}, u32[]{:S(2)}) collective-permute-start(bf16[4,256,128]{2,1,0:T(8,128)(2,1)S(1)} %join_near.1.refs_0_), channel_id=1, source_target_pairs={{0,2},{2,0},{4,6},{6,4},{8,24},{10,26},{12,28},{14,30},{16,18},{18... | collective-permute-start | bytes 786440 | tf_op jit(solution)/shard_map/ppermute | solution.py:299
  42.4 8.5 %collective-permute-start.4 = (bf16[4,256,128]{2,1,0:T(8,128)(2,1)S(1)}, bf16[4,256,128]{2,1,0:T(8,128)(2,1)S(1)}, u32[]{:S(2)}, u32[]{:S(2)}) collective-permute-start(bf16[4,256,128]{2,1,0:T(8,128)(2,1)S(1)} %join_near.1.refs_0_), channel_id=1, source_target_pairs={{0,4},{2,6},{4,0},{6,2},{8,40},{10,42},{12,44},{14,46},{16,20},{18... | collective-permute-start | bytes 786440 | tf_op jit(solution)/shard_map/ppermute | solution.py:299
  44.3 9.5 %collective-permute-start.5 = (bf16[4,256,128]{2,1,0:T(8,128)(2,1)S(1)}, bf16[4,256,128]{2,1,0:T(8,128)(2,1)S(1)}, u32[]{:S(2)}, u32[]{:S(2)}) collective-permute-start(bf16[4,256,128]{2,1,0:T(8,128)(2,1)S(1)} %join_near.1.refs_0_), channel_id=1, source_target_pairs={{0,6},{2,4},{4,2},{6,0},{8,56},{10,58},{12,60},{14,62},{16,22},{18... | collective-permute-start | bytes 786440 | tf_op jit(solution)/shard_map/ppermute | solution.py:299
  53.9 8.4 %collective-permute-start.12 = (bf16[8,256,128]{2,1,0:T(8,128)(2,1)S(1)}, bf16[8,256,128]{2,1,0:T(8,128)(2,1)S(1)}, u32[]{:S(2)}, u32[]{:S(2)}) collective-permute-start(bf16[8,256,128]{2,1,0:T(8,128)(2,1)S(1)} %join_far.1.refs_0_), channel_id=1, source_target_pairs={{0,16},{2,18},{4,20},{6,22},{8,10},{10,8},{12,14},{14,12},{16,0},{... | collective-permute-start | bytes 1572872 | tf_op jit(solution)/shard_map/ppermute | solution.py:299
  54.9 13.6 %collective-permute-start.9 = (bf16[8,256,128]{2,1,0:T(8,128)(2,1)S(1)}, bf16[8,256,128]{2,1,0:T(8,128)(2,1)S(1)}, u32[]{:S(2)}, u32[]{:S(2)}) collective-permute-start(bf16[8,256,128]{2,1,0:T(8,128)(2,1)S(1)} %join_far.1.refs_0_), channel_id=1, source_target_pairs={{0,48},{2,50},{4,52},{6,54},{8,14},{10,12},{12,10},{14,8},{16,32},... | collective-permute-start | bytes 1572872 | tf_op jit(solution)/shard_map/ppermute | solution.py:299
  56.8 17.8 %collective-permute-start.7 = (bf16[8,256,128]{2,1,0:T(8,128)(2,1)S(1)}, bf16[8,256,128]{2,1,0:T(8,128)(2,1)S(1)}, u32[]{:S(2)}, u32[]{:S(2)}) collective-permute-start(bf16[8,256,128]{2,1,0:T(8,128)(2,1)S(1)} %join_far.1.refs_0_), channel_id=1, source_target_pairs={{0,32},{2,34},{4,36},{6,38},{8,12},{10,14},{12,8},{14,10},{16,48},... | collective-permute-start | bytes 1572872 | tf_op jit(solution)/shard_map/ppermute | solution.py:299
  57.7 22.4 %collective-permute-start.11 = (bf16[8,256,128]{2,1,0:T(8,128)(2,1)S(1)}, bf16[8,256,128]{2,1,0:T(8,128)(2,1)S(1)}, u32[]{:S(2)}, u32[]{:S(2)}) collective-permute-start(bf16[8,256,128]{2,1,0:T(8,128)(2,1)S(1)} %join_far.1.refs_0_), channel_id=1, source_target_pairs={{0,8},{8,0},{1,9},{9,1},{2,10},{10,2},{3,11},{11,3},{4,12},{12,4},... | collective-permute-start | bytes 1572872 | tf_op jit(solution)/shard_map/ppermute | solution.py:290
  62.2 17.1 %collective-permute-start.6 = (bf16[256,1024]{1,0:T(8,128)(2,1)S(1)}, bf16[256,1024]{1,0:T(8,128)(2,1)S(1)}, u32[]{:S(2)}, u32[]{:S(2)}) collective-permute-start(bf16[256,1024]{1,0:T(8,128)(2,1)S(1)} %lay.1.mine), channel_id=1, source_target_pairs={{0,8},{8,0},{1,9},{9,1},{2,10},{10,2},{3,11},{11,3},{4,12},{12,4},... | collective-permute-start | bytes 1572872 | tf_op jit(solution)/shard_map/ppermute | solution.py:290
  62.3 17.8 %collective-permute-start.13 = (bf16[8,256,128]{2,1,0:T(8,128)(2,1)S(1)}, bf16[8,256,128]{2,1,0:T(8,128)(2,1)S(1)}, u32[]{:S(2)}, u32[]{:S(2)}) collective-permute-start(bf16[8,256,128]{2,1,0:T(8,128)(2,1)S(1)} %collective-permute-done.12.refs_2_), channel_id=1, source_target_pairs={{0,8},{8,0},{1,9},{9,1},{2,10},{10,2},{3,11},{11,3},{4,12},{12,4},... | collective-permute-start | bytes 1572872 | tf_op jit(solution)/shard_map/ppermute | solution.py:290
  68.5 13.2 %collective-permute-start.10 = (bf16[8,256,128]{2,1,0:T(8,128)(2,1)S(1)}, bf16[8,256,128]{2,1,0:T(8,128)(2,1)S(1)}, u32[]{:S(2)}, u32[]{:S(2)}) collective-permute-start(bf16[8,256,128]{2,1,0:T(8,128)(2,1)S(1)} %collective-permute-done.9.refs_2_), channel_id=1, source_target_pairs={{0,8},{8,0},{1,9},{9,1},{2,10},{10,2},{3,11},{11,3},{4,12},{12,4},... | collective-permute-start | bytes 1572872 | tf_op jit(solution)/shard_map/ppermute | solution.py:290
  74.5 7.2 %collective-permute-start.8 = (bf16[8,256,128]{2,1,0:T(8,128)(2,1)S(1)}, bf16[8,256,128]{2,1,0:T(8,128)(2,1)S(1)}, u32[]{:S(2)}, u32[]{:S(2)}) collective-permute-start(bf16[8,256,128]{2,1,0:T(8,128)(2,1)S(1)} %collective-permute-done.7.refs_0_), channel_id=1, source_target_pairs={{0,8},{8,0},{1,9},{9,1},{2,10},{10,2},{3,11},{11,3},{4,12},{12,4},... | collective-permute-start | bytes 1572872 | tf_op jit(solution)/shard_map/ppermute | solution.py:290

commit v3 on v2

--- a/solution.py
+++ b/solution.py
@@ -11,6 +11,7 @@
 from jax.sharding import PartitionSpec as P
 
 GROUP = 64
+EXTRACT_MIB = 62
 REPLICA = ("zh", "y", "c")
 SHARD = ("x", "zl")
 beta_decay = 0.9
@@ -31,7 +32,7 @@
     four = np.kron(np.eye(4), table)
     high = four.astype(jnp.bfloat16)
     low = (four - high.astype(np.float64)).astype(jnp.bfloat16)
-    return [np.ascontiguousarray(part) for part in (high, low, high.T, low.T)]
+    return np.stack([high, low, high.T, low.T])
 
 
 def two_parts(value):
@@ -66,18 +67,26 @@
     return two_parts(jnp.where(line == column, values, 0.0))
 
 
-def extract_kernel(momentum, grad, positions, bh, bl, out, places):
+def extract_kernel(momentum, grad, positions, weight, table, out, column, basis, places, sems):
     g = pl.program_id(0)
+    place = pl.multiple_of((lax.axis_index("y") * 2 + lax.axis_index("c")) * 128, 128)
+    copies = [
+        pltpu.make_async_copy(weight.at[:, pl.ds(place, 128)], column, sems.at[0]),
+        pltpu.make_async_copy(table, basis, sems.at[1]),
+    ]
 
     @pl.when(g == 0)
     def _():
+        for copy in copies[::-1]:
+            copy.start()
         for x in range(4):
             places[:, 32 * x : 32 * x + 32] = positions[x]
-
-    basis = (bh[...], bl[...])
+        copies[1].wait()
+
+    straight = (basis[0], basis[1])
     moved = beta_decay * momentum[...] + grad[...].astype(F32)
-    half = product(rows_by_rows, basis, two_parts(moved))
-    coeff = jnp.stack(two_parts(product(rows_by_rows, two_parts(half), basis)))
+    half = product(rows_by_rows, straight, two_parts(moved))
+    coeff = jnp.stack(two_parts(product(rows_by_rows, two_parts(half), straight)))
     lines = []
     for q in range(4):
         flat = places[pl.ds(4 * g + q, 1), :]
@@ -92,30 +101,43 @@
     for z in range(4):
         out[4 * z + g] = tile
 
-
-def extract(momentum, grad, positions, basis):
-    column = lambda g: (0, g)
+    @pl.when(g == 3)
+    def _():
+        copies[0].wait()
+
+
+def extract(momentum, grad, positions, weight, table):
+    block = pl.BlockSpec((256, 256), lambda g: (0, g))
     whole = lambda *shape: pl.BlockSpec(shape, lambda g: (0,) * len(shape))
     return pl.pallas_call(
         extract_kernel,
         grid=(4,),
-        in_specs=[
-            pl.BlockSpec((256, 256), column),
-            pl.BlockSpec((256, 256), column),
-            whole(4, 16, 32),
-            whole(256, 256),
-            whole(256, 256),
+        in_specs=[block, block, whole(4, 16, 32), ANY, ANY],
+        out_specs=[whole(16, 8, 128), VMEM, VMEM],
+        out_shape=[
+            jax.ShapeDtypeStruct((16, 8, 128), F32),
+            jax.ShapeDtypeStruct((256, 128), BF16),
+            jax.ShapeDtypeStruct((4, 256, 256), BF16),
         ],
-        out_specs=whole(16, 8, 128),
-        out_shape=jax.ShapeDtypeStruct((16, 8, 128), F32),
-        scratch_shapes=[pltpu.VMEM((16, 128), jnp.int32)],
+        scratch_shapes=[pltpu.VMEM((16, 128), jnp.int32), pltpu.SemaphoreType.DMA((2,))],
         cost_estimate=pl.CostEstimate(flops=10**9, bytes_accessed=2 * 2**20, transcendentals=0),
-        compiler_params=limit(12),
+        compiler_params=limit(EXTRACT_MIB),
         name="extract",
-    )(momentum, grad, positions, basis[0], basis[1])
-
-
-def kept_kernel(momentum, grad, sent, bh, bl, th, tl, out):
+    )(momentum, grad, positions, weight, table)
+
+
+def kept_kernel(momentum, grad, sent, basis, *refs):
+    g = pl.program_id(0)
+    pieces, out, laid = refs[:4], refs[4], refs[5]
+    core, y = lax.axis_index("c"), lax.axis_index("y")
+    for k in range(4):
+
+        @pl.when(g == k)
+        def _():
+            for other in range(2):
+                tile = jnp.bitwise_xor(y, k) * 2 + jnp.bitwise_xor(core, other)
+                laid[:, pl.ds(pl.multiple_of(tile * 128, 128), 128)] = pieces[k][2 + other]
+
     tile = sent[0]
     blocks = []
     for q in range(4):
@@ -124,33 +146,30 @@
         hot = one_hot_rows(row, 4 * GROUP, BF16)
         blocks.append(rows_by_rows(high, hot) + rows_by_rows(low, hot))
     grid = two_parts(jnp.concatenate(blocks, axis=0))
-    half = product(rows_by_rows, (th[...], tl[...]), grid)
-    dense = product(rows_by_cols, two_parts(half), (bh[...], bl[...]))
+    half = product(rows_by_rows, (basis[2], basis[3]), grid)
+    dense = product(rows_by_cols, two_parts(half), (basis[0], basis[1]))
     moved = beta_decay * momentum[...] + grad[...].astype(F32)
     out[...] = moved - dense
 
 
-def kept(momentum, grad, sent, basis):
-    column = lambda g: (0, g)
+def kept(momentum, grad, sent, basis, pieces):
+    block = pl.BlockSpec((256, 256), lambda g: (0, g))
     whole = lambda *shape: pl.BlockSpec(shape, lambda g: (0,) * len(shape))
     return pl.pallas_call(
         kept_kernel,
         grid=(4,),
-        in_specs=[pl.BlockSpec((256, 256), column)] * 2 + [pl.BlockSpec((1, 8, 128), lambda g: (g, 0, 0))] + [whole(256, 256)] * 4,
-        out_specs=pl.BlockSpec((256, 256), column),
-        out_shape=jax.ShapeDtypeStruct((256, 1024), F32),
+        in_specs=[block, block, pl.BlockSpec((1, 8, 128), lambda g: (g, 0, 0)), VMEM] + [VMEM] * 4,
+        out_specs=[block, VMEM],
+        out_shape=[jax.ShapeDtypeStruct((256, 1024), F32), jax.ShapeDtypeStruct((256, 1024), BF16)],
         cost_estimate=pl.CostEstimate(flops=2 * 10**9, bytes_accessed=3 * 2**20, transcendentals=0),
         compiler_params=limit(12),
         name="kept",
-    )(momentum, grad, sent, *basis)
+    )(momentum, grad, sent, basis, *pieces)
 
 
 def decode_kernel(*refs):
-    entries, (weight, bh, bl, th, tl), (fresh, smooth_out, staged, sem) = refs[:2], refs[2:7], refs[7:]
+    entries, (column, basis, fresh, smooth_out) = refs[:2], refs[2:]
     core = lax.axis_index("c")
-    place = pl.multiple_of((lax.axis_index("y") * 2 + core) * 128, 128)
-    copy = pltpu.make_async_copy(weight.at[:, pl.ds(place, 128)], staged, sem)
-    copy.start()
     tiles = []
     for ref in entries:
         for source in range(16):
@@ -162,31 +181,29 @@
         for pair in range(0, len(tiles), 2):
             lefts, hots = [], []
             for tile in tiles[pair : pair + 2]:
-                row, column = split_place(tile[2 * j + 1 : 2 * j + 2].astype(jnp.int32))
-                lefts.append(jnp.concatenate(spread(tile[2 * j : 2 * j + 1], column), axis=0))
+                row, line = split_place(tile[2 * j + 1 : 2 * j + 2].astype(jnp.int32))
+                lefts.append(jnp.concatenate(spread(tile[2 * j : 2 * j + 1], line), axis=0))
                 hots.append(one_hot_rows(row, 4 * GROUP, BF16))
             total = total + rows_by_rows(jnp.concatenate(lefts, axis=1), jnp.concatenate(hots, axis=1))
         blocks.append(total[:GROUP] + total[GROUP:])
     grid = two_parts(jnp.concatenate(blocks, axis=0))
-    half = product(rows_by_rows, (th[...], tl[...]), grid)
-    dense = product(rows_by_cols, two_parts(half), (bh[:128, :128], bl[:128, :128]))
+    half = product(rows_by_rows, (basis[2], basis[3]), grid)
+    dense = product(rows_by_cols, two_parts(half), (basis[0, :128, :128], basis[1, :128, :128]))
     smooth = jnp.tanh(dense)
     smooth_out[0] = smooth.astype(BF16)
-    copy.wait()
-    fresh[0] = (staged[...].astype(F32) - step_rate * smooth).astype(BF16)
-
-
-def decode(entries, weight, basis):
+    fresh[0] = (column[...].astype(F32) - step_rate * smooth).astype(BF16)
+
+
+def decode(entries, column, basis):
     return pl.pallas_call(
         decode_kernel,
-        in_specs=[VMEM] * 2 + [ANY] + [VMEM] * 4,
+        in_specs=[VMEM] * 4,
         out_specs=[VMEM] * 2,
         out_shape=[jax.ShapeDtypeStruct((1, 256, 128), BF16)] * 2,
-        scratch_shapes=[pltpu.VMEM((256, 128), BF16), pltpu.SemaphoreType.DMA],
         cost_estimate=pl.CostEstimate(flops=10**9, bytes_accessed=2**20, transcendentals=32768),
         compiler_params=limit(12),
         name="decode",
-    )(*entries, weight, *basis)
+    )(*entries, column, basis)
 
 
 def join_kernel(size, *refs):
@@ -244,26 +261,6 @@
     )(*pieces, *before)
 
 
-def lay_kernel(*refs):
-    pieces, out = refs[:4], refs[4]
-    core, y = lax.axis_index("c"), lax.axis_index("y")
-    for other in range(2):
-        for k in range(4):
-            tile = jnp.bitwise_xor(y, k) * 2 + jnp.bitwise_xor(core, other)
-            out[:, pl.ds(pl.multiple_of(tile * 128, 128), 128)] = pieces[k][2 + other]
-
-
-def lay(pieces):
-    return pl.pallas_call(
-        lay_kernel,
-        in_specs=[VMEM] * 4,
-        out_specs=VMEM,
-        out_shape=jax.ShapeDtypeStruct((256, 1024), BF16),
-        compiler_params=limit(4),
-        name="lay",
-    )(*pieces)
-
-
 def choose_kernel(mine, theirs, out, sem):
     for core, source in enumerate((theirs, mine)):
 
@@ -300,21 +297,20 @@
 
 
 def per_device(weight, momentum, grad, positions):
-    basis = [jnp.asarray(part) for part in basis_parts()]
-    sent = extract(momentum[0], grad[0], positions[0], basis)
+    table = jnp.asarray(basis_parts())
+    sent, column, basis = extract(momentum[0], grad[0], positions[0], weight, table)
     arrived = lax.all_to_all(sent, ("zh", "y"), 0, 0, tiled=True)
-    fresh, smooth = decode([arrived, swapped(arrived, "c", 2, 1)], weight, basis)
+    fresh, smooth = decode([arrived, swapped(arrived, "c", 2, 1)], column, basis)
     near = [fresh, swapped(fresh, "zl", 2, 1), smooth, swapped(smooth, "c", 2, 1)]
     held = join(near, 1, "join_near")
     firsts = [held] + [crossed(held, 0, k) for k in (1, 2, 3)]
     far = join(firsts, 2, "join_far")
     parts = [far] + [crossed(far, 1, k) for k in (1, 2, 3)]
     others = [swapped(part, "c", 2, 1) for part in parts]
-    laid = lay(firsts)
+    kept_state, laid = kept(momentum[0], grad[0], sent, basis, firsts)
     direction = choose(laid, swapped(laid, "c", 2, 1))
     new_weight = assemble([0, 1], [parts[0], others[0], parts[1], others[1]], None, "assemble_a")
     new_weight = assemble([2, 3], [parts[2], others[2], parts[3], others[3]], new_weight, "assemble_b")
-    kept_state = kept(momentum[0], grad[0], sent, basis)
     return (kept_state[None], direction, new_weight)
 
 

time: 83.7 us -> 72.5 us (0.87)
  starting transfers between devices: 26.6 us -> 17 us
  local copies, waits for them, and re-layouts: 8.59 us -> 1.89 us
  Pallas kernels: 14.8 us -> 17.9 us
  waiting for transfers between devices: 11.9 us -> 13.7 us
    ppermute x8, starting transfers between devices: 18.8 us -> 9.94 us  [swapped(): return lax.ppermute(array, axis, [(i, i ^ k) for i in range(size)])]
    unnamed x24 -> x10, local copies, waits for them, and re-layouts: 8.59 us -> 1.89 us
    pallas_call x4 -> x3, Pallas kernels: 10.7 us -> 13.9 us  [the longest x1 6.56 us: extract(): pl.pallas_call(extract_kernel, grid=(4,), in_specs=[block, block, whole(4...]
    ppermute x6, waiting for transfers between devices: 9.22 us -> 11.1 us  [crossed(): return lax.ppermute(array, ('y', 'c', 'x'), perm)]
  transfers between devices with their start and end apart: 14 -> 14, of which waited for: 6 -> 5; matrix products, arithmetic and copies ran while one was open for 0% -> 0% of each run, Pallas kernels for 9% -> 10%
where the time goes in v3:
time: 72.5 us; the launch traced here: 72.2 us
  blocking collectives  20.8 us (29%)
  Pallas kernels  17.9 us (25%)
  starting transfers between devices  17 us (23%)
  waiting for transfers between devices  13.7 us (19%)
  local copies, waits for them, and re-layouts  1.89 us (3%)
  between operations  0.74 us (1%)
    all_to_all x1, blocking collectives, per_device(): arrived = lax.all_to_all(sent, ('zh', 'y'), 0, 0, tiled=True)  20.8 us
    ppermute x6, waiting for transfers between devices, crossed(): return lax.ppermute(array, ('y', 'c', 'x'), perm)  11.1 us
    ppermute x8, starting transfers between devices, swapped(): return lax.ppermute(array, axis, [(i, i ^ k) for i in range(size)])  9.94 us
    ppermute x6, starting transfers between devices, crossed(): return lax.ppermute(array, ('y', 'c', 'x'), perm)  7.09 us
    pallas_call x1, Pallas kernels, extract(): pl.pallas_call(extract_kernel, grid=(4,), in_specs=[block, block, whole(4...  6.56 us
    pallas_call x1, Pallas kernels, kept(): pl.pallas_call(kept_kernel, grid=(4,), in_specs=[block, block, pl.BlockSp...  4.96 us
    pallas_call x2, Pallas kernels, assemble(): pl.pallas_call(functools.partial(assemble_kernel, steps), in_specs=[ANY]...  3.18 us
    ppermute x8, waiting for transfers between devices, swapped(): return lax.ppermute(array, axis, [(i, i ^ k) for i in range(size)])  2.68 us
  transfers between devices with their start and end apart: 14, of which 5 were waited for; matrix products, arithmetic and copies ran while one was open for 0% of the time, Pallas kernels for 10%

profile of v3, /device:TPU:1, one launch (start us, length us, event | category | flops | bytes accessed | tf_op | source)
XLA Modules:
  0.0 72.2 jit_solution(12319909610236063301)
XLA Ops:
  0.6 0.0 copy-start.1
  0.6 0.0 copy-start.2
  0.7 6.6 %extract.1 = (f32[16,8,128]{2,1,0:T(8,128)}, bf16[256,128]{1,0:T(8,128)(2,1)}, bf16[4,256,256]{2,1,0:T(8,128)(2,1)}) custom-call(f32[256,1024]{1,0:T(8,128)} %bitcast.4, bf16[256,1024]{1,0:T(8,128)(2,1)} %bitcast.6, s32[4,16,32]{2,1,0:T(8,128)} %bitcast.8, bf16[256,1024]{1,0:T(8,128)(2,1)} %weight.1, bf16[4,256,256]{2,1,0:T(8,128)(2,1)} %constant.2.clone.table), custom_call_target="tpu_custom_call" | custom-call | flops 1000000000 | bytes 2097152 | tf_op jit(solution)/shard_map/extract/pallas_call | solution.py:112
  7.2 0.0 copy-start
  7.2 20.8 %all_to_all.5.refs_0_ = f32[16,8,128]{2,1,0:T(8,128)S(1)} all-to-all(f32[16,8,128]{2,1,0:T(8,128)} %get-tuple-element.10.sent), channel_id=1, replica_groups=mesh['zh'=4,'y'=4,'c'=2,'x'=4,'zl'=2] {'zh','y'}, dimensions={0} | all-to-all | bytes 131072 | tf_op jit(solution)/shard_map/all_to_all | solution.py:302
  28.1 2.1 %collective-permute-start = (f32[16,8,128]{2,1,0:T(8,128)S(1)}, f32[16,8,128]{2,1,0:T(8,128)S(1)}, u32[]{:S(2)}, u32[]{:S(2)}) collective-permute-start(f32[16,8,128]{2,1,0:T(8,128)S(1)} %all_to_all.5.refs_0_), channel_id=1, source_target_pairs={{0,8},{8,0},{1,9},{9,1},{2,10},{10,2},{3,11},{11,3},{4,12},{12,4},... | collective-permute-start | bytes 196616 | tf_op jit(solution)/shard_map/ppermute | solution.py:287
  30.2 0.9 %collective-permute-done.refs_1_ = f32[16,8,128]{2,1,0:T(8,128)S(1)} collective-permute-done((f32[16,8,128]{2,1,0:T(8,128)S(1)}, f32[16,8,128]{2,1,0:T(8,128)S(1)}, u32[]{:S(2)}, u32[]{:S(2)}) %collective-permute-start) | collective-permute-done | bytes 65568 | tf_op jit(solution)/shard_map/ppermute | solution.py:287
  31.1 0.0 copy-start.3
  31.1 1.0 %copy-done.3 = bf16[4,256,256]{2,1,0:T(8,128)(2,1)S(1)} copy-done((bf16[4,256,256]{2,1,0:T(8,128)(2,1)S(1)}, bf16[4,256,256]{2,1,0:T(8,128)(2,1)}, u32[]{:S(2)}) %copy-start.3) | copy-done | bytes 524312
  32.1 0.0 copy-start.4
  32.1 0.8 %copy-done.4 = bf16[256,128]{1,0:T(8,128)(2,1)S(1)} copy-done((bf16[256,128]{1,0:T(8,128)(2,1)S(1)}, bf16[256,128]{1,0:T(8,128)(2,1)}, u32[]{:S(2)}) %copy-start.4) | copy-done | bytes 65560
  32.9 2.4 %decode.1 = (bf16[1,256,128]{2,1,0:T(8,128)(2,1)S(1)}, bf16[1,256,128]{2,1,0:T(8,128)(2,1)S(1)}) custom-call(f32[16,8,128]{2,1,0:T(8,128)S(1)} %all_to_all.5.refs_0_, f32[16,8,128]{2,1,0:T(8,128)S(1)} %collective-permute-done.refs_1_, bf16[256,128]{1,0:T(8,128)(2,1)S(1)} %copy-done.4, bf16[4,256,256]{2,1,0:T(8,128)(2,1)S(1)} %copy-done.3), custom_call_target="tpu_custom_call" | custom-call | flops 1000000000 | bytes 1048576 | tf_op jit(solution)/shard_map/decode/pallas_call | solution.py:198
  35.3 0.8 %collective-permute-start.1 = (bf16[1,256,128]{2,1,0:T(8,128)(2,1)S(1)}, bf16[1,256,128]{2,1,0:T(8,128)(2,1)S(1)}, u32[]{:S(2)}, u32[]{:S(2)}) collective-permute-start(bf16[1,256,128]{2,1,0:T(8,128)(2,1)S(1)} %get-tuple-element.13.refs_0_), channel_id=1, source_target_pairs={{0,1},{1,0},{2,3},{3,2},{4,5},{5,4},{6,7},{7,6},{8,9},{9,8},{10,11... | collective-permute-start | bytes 196616 | tf_op jit(solution)/shard_map/ppermute | solution.py:287
  36.1 0.6 collective-permute-start.2
  36.8 1.8 %collective-permute-done.1.refs_1_ = bf16[1,256,128]{2,1,0:T(8,128)(2,1)S(1)} collective-permute-done((bf16[1,256,128]{2,1,0:T(8,128)(2,1)S(1)}, bf16[1,256,128]{2,1,0:T(8,128)(2,1)S(1)}, u32[]{:S(2)}, u32[]{:S(2)}) %collective-permute-start.1) | collective-permute-done | bytes 65568 | tf_op jit(solution)/shard_map/ppermute | solution.py:287
  38.5 0.0 collective-permute-done.2.refs_3_
  38.5 1.1 %collective-permute-start.5 = (bf16[4,256,128]{2,1,0:T(8,128)(2,1)S(1)}, bf16[4,256,128]{2,1,0:T(8,128)(2,1)S(1)}, u32[]{:S(2)}, u32[]{:S(2)}) collective-permute-start(bf16[4,256,128]{2,1,0:T(8,128)(2,1)S(1)} %join_near.1.refs_0_), channel_id=1, source_target_pairs={{0,6},{2,4},{4,2},{6,0},{8,56},{10,58},{12,60},{14,62},{16,22},{18... | collective-permute-start | bytes 786440 | tf_op jit(solution)/shard_map/ppermute | solution.py:296
  39.7 1.0 %collective-permute-start.4 = (bf16[4,256,128]{2,1,0:T(8,128)(2,1)S(1)}, bf16[4,256,128]{2,1,0:T(8,128)(2,1)S(1)}, u32[]{:S(2)}, u32[]{:S(2)}) collective-permute-start(bf16[4,256,128]{2,1,0:T(8,128)(2,1)S(1)} %join_near.1.refs_0_), channel_id=1, source_target_pairs={{0,4},{2,6},{4,0},{6,2},{8,40},{10,42},{12,44},{14,46},{16,20},{18... | collective-permute-start | bytes 786440 | tf_op jit(solution)/shard_map/ppermute | solution.py:296
  40.7 1.2 %collective-permute-start.3 = (bf16[4,256,128]{2,1,0:T(8,128)(2,1)S(1)}, bf16[4,256,128]{2,1,0:T(8,128)(2,1)S(1)}, u32[]{:S(2)}, u32[]{:S(2)}) collective-permute-start(bf16[4,256,128]{2,1,0:T(8,128)(2,1)S(1)} %join_near.1.refs_0_), channel_id=1, source_target_pairs={{0,2},{2,0},{4,6},{6,4},{8,24},{10,26},{12,28},{14,30},{16,18},{18... | collective-permute-start | bytes 786440 | tf_op jit(solution)/shard_map/ppermute | solution.py:296
  41.9 6.3 %collective-permute-done.5.refs_3_ = bf16[4,256,128]{2,1,0:T(8,128)(2,1)S(1)} collective-permute-done((bf16[4,256,128]{2,1,0:T(8,128)(2,1)S(1)}, bf16[4,256,128]{2,1,0:T(8,128)(2,1)S(1)}, u32[]{:S(2)}, u32[]{:S(2)}) %collective-permute-start.5) | collective-permute-done | bytes 262176 | tf_op jit(solution)/shard_map/ppermute | solution.py:296
  48.2 0.0 collective-permute-done.4.refs_2_
  48.2 0.6 collective-permute-done.3.refs_1_
  48.8 1.3 %collective-permute-start.12 = (bf16[8,256,128]{2,1,0:T(8,128)(2,1)S(1)}, bf16[8,256,128]{2,1,0:T(8,128)(2,1)S(1)}, u32[]{:S(2)}, u32[]{:S(2)}) collective-permute-start(bf16[8,256,128]{2,1,0:T(8,128)(2,1)S(1)} %join_far.1.refs_0_), channel_id=1, source_target_pairs={{0,16},{2,18},{4,20},{6,22},{8,10},{10,8},{12,14},{14,12},{16,0},{... | collective-permute-start | bytes 1572872 | tf_op jit(solution)/shard_map/ppermute | solution.py:296
  50.1 1.8 %collective-permute-start.9 = (bf16[8,256,128]{2,1,0:T(8,128)(2,1)S(1)}, bf16[8,256,128]{2,1,0:T(8,128)(2,1)S(1)}, u32[]{:S(2)}, u32[]{:S(2)}) collective-permute-start(bf16[8,256,128]{2,1,0:T(8,128)(2,1)S(1)} %join_far.1.refs_0_), channel_id=1, source_target_pairs={{0,48},{2,50},{4,52},{6,54},{8,14},{10,12},{12,10},{14,8},{16,32},... | collective-permute-start | bytes 1572872 | tf_op jit(solution)/shard_map/ppermute | solution.py:296
  51.9 0.6 collective-permute-start.7
  52.6 3.1 %collective-permute-start.11 = (bf16[8,256,128]{2,1,0:T(8,128)(2,1)S(1)}, bf16[8,256,128]{2,1,0:T(8,128)(2,1)S(1)}, u32[]{:S(2)}, u32[]{:S(2)}) collective-permute-start(bf16[8,256,128]{2,1,0:T(8,128)(2,1)S(1)} %join_far.1.refs_0_), channel_id=1, source_target_pairs={{0,8},{8,0},{1,9},{9,1},{2,10},{10,2},{3,11},{11,3},{4,12},{12,4},... | collective-permute-start | bytes 1572872 | tf_op jit(solution)/shard_map/ppermute | solution.py:287
  55.6 0.0 copy-done.1
  55.6 0.0 copy-done.2
  55.7 0.0 copy-done
  55.7 5.0 %kept.1 = (f32[256,1024]{1,0:T(8,128)}, bf16[256,1024]{1,0:T(8,128)(2,1)S(1)}) custom-call(f32[256,1024]{1,0:T(8,128)S(1)} %bitcast.5, bf16[256,1024]{1,0:T(8,128)(2,1)S(1)} %bitcast.7, f32[16,8,128]{2,1,0:T(8,128)S(1)} %copy-done, bf16[4,256,256]{2,1,0:T(8,128)(2,1)S(1)} %copy-done.3, bf16[4,256,128]{2,1,0:T(8,128)(2,1)S(1)} %join_near.1.refs_0_, ...), custom_call_target="tpu_custom_call" | custom-call | flops 2000000000 | bytes 3145728 | tf_op jit(solution)/shard_map/kept/pallas_call | solution.py:158
  60.6 0.0 collective-permute-start.6
  60.6 0.0 collective-permute-done.12.refs_2_
  60.6 0.5 collective-permute-start.13
  61.1 4.2 %collective-permute-done.9.refs_2_ = bf16[8,256,128]{2,1,0:T(8,128)(2,1)S(1)} collective-permute-done((bf16[8,256,128]{2,1,0:T(8,128)(2,1)S(1)}, bf16[8,256,128]{2,1,0:T(8,128)(2,1)S(1)}, u32[]{:S(2)}, u32[]{:S(2)}) %collective-permute-start.9) | collective-permute-done | bytes 524320 | tf_op jit(solution)/shard_map/ppermute | solution.py:296
  65.3 2.8 %collective-permute-start.10 = (bf16[8,256,128]{2,1,0:T(8,128)(2,1)S(1)}, bf16[8,256,128]{2,1,0:T(8,128)(2,1)S(1)}, u32[]{:S(2)}, u32[]{:S(2)}) collective-permute-start(bf16[8,256,128]{2,1,0:T(8,128)(2,1)S(1)} %collective-permute-done.9.refs_2_), channel_id=1, source_target_pairs={{0,8},{8,0},{1,9},{9,1},{2,10},{10,2},{3,11},{11,3},{4,12},{12,4},... | collective-permute-start | bytes 1572872 | tf_op jit(solution)/shard_map/ppermute | solution.py:287
  68.1 0.0 collective-permute-done.7.refs_0_
  68.1 0.0 collective-permute-start.8
  68.1 0.0 collective-permute-done.6.theirs
  68.1 0.8 %choose.1 = bf16[256,1024]{1,0:T(8,128)(2,1)} custom-call(bf16[256,1024]{1,0:T(8,128)(2,1)S(1)} %get-tuple-element.16.mine, bf16[256,1024]{1,0:T(8,128)(2,1)S(1)} %collective-permute-done.6.theirs), custom_call_target="tpu_custom_call" | custom-call | tf_op jit(solution)/shard_map/choose/pallas_call | solution.py:275
  69.0 0.0 collective-permute-done.11.refs_1_
  69.0 0.0 collective-permute-done.13.refs_3_
  69.0 1.6 %assemble_a.1.refs_4_ = bf16[256,8192]{1,0:T(8,128)(2,1)} custom-call(bf16[8,256,128]{2,1,0:T(8,128)(2,1)S(1)} %join_far.1.refs_0_, bf16[8,256,128]{2,1,0:T(8,128)(2,1)S(1)} %collective-permute-done.11.refs_1_, bf16[8,256,128]{2,1,0:T(8,128)(2,1)S(1)} %collective-permute-done.12.refs_2_, bf16[8,256,128]{2,1,0:T(8,128)(2,1)S(1)} %collective-permute-done.13.refs_3_), custom_call_target="tpu_custom_call" | custom-call | bytes 2097152 | tf_op jit(solution)/shard_map/assemble_a/pallas_call | solution.py:251
  70.6 0.0 collective-permute-done.10.refs_3_
  70.6 0.0 collective-permute-done.8.refs_1_
  70.6 1.6 %assemble_b.1 = bf16[256,8192]{1,0:T(8,128)(2,1)} custom-call(bf16[8,256,128]{2,1,0:T(8,128)(2,1)S(1)} %collective-permute-done.7.refs_0_, bf16[8,256,128]{2,1,0:T(8,128)(2,1)S(1)} %collective-permute-done.8.refs_1_, bf16[8,256,128]{2,1,0:T(8,128)(2,1)S(1)} %collective-permute-done.9.refs_2_, ...), custom_call_target="tpu_custom_call", output_to_operand_aliasing={{}: (4, {})} | custom-call | bytes 2097152 | tf_op jit(solution)/shard_map/assemble_b/pallas_call | solution.py:251
  (2 shorter events, 0.1 us)
Async XLA Ops:
  0.6 55.0 %copy-start.1 = (f32[1,256,1024]{2,1,0:T(8,128)S(1)}, f32[1,256,1024]{2,1,0:T(8,128)}, u32[]{:S(2)}) copy-start(f32[1,256,1024]{2,1,0:T(8,128)} %param.6) | copy-start | bytes 3145732
  0.6 55.0 %copy-start.2 = (bf16[1,256,1024]{2,1,0:T(8,128)(2,1)S(1)}, bf16[1,256,1024]{2,1,0:T(8,128)(2,1)}, u32[]{:S(2)}) copy-start(bf16[1,256,1024]{2,1,0:T(8,128)(2,1)} %param.7) | copy-start | bytes 1572868
  7.2 48.4 %copy-start = (f32[16,8,128]{2,1,0:T(8,128)S(1)}, f32[16,8,128]{2,1,0:T(8,128)}, u32[]{:S(2)}) copy-start(f32[16,8,128]{2,1,0:T(8,128)} %get-tuple-element.10.sent) | copy-start | bytes 196612
  28.1 3.0 %collective-permute-start = (f32[16,8,128]{2,1,0:T(8,128)S(1)}, f32[16,8,128]{2,1,0:T(8,128)S(1)}, u32[]{:S(2)}, u32[]{:S(2)}) collective-permute-start(f32[16,8,128]{2,1,0:T(8,128)S(1)} %all_to_all.5.refs_0_), channel_id=1, source_target_pairs={{0,8},{8,0},{1,9},{9,1},{2,10},{10,2},{3,11},{11,3},{4,12},{12,4},... | collective-permute-start | bytes 196616 | tf_op jit(solution)/shard_map/ppermute | solution.py:287
  31.1 1.0 %copy-start.3 = (bf16[4,256,256]{2,1,0:T(8,128)(2,1)S(1)}, bf16[4,256,256]{2,1,0:T(8,128)(2,1)}, u32[]{:S(2)}) copy-start(bf16[4,256,256]{2,1,0:T(8,128)(2,1)} %get-tuple-element.11.refs_3_.basis) | copy-start | bytes 1572868
  32.1 0.8 %copy-start.4 = (bf16[256,128]{1,0:T(8,128)(2,1)S(1)}, bf16[256,128]{1,0:T(8,128)(2,1)}, u32[]{:S(2)}) copy-start(bf16[256,128]{1,0:T(8,128)(2,1)} %get-tuple-element.12.refs_2_) | copy-start | bytes 196612
  35.3 3.2 %collective-permute-start.1 = (bf16[1,256,128]{2,1,0:T(8,128)(2,1)S(1)}, bf16[1,256,128]{2,1,0:T(8,128)(2,1)S(1)}, u32[]{:S(2)}, u32[]{:S(2)}) collective-permute-start(bf16[1,256,128]{2,1,0:T(8,128)(2,1)S(1)} %get-tuple-element.13.refs_0_), channel_id=1, source_target_pairs={{0,1},{1,0},{2,3},{3,2},{4,5},{5,4},{6,7},{7,6},{8,9},{9,8},{10,11... | collective-permute-start | bytes 196616 | tf_op jit(solution)/shard_map/ppermute | solution.py:287
  36.1 2.4 %collective-permute-start.2 = (bf16[1,256,128]{2,1,0:T(8,128)(2,1)S(1)}, bf16[1,256,128]{2,1,0:T(8,128)(2,1)S(1)}, u32[]{:S(2)}, u32[]{:S(2)}) collective-permute-start(bf16[1,256,128]{2,1,0:T(8,128)(2,1)S(1)} %get-tuple-element.14.refs_2_), channel_id=1, source_target_pairs={{0,8},{8,0},{1,9},{9,1},{2,10},{10,2},{3,11},{11,3},{4,12},{12,4},... | collective-permute-start | bytes 196616 | tf_op jit(solution)/shard_map/ppermute | solution.py:287
  38.5 9.6 %collective-permute-start.5 = (bf16[4,256,128]{2,1,0:T(8,128)(2,1)S(1)}, bf16[4,256,128]{2,1,0:T(8,128)(2,1)S(1)}, u32[]{:S(2)}, u32[]{:S(2)}) collective-permute-start(bf16[4,256,128]{2,1,0:T(8,128)(2,1)S(1)} %join_near.1.refs_0_), channel_id=1, source_target_pairs={{0,6},{2,4},{4,2},{6,0},{8,56},{10,58},{12,60},{14,62},{16,22},{18... | collective-permute-start | bytes 786440 | tf_op jit(solution)/shard_map/ppermute | solution.py:296
  39.7 8.5 %collective-permute-start.4 = (bf16[4,256,128]{2,1,0:T(8,128)(2,1)S(1)}, bf16[4,256,128]{2,1,0:T(8,128)(2,1)S(1)}, u32[]{:S(2)}, u32[]{:S(2)}) collective-permute-start(bf16[4,256,128]{2,1,0:T(8,128)(2,1)S(1)} %join_near.1.refs_0_), channel_id=1, source_target_pairs={{0,4},{2,6},{4,0},{6,2},{8,40},{10,42},{12,44},{14,46},{16,20},{18... | collective-permute-start | bytes 786440 | tf_op jit(solution)/shard_map/ppermute | solution.py:296
  40.7 8.1 %collective-permute-start.3 = (bf16[4,256,128]{2,1,0:T(8,128)(2,1)S(1)}, bf16[4,256,128]{2,1,0:T(8,128)(2,1)S(1)}, u32[]{:S(2)}, u32[]{:S(2)}) collective-permute-start(bf16[4,256,128]{2,1,0:T(8,128)(2,1)S(1)} %join_near.1.refs_0_), channel_id=1, source_target_pairs={{0,2},{2,0},{4,6},{6,4},{8,24},{10,26},{12,28},{14,30},{16,18},{18... | collective-permute-start | bytes 786440 | tf_op jit(solution)/shard_map/ppermute | solution.py:296
  48.8 11.8 %collective-permute-start.12 = (bf16[8,256,128]{2,1,0:T(8,128)(2,1)S(1)}, bf16[8,256,128]{2,1,0:T(8,128)(2,1)S(1)}, u32[]{:S(2)}, u32[]{:S(2)}) collective-permute-start(bf16[8,256,128]{2,1,0:T(8,128)(2,1)S(1)} %join_far.1.refs_0_), channel_id=1, source_target_pairs={{0,16},{2,18},{4,20},{6,22},{8,10},{10,8},{12,14},{14,12},{16,0},{... | collective-permute-start | bytes 1572872 | tf_op jit(solution)/shard_map/ppermute | solution.py:296
  50.1 15.2 %collective-permute-start.9 = (bf16[8,256,128]{2,1,0:T(8,128)(2,1)S(1)}, bf16[8,256,128]{2,1,0:T(8,128)(2,1)S(1)}, u32[]{:S(2)}, u32[]{:S(2)}) collective-permute-start(bf16[8,256,128]{2,1,0:T(8,128)(2,1)S(1)} %join_far.1.refs_0_), channel_id=1, source_target_pairs={{0,48},{2,50},{4,52},{6,54},{8,14},{10,12},{12,10},{14,8},{16,32},... | collective-permute-start | bytes 1572872 | tf_op jit(solution)/shard_map/ppermute | solution.py:296
  51.9 16.2 %collective-permute-start.7 = (bf16[8,256,128]{2,1,0:T(8,128)(2,1)S(1)}, bf16[8,256,128]{2,1,0:T(8,128)(2,1)S(1)}, u32[]{:S(2)}, u32[]{:S(2)}) collective-permute-start(bf16[8,256,128]{2,1,0:T(8,128)(2,1)S(1)} %join_far.1.refs_0_), channel_id=1, source_target_pairs={{0,32},{2,34},{4,36},{6,38},{8,12},{10,14},{12,8},{14,10},{16,48},... | collective-permute-start | bytes 1572872 | tf_op jit(solution)/shard_map/ppermute | solution.py:296
  52.6 16.4 %collective-permute-start.11 = (bf16[8,256,128]{2,1,0:T(8,128)(2,1)S(1)}, bf16[8,256,128]{2,1,0:T(8,128)(2,1)S(1)}, u32[]{:S(2)}, u32[]{:S(2)}) collective-permute-start(bf16[8,256,128]{2,1,0:T(8,128)(2,1)S(1)} %join_far.1.refs_0_), channel_id=1, source_target_pairs={{0,8},{8,0},{1,9},{9,1},{2,10},{10,2},{3,11},{11,3},{4,12},{12,4},... | collective-permute-start | bytes 1572872 | tf_op jit(solution)/shard_map/ppermute | solution.py:287
  60.6 7.5 %collective-permute-start.6 = (bf16[256,1024]{1,0:T(8,128)(2,1)S(1)}, bf16[256,1024]{1,0:T(8,128)(2,1)S(1)}, u32[]{:S(2)}, u32[]{:S(2)}) collective-permute-start(bf16[256,1024]{1,0:T(8,128)(2,1)S(1)} %get-tuple-element.16.mine), channel_id=1, source_target_pairs={{0,8},{8,0},{1,9},{9,1},{2,10},{10,2},{3,11},{11,3},{4,12},{12,4},... | collective-permute-start | bytes 1572872 | tf_op jit(solution)/shard_map/ppermute | solution.py:287
  60.6 8.3 %collective-permute-start.13 = (bf16[8,256,128]{2,1,0:T(8,128)(2,1)S(1)}, bf16[8,256,128]{2,1,0:T(8,128)(2,1)S(1)}, u32[]{:S(2)}, u32[]{:S(2)}) collective-permute-start(bf16[8,256,128]{2,1,0:T(8,128)(2,1)S(1)} %collective-permute-done.12.refs_2_), channel_id=1, source_target_pairs={{0,8},{8,0},{1,9},{9,1},{2,10},{10,2},{3,11},{11,3},{4,12},{12,4},... | collective-permute-start | bytes 1572872 | tf_op jit(solution)/shard_map/ppermute | solution.py:287
  65.3 5.3 %collective-permute-start.10 = (bf16[8,256,128]{2,1,0:T(8,128)(2,1)S(1)}, bf16[8,256,128]{2,1,0:T(8,128)(2,1)S(1)}, u32[]{:S(2)}, u32[]{:S(2)}) collective-permute-start(bf16[8,256,128]{2,1,0:T(8,128)(2,1)S(1)} %collective-permute-done.9.refs_2_), channel_id=1, source_target_pairs={{0,8},{8,0},{1,9},{9,1},{2,10},{10,2},{3,11},{11,3},{4,12},{12,4},... | collective-permute-start | bytes 1572872 | tf_op jit(solution)/shard_map/ppermute | solution.py:287
  68.1 2.5 %collective-permute-start.8 = (bf16[8,256,128]{2,1,0:T(8,128)(2,1)S(1)}, bf16[8,256,128]{2,1,0:T(8,128)(2,1)S(1)}, u32[]{:S(2)}, u32[]{:S(2)}) collective-permute-start(bf16[8,256,128]{2,1,0:T(8,128)(2,1)S(1)} %collective-permute-done.7.refs_0_), channel_id=1, source_target_pairs={{0,8},{8,0},{1,9},{9,1},{2,10},{10,2},{3,11},{11,3},{4,12},{12,4},... | collective-permute-start | bytes 1572872 | tf_op jit(solution)/shard_map/ppermute | solution.py:287

commit v4 on v3

v4 whole, which is shorter than its diff:
```python
import functools
import math

import jax
import jax.numpy as jnp
import numpy as np
from jax import lax
from jax.experimental import pallas as pl
from jax.experimental.pallas import tpu as pltpu
from jax.sharding import Mesh
from jax.sharding import PartitionSpec as P

GROUP = 64
REPLICA = ("zh", "y", "c")
SHARD = ("x", "zl")
beta_decay = 0.9
step_rate = 0.02
F32, BF16 = jnp.float32, jnp.bfloat16
VMEM = pl.BlockSpec(memory_space=pltpu.VMEM)
ANY = pl.BlockSpec(memory_space=pl.ANY)
HBM = pl.BlockSpec(memory_space=pltpu.HBM)


def limit(mib):
    return pltpu.CompilerParams(vmem_limit_bytes=int(mib * 2**20))


def basis_parts():
    freq, cells = np.arange(GROUP)[:, None], np.arange(GROUP)[None, :]
    scales = np.where(freq == 0, math.sqrt(1.0 / GROUP), math.sqrt(2.0 / GROUP))
    table = scales * np.cos(math.pi * (2.0 * cells + 1.0) * freq / (2.0 * GROUP))
    four = np.kron(np.eye(4), table)
    high = four.astype(jnp.bfloat16)
    low = (four - high.astype(np.float64)).astype(jnp.bfloat16)
    return np.stack([high, low, high.T, low.T])


def two_parts(value):
    high = value.astype(BF16)
    return high, (value - high.astype(F32)).astype(BF16)


def rows_by_rows(left, right):
    return lax.dot_general(left, right, (((1,), (1,)), ((), ())), preferred_element_type=F32)


def rows_by_cols(left, right):
    return lax.dot_general(left, right, (((1,), (0,)), ((), ())), preferred_element_type=F32)


def product(dot, left, right):
    return dot(left[0], right[0]) + dot(left[0], right[1]) + dot(left[1], right[0])


def one_hot_rows(place, lines, dtype):
    line = lax.broadcasted_iota(jnp.int32, (lines, place.shape[1]), 0)
    return jnp.where(line == place, 1.0, 0.0).astype(dtype)


def split_place(flat):
    lane = lax.broadcasted_iota(jnp.int32, flat.shape, 1)
    return (flat >> 6) + ((lane >> 5) << 6), flat & 63


def spread(values, column):
    line = lax.broadcasted_iota(jnp.int32, (GROUP, values.shape[1]), 0)
    return two_parts(jnp.where(line == column, values, 0.0))


def extract_kernel(momentum, grad, positions, table, out, m_in, g_in, p_in, basis, places, sems):
    copies = []
    for half in range(2):
        columns = pl.ds(512 * half, 512)
        copies.append((momentum.at[:, columns], m_in.at[half]))
        copies.append((grad.at[:, columns], g_in.at[half]))
        if half == 0:
            copies.append((table.at[pl.ds(0, 2)], basis))
            copies.append((positions, p_in))
    copies = [pltpu.make_async_copy(*pair, sems.at[n]) for n, pair in enumerate(copies)]
    for copy in copies:
        copy.start()
    for half in range(2):
        for copy in copies[4:] if half else copies[:4]:
            copy.wait()
        if half == 0:
            for x in range(4):
                places[:, 32 * x : 32 * x + 32] = p_in[x]
        straight = (basis[0], basis[1])
        moved = beta_decay * m_in[half] + g_in[half].astype(F32)
        moved = [two_parts(moved[:, 256 * g : 256 * g + 256]) for g in range(2)]
        rows = [two_parts(product(rows_by_rows, straight, value)) for value in moved]
        coeff = [two_parts(product(rows_by_rows, value, straight)) for value in rows]
        for g in range(2):
            lines = []
            for q in range(4):
                at = 8 * half + 4 * g + q
                flat = places[at : at + 1, :]
                row, column = split_place(flat)
                block = jnp.concatenate([part[GROUP * q : GROUP * (q + 1)] for part in coeff[g]], axis=0)
                found = rows_by_cols(block, one_hot_rows(row, 4 * GROUP, BF16))
                found = found[:GROUP] + found[GROUP:]
                line = lax.broadcasted_iota(jnp.int32, found.shape, 0)
                lines.append(jnp.sum(jnp.where(line == column, found, 0.0), axis=0, keepdims=True))
                lines.append(flat.astype(F32))
            tile = jnp.concatenate(lines, axis=0)
            for z in range(4):
                out[4 * z + 2 * half + g] = tile


def extract(momentum, grad, positions, table):
    return pl.pallas_call(
        extract_kernel,
        in_specs=[HBM] * 4,
        out_specs=VMEM,
        out_shape=jax.ShapeDtypeStruct((16, 8, 128), F32),
        scratch_shapes=[
            pltpu.VMEM((2, 256, 512), F32),
            pltpu.VMEM((2, 256, 512), BF16),
            pltpu.VMEM((4, 16, 32), jnp.int32),
            pltpu.VMEM((2, 256, 256), BF16),
            pltpu.VMEM((16, 128), jnp.int32),
            pltpu.SemaphoreType.DMA((6,)),
        ],
        cost_estimate=pl.CostEstimate(flops=10**9, bytes_accessed=2 * 2**20, transcendentals=0),
        compiler_params=limit(59),
        name="extract",
    )(momentum, grad, positions, table)


def kept_kernel(momentum, grad, sent, basis, out, token):
    straight, turned = (basis[0], basis[1]), (basis[2], basis[3])
    grids = []
    for g in range(2):
        tile, blocks = sent[g], []
        for q in range(4):
            row, column = split_place(tile[2 * q + 1 : 2 * q + 2].astype(jnp.int32))
            high, low = spread(tile[2 * q : 2 * q + 1], column)
            hot = one_hot_rows(row, 4 * GROUP, BF16)
            blocks.append(rows_by_rows(high, hot) + rows_by_rows(low, hot))
        grids.append(two_parts(jnp.concatenate(blocks, axis=0)))
    half = [two_parts(product(rows_by_rows, turned, grid)) for grid in grids]
    dense = [product(rows_by_cols, value, straight) for value in half]
    moved = beta_decay * momentum[...] + grad[...].astype(F32)
    for g in range(2):
        columns = slice(256 * g, 256 * g + 256)
        out[:, columns] = moved[:, columns] - dense[g]
    token[...] = jnp.zeros_like(token)


def kept(momentum, grad, sent, table):
    block = pl.BlockSpec((256, 512), lambda g: (0, g))
    whole = lambda *shape: pl.BlockSpec(shape, lambda g: (0,) * len(shape))
    return pl.pallas_call(
        kept_kernel,
        grid=(2,),
        in_specs=[block, block, pl.BlockSpec((2, 8, 128), lambda g: (g, 0, 0)), whole(4, 256, 256)],
        out_specs=[block, whole(8, 128)],
        out_shape=[jax.ShapeDtypeStruct((256, 1024), F32), jax.ShapeDtypeStruct((8, 128), F32)],
        cost_estimate=pl.CostEstimate(flops=2 * 10**9, bytes_accessed=3 * 2**20, transcendentals=0),
        compiler_params=limit(12),
        name="kept",
    )(momentum, grad, sent, table)


def decode_kernel(*refs):
    entries, (weight, basis, fresh, smooth_out) = refs[:2], refs[2:]
    core = lax.axis_index("c")
    place = pl.multiple_of((lax.axis_index("y") * 2 + core) * 128, 128)
    tiles = []
    for ref in entries:
        for source in range(16):
            tile = ref[source]
            tiles.append(jnp.where(core == 0, tile[:4], tile[4:]))
    totals = [jnp.zeros((2 * GROUP, 4 * GROUP), F32)] * 2
    for pair in range(0, len(tiles), 2):
        for j in range(2):
            lefts, hots = [], []
            for tile in tiles[pair : pair + 2]:
                row, line = split_place(tile[2 * j + 1 : 2 * j + 2].astype(jnp.int32))
                lefts.append(jnp.concatenate(spread(tile[2 * j : 2 * j + 1], line), axis=0))
                hots.append(one_hot_rows(row, 4 * GROUP, BF16))
            found = rows_by_rows(jnp.concatenate(lefts, axis=1), jnp.concatenate(hots, axis=1))
            totals[j] = totals[j] + found
    blocks = [total[:GROUP] + total[GROUP:] for total in totals]
    grid = two_parts(jnp.concatenate(blocks, axis=0))
    half = product(rows_by_rows, (basis[2], basis[3]), grid)
    dense = product(rows_by_cols, two_parts(half), (basis[0, :128, :128], basis[1, :128, :128]))
    smooth = jnp.tanh(dense)
    smooth_out[0] = smooth.astype(BF16)
    fresh[0] = (weight[:, pl.ds(place, 128)].astype(F32) - step_rate * smooth).astype(BF16)


def decode(entries, weight, table):
    return pl.pallas_call(
        decode_kernel,
        in_specs=[VMEM] * 4,
        out_specs=[VMEM] * 2,
        out_shape=[jax.ShapeDtypeStruct((1, 256, 128), BF16)] * 2,
        cost_estimate=pl.CostEstimate(flops=10**9, bytes_accessed=2**20, transcendentals=32768),
        compiler_params=limit(12),
        name="decode",
    )(*entries, weight, table)


def near_kernel(a, b, c, d, out):
    for k, ref in enumerate((a, b, c, d)):
        out[k] = ref[0]


def join_near(arrays):
    return pl.pallas_call(
        near_kernel,
        in_specs=[VMEM] * 4,
        out_specs=VMEM,
        out_shape=jax.ShapeDtypeStruct((4, 256, 128), BF16),
        compiler_params=limit(4),
        name="join_near",
    )(*arrays)


def own_kernel(a, b, c, d, token, out):
    for k, ref in enumerate((a, b, c, d)):
        out[k] = ref[0]


def join_own(arrays, token):
    return pl.pallas_call(
        own_kernel,
        in_specs=[VMEM] * 4 + [ANY],
        out_specs=VMEM,
        out_shape=jax.ShapeDtypeStruct((4, 256, 128), BF16),
        compiler_params=limit(4),
        name="join_own",
    )(*arrays, token)


def far_kernel(own, a, b, c, d, out):
    out[:4] = own[...]
    for k, ref in enumerate((a, b, c, d)):
        out[4 + k] = ref[1]


def join_far(own, arrays):
    return pl.pallas_call(
        far_kernel,
        in_specs=[VMEM] * 5,
        out_specs=VMEM,
        out_shape=jax.ShapeDtypeStruct((8, 256, 128), BF16),
        compiler_params=limit(4),
        name="join_far",
    )(own, *arrays)


def piece_copies(groups, pieces, out, sems):
    core, x, y, zl = (lax.axis_index(name) for name in ("c", "x", "y", "zl"))
    copies = []
    for n, (k2, zs) in enumerate(groups):
        for other in range(2):
            at_core = jnp.bitwise_xor(core, other)
            for i, dz in enumerate(zs):
                for k1 in range(4):
                    dx = jnp.where(at_core == 0, k1, k2)
                    dy = jnp.where(at_core == 0, k2, k1)
                    shard = jnp.bitwise_xor(x, dx) * 2 + jnp.bitwise_xor(zl, dz)
                    tile = shard * 8 + jnp.bitwise_xor(y, dy) * 2 + at_core
                    columns = pl.ds(pl.multiple_of(tile * 128, 128), 128)
                    copies.append(
                        pltpu.make_async_copy(
                            pieces[2 * n + other].at[4 * i + k1], out.at[:, columns], sems.at[len(copies)]
                        )
                    )
    return copies


def count_copies(groups):
    return sum(8 * len(zs) for _, zs in groups)


NEW_WEIGHT = jax.ShapeDtypeStruct((256, 8192), BF16)
LAID = jax.ShapeDtypeStruct((256, 1024), BF16)


def lay_kernel(groups, *refs):
    firsts, pieces, (laid, out, sems) = refs[:4], refs[4:-3], refs[-3:]
    copies = piece_copies(groups, pieces, out, sems)
    for copy in copies:
        copy.start()
    core, y = lax.axis_index("c"), lax.axis_index("y")
    for k in range(4):
        for other in range(2):
            tile = jnp.bitwise_xor(y, k) * 2 + jnp.bitwise_xor(core, other)
            laid[:, pl.ds(pl.multiple_of(tile * 128, 128), 128)] = firsts[k][2 + other]
    for copy in copies:
        copy.wait()


def lay(firsts, groups, pieces):
    return pl.pallas_call(
        functools.partial(lay_kernel, groups),
        in_specs=[VMEM] * 4 + [ANY] * len(pieces),
        out_specs=[VMEM, ANY],
        out_shape=[LAID, NEW_WEIGHT],
        scratch_shapes=[pltpu.SemaphoreType.DMA((count_copies(groups),))],
        compiler_params=limit(4),
        name="lay",
    )(*firsts, *pieces)


def choose_kernel(groups, mine, theirs, *refs):
    pieces, (direction, out, sems, sem) = refs[: 2 * len(groups)], refs[-4:]
    copies = piece_copies(groups, pieces, out, sems)
    for copy in copies:
        copy.start()
    for core, source in enumerate((theirs, mine)):

        @pl.when(lax.axis_index("c") == core)
        def _():
            copy = pltpu.make_async_copy(source, direction, sem)
            copy.start()
            copy.wait()

    for copy in copies:
        copy.wait()


def choose(mine, theirs, groups, pieces, done):
    return pl.pallas_call(
        functools.partial(choose_kernel, groups),
        in_specs=[ANY] * (3 + len(pieces)),
        out_specs=[ANY] * 2,
        out_shape=[LAID, NEW_WEIGHT],
        scratch_shapes=[pltpu.SemaphoreType.DMA((count_copies(groups),)), pltpu.SemaphoreType.DMA],
        input_output_aliases={2 + len(pieces): 1},
        compiler_params=limit(1),
        name="choose",
    )(mine, theirs, *pieces, done)


def finish_kernel(groups, *refs):
    pieces, (out, sems) = refs[: 2 * len(groups)], refs[-2:]
    copies = piece_copies(groups, pieces, out, sems)
    for copy in copies:
        copy.start()
    for copy in copies:
        copy.wait()


def finish(groups, pieces, done):
    return pl.pallas_call(
        functools.partial(finish_kernel, groups),
        in_specs=[ANY] * (1 + len(pieces)),
        out_specs=ANY,
        out_shape=NEW_WEIGHT,
        scratch_shapes=[pltpu.SemaphoreType.DMA((count_copies(groups),))],
        input_output_aliases={len(pieces): 0},
        compiler_params=limit(1),
        name="finish",
    )(*pieces, done)


def swapped(array, axis, size, k):
    return lax.ppermute(array, axis, [(i, i ^ k) for i in range(size)])


def crossed(array, first, k):
    perm = []
    for i in range(32):
        y, c, x = i >> 3, (i >> 2) & 1, i & 3
        to = (y, c, x ^ k) if c == first else (y ^ k, c, x)
        perm.append((i, (to[0] << 3) | (to[1] << 2) | to[2]))
    return lax.ppermute(array, ("y", "c", "x"), perm)


def other_core(array):
    return swapped(array, "c", 2, 1)


def per_device(weight, momentum, grad, positions):
    table = jnp.asarray(basis_parts())
    sent = extract(momentum[0], grad[0], positions[0], table)
    arrived = lax.all_to_all(sent, ("zh", "y"), 0, 0, tiled=True)
    fresh, smooth = decode([arrived, other_core(arrived)], other_core(weight), other_core(table))
    near = join_near([fresh, swapped(fresh, "zl", 2, 1), smooth, other_core(smooth)])
    firsts = [near] + [crossed(near, 0, k) for k in (1, 2, 3)]
    kept_state, token = kept(momentum[0], grad[0], sent, table)
    own = join_own(firsts, token)
    two = crossed(own, 1, 2)
    far = join_far(own, firsts)
    one, three = crossed(far, 1, 1), crossed(far, 1, 3)
    two_z = swapped(two, "zl", 2, 1)
    both = lambda array: [array, other_core(array)]
    laid, new_weight = lay(firsts, [(0, (0, 1))], both(far))
    direction, new_weight = choose(
        laid,
        other_core(laid),
        [(1, (0, 1)), (2, (0,)), (2, (1,))],
        both(one) + both(two) + both(two_z),
        new_weight,
    )
    new_weight = finish([(3, (0, 1))], both(three), new_weight)
    return (kept_state[None], direction, new_weight)


def solution(mesh):
    split = Mesh(mesh.devices.reshape(4, 4, 2, 4, 2), ("zh", "y", "c", "x", "zl"))
    in_specs = (
        P(None, SHARD),
        P(REPLICA, None, SHARD),
        P(REPLICA, None, SHARD),
        P(REPLICA, None, SHARD, None),
    )
    out_specs = (P(REPLICA, None, SHARD), P(None, SHARD), P())
    return jax.shard_map(
        per_device, mesh=split, in_specs=in_specs, out_specs=out_specs, check_vma=False
    )
```

time: 72.5 us -> 74.8 us (1.032)
  starting transfers between devices: 17 us -> 24.3 us
  Pallas kernels: 17.9 us -> 13.4 us
  waiting for transfers between devices: 13.7 us -> 17.7 us
  blocking collectives: 20.8 us -> 18.3 us
  local copies, waits for them, and re-layouts: 1.89 us -> 0.02 us
    ppermute x8 -> x12, starting transfers between devices: 9.94 us -> 17.1 us  [swapped(): return lax.ppermute(array, axis, [(i, i ^ k) for i in range(size)])]
    pallas_call x7 -> x8, Pallas kernels: 15.6 us -> 11.1 us  [the longest x1 3.77 us: extract(): pl.pallas_call(extract_kernel, in_specs=[HBM] * 4, out_specs=VMEM, out_sh...]
    ppermute x8 -> x12, waiting for transfers between devices: 2.68 us -> 5.31 us  [swapped(): return lax.ppermute(array, axis, [(i, i ^ k) for i in range(size)])]
    all_to_all x1, blocking collectives: 20.8 us -> 18.3 us  [per_device(): arrived = lax.all_to_all(sent, ('zh', 'y'), 0, 0, tiled=True)]
    unnamed x10 -> x8, local copies, waits for them, and re-layouts: 1.89 us -> 0.02 us
    ppermute x6, waiting for transfers between devices: 11.1 us -> 12.4 us  [crossed(): return lax.ppermute(array, ('y', 'c', 'x'), perm)]
  transfers between devices with their start and end apart: 14 -> 18, of which waited for: 5 -> 7; matrix products, arithmetic and copies ran while one was open for 0% -> 0% of each run, Pallas kernels for 10% -> 13%
where the time goes in v4:
time: 74.8 us; the launch traced here: 74.6 us
  starting transfers between devices  24.3 us (32%)
  blocking collectives  18.3 us (24%)
  waiting for transfers between devices  17.7 us (24%)
  Pallas kernels  13.4 us (18%)
  between operations  0.9 us (1%)
    all_to_all x1, blocking collectives, per_device(): arrived = lax.all_to_all(sent, ('zh', 'y'), 0, 0, tiled=True)  18.3 us
    ppermute x12, starting transfers between devices, swapped(): return lax.ppermute(array, axis, [(i, i ^ k) for i in range(size)])  17.1 us
    ppermute x6, waiting for transfers between devices, crossed(): return lax.ppermute(array, ('y', 'c', 'x'), perm)  12.4 us
    ppermute x6, starting transfers between devices, crossed(): return lax.ppermute(array, ('y', 'c', 'x'), perm)  7.2 us
    ppermute x12, waiting for transfers between devices, swapped(): return lax.ppermute(array, axis, [(i, i ^ k) for i in range(size)])  5.31 us
    pallas_call x1, Pallas kernels, extract(): pl.pallas_call(extract_kernel, in_specs=[HBM] * 4, out_specs=VMEM, out_sh...  3.77 us
    pallas_call x1, Pallas kernels, kept(): pl.pallas_call(kept_kernel, grid=(2,), in_specs=[block, block, pl.BlockSp...  3.2 us
    pallas_call x1, Pallas kernels, decode(): pl.pallas_call(decode_kernel, in_specs=[VMEM] * 4, out_specs=[VMEM] * 2,...  2.3 us
  transfers between devices with their start and end apart: 18, of which 7 were waited for; matrix products, arithmetic and copies ran while one was open for 0% of the time, Pallas kernels for 13%

profile of v4, /device:TPU:1, one launch (start us, length us, event | category | flops | bytes accessed | tf_op | source)
XLA Modules:
  0.0 74.6 jit_solution(13909818526726139954)
XLA Ops:
  0.6 0.0 copy-start.3
  0.6 0.0 copy-start.1
  0.7 0.0 copy-start.2
  0.7 3.3 %collective-permute-start.1 = (bf16[256,1024]{1,0:T(8,128)(2,1)}, bf16[256,1024]{1,0:T(8,128)(2,1)S(1)}, u32[]{:S(2)}, u32[]{:S(2)}) collective-permute-start(bf16[256,1024]{1,0:T(8,128)(2,1)} %param.5), channel_id=1, source_target_pairs={{0,8},{8,0},{1,9},{9,1},{2,10},{10,2},{3,11},{11,3},{4,12},{12,4},... | collective-permute-start | bytes 1572872 | tf_op jit(solution)/shard_map/ppermute | solution.py:362
  4.0 0.1 collective-permute-start.2
  4.1 3.8 %extract.1.sent = f32[16,8,128]{2,1,0:T(8,128)} custom-call(f32[256,1024]{1,0:T(8,128)} %bitcast.4, bf16[256,1024]{1,0:T(8,128)(2,1)} %bitcast.6, s32[4,16,32]{2,1,0:T(8,128)} %bitcast.8, bf16[4,256,256]{2,1,0:T(8,128)(2,1)} %constant.2.clone.table.basis), custom_call_target="tpu_custom_call" | custom-call | flops 1000000000 | bytes 2097152 | tf_op jit(solution)/shard_map/extract/pallas_call | solution.py:111
  7.9 0.0 copy-start
  7.9 18.3 %all_to_all.5.refs_0_ = f32[16,8,128]{2,1,0:T(8,128)S(1)} all-to-all(f32[16,8,128]{2,1,0:T(8,128)} %extract.1.sent), channel_id=1, replica_groups=mesh['zh'=4,'y'=4,'c'=2,'x'=4,'zl'=2] {'zh','y'}, dimensions={0} | all-to-all | bytes 131072 | tf_op jit(solution)/shard_map/all_to_all | solution.py:381
  26.1 2.0 %collective-permute-start = (f32[16,8,128]{2,1,0:T(8,128)S(1)}, f32[16,8,128]{2,1,0:T(8,128)S(1)}, u32[]{:S(2)}, u32[]{:S(2)}) collective-permute-start(f32[16,8,128]{2,1,0:T(8,128)S(1)} %all_to_all.5.refs_0_), channel_id=1, source_target_pairs={{0,8},{8,0},{1,9},{9,1},{2,10},{10,2},{3,11},{11,3},{4,12},{12,4},... | collective-permute-start | bytes 196616 | tf_op jit(solution)/shard_map/ppermute | solution.py:362
  28.1 0.9 %collective-permute-done.refs_1_ = f32[16,8,128]{2,1,0:T(8,128)S(1)} collective-permute-done((f32[16,8,128]{2,1,0:T(8,128)S(1)}, f32[16,8,128]{2,1,0:T(8,128)S(1)}, u32[]{:S(2)}, u32[]{:S(2)}) %collective-permute-start) | collective-permute-done | bytes 65568 | tf_op jit(solution)/shard_map/ppermute | solution.py:362
  29.0 0.0 collective-permute-done.1.refs_2_
  29.0 0.0 collective-permute-done.2.refs_3_
  29.0 2.3 %decode.1 = (bf16[1,256,128]{2,1,0:T(8,128)(2,1)S(1)}, bf16[1,256,128]{2,1,0:T(8,128)(2,1)S(1)}) custom-call(f32[16,8,128]{2,1,0:T(8,128)S(1)} %all_to_all.5.refs_0_, f32[16,8,128]{2,1,0:T(8,128)S(1)} %collective-permute-done.refs_1_, bf16[256,1024]{1,0:T(8,128)(2,1)S(1)} %collective-permute-done.1.refs_2_, ...), custom_call_target="tpu_custom_call" | custom-call | flops 1000000000 | bytes 1048576 | tf_op jit(solution)/shard_map/decode/pallas_call | solution.py:194
  31.3 0.7 collective-permute-start.3
  32.0 0.6 collective-permute-start.4
  32.7 1.9 %collective-permute-done.3.b = bf16[1,256,128]{2,1,0:T(8,128)(2,1)S(1)} collective-permute-done((bf16[1,256,128]{2,1,0:T(8,128)(2,1)S(1)}, bf16[1,256,128]{2,1,0:T(8,128)(2,1)S(1)}, u32[]{:S(2)}, u32[]{:S(2)}) %collective-permute-start.3) | collective-permute-done | bytes 65568 | tf_op jit(solution)/shard_map/ppermute | solution.py:362
  34.5 0.0 collective-permute-done.4.d
  34.6 0.4 collective-permute-start.5
  34.9 1.8 %collective-permute-start.6 = (bf16[4,256,128]{2,1,0:T(8,128)(2,1)S(1)}, bf16[4,256,128]{2,1,0:T(8,128)(2,1)S(1)}, u32[]{:S(2)}, u32[]{:S(2)}) collective-permute-start(bf16[4,256,128]{2,1,0:T(8,128)(2,1)S(1)} %join_near.1.a.refs_0_), channel_id=1, source_target_pairs={{0,4},{2,6},{4,0},{6,2},{8,40},{10,42},{12,44},{14,46},{16,20},{18... | collective-permute-start | bytes 786440 | tf_op jit(solution)/shard_map/ppermute | solution.py:371
  36.7 1.8 %collective-permute-start.7 = (bf16[4,256,128]{2,1,0:T(8,128)(2,1)S(1)}, bf16[4,256,128]{2,1,0:T(8,128)(2,1)S(1)}, u32[]{:S(2)}, u32[]{:S(2)}) collective-permute-start(bf16[4,256,128]{2,1,0:T(8,128)(2,1)S(1)} %join_near.1.a.refs_0_), channel_id=1, source_target_pairs={{0,6},{2,4},{4,2},{6,0},{8,56},{10,58},{12,60},{14,62},{16,22},{18... | collective-permute-start | bytes 786440 | tf_op jit(solution)/shard_map/ppermute | solution.py:371
  38.5 0.0 copy-done.3
  38.5 0.0 copy-done.1
  38.5 0.0 copy-done.2
  38.5 0.0 copy-done
  38.5 3.2 %kept.1 = (f32[256,1024]{1,0:T(8,128)}, f32[8,128]{1,0:T(8,128)S(1)}) custom-call(f32[256,1024]{1,0:T(8,128)S(1)} %bitcast.5, bf16[256,1024]{1,0:T(8,128)(2,1)S(1)} %bitcast.7, f32[16,8,128]{2,1,0:T(8,128)S(1)} %copy-done, bf16[4,256,256]{2,1,0:T(8,128)(2,1)S(1)} %copy-done.3), custom_call_target="tpu_custom_call" | custom-call | flops 2000000000 | bytes 3145728 | tf_op jit(solution)/shard_map/kept/pallas_call | solution.py:153
  41.7 0.0 collective-permute-done.5.b.refs_1_
  41.7 1.7 %collective-permute-done.6.c.refs_2_ = bf16[4,256,128]{2,1,0:T(8,128)(2,1)S(1)} collective-permute-done((bf16[4,256,128]{2,1,0:T(8,128)(2,1)S(1)}, bf16[4,256,128]{2,1,0:T(8,128)(2,1)S(1)}, u32[]{:S(2)}, u32[]{:S(2)}) %collective-permute-start.6) | collective-permute-done | bytes 262176 | tf_op jit(solution)/shard_map/ppermute | solution.py:371
  43.4 2.9 %collective-permute-done.7.d.refs_3_ = bf16[4,256,128]{2,1,0:T(8,128)(2,1)S(1)} collective-permute-done((bf16[4,256,128]{2,1,0:T(8,128)(2,1)S(1)}, bf16[4,256,128]{2,1,0:T(8,128)(2,1)S(1)}, u32[]{:S(2)}, u32[]{:S(2)}) %collective-permute-start.7) | collective-permute-done | bytes 262176 | tf_op jit(solution)/shard_map/ppermute | solution.py:371
  46.3 4.2 %collective-permute-start.8 = (bf16[8,256,128]{2,1,0:T(8,128)(2,1)S(1)}, bf16[8,256,128]{2,1,0:T(8,128)(2,1)S(1)}, u32[]{:S(2)}, u32[]{:S(2)}) collective-permute-start(bf16[8,256,128]{2,1,0:T(8,128)(2,1)S(1)} %join_far.1.refs_4_), channel_id=1, source_target_pairs={{0,8},{8,0},{1,9},{9,1},{2,10},{10,2},{3,11},{11,3},{4,12},{12,4},... | collective-permute-start | bytes 1572872 | tf_op jit(solution)/shard_map/ppermute | solution.py:362
  50.5 0.0 collective-permute-start.10
  50.5 0.2 collective-permute-start.16
  50.7 3.1 %collective-permute-start.12 = (bf16[4,256,128]{2,1,0:T(8,128)(2,1)S(1)}, bf16[4,256,128]{2,1,0:T(8,128)(2,1)S(1)}, u32[]{:S(2)}, u32[]{:S(2)}) collective-permute-start(bf16[4,256,128]{2,1,0:T(8,128)(2,1)S(1)} %join_own.1.own), channel_id=1, source_target_pairs={{0,32},{2,34},{4,36},{6,38},{8,12},{10,14},{12,8},{14,10},{16,48},... | collective-permute-start | bytes 786440 | tf_op jit(solution)/shard_map/ppermute | solution.py:371
  53.8 7.8 %collective-permute-done.12.refs_2_ = bf16[4,256,128]{2,1,0:T(8,128)(2,1)S(1)} collective-permute-done((bf16[4,256,128]{2,1,0:T(8,128)(2,1)S(1)}, bf16[4,256,128]{2,1,0:T(8,128)(2,1)S(1)}, u32[]{:S(2)}, u32[]{:S(2)}) %collective-permute-start.12) | collective-permute-done | bytes 262176 | tf_op jit(solution)/shard_map/ppermute | solution.py:371
  61.6 0.6 collective-permute-start.14
  62.2 0.0 collective-permute-done.8.refs_5_
  62.2 1.2 %lay.1 = (bf16[256,1024]{1,0:T(8,128)(2,1)S(1)}, bf16[256,8192]{1,0:T(8,128)(2,1)}) custom-call(bf16[4,256,128]{2,1,0:T(8,128)(2,1)S(1)} %join_near.1.a.refs_0_, bf16[4,256,128]{2,1,0:T(8,128)(2,1)S(1)} %collective-permute-done.5.b.refs_1_, bf16[4,256,128]{2,1,0:T(8,128)(2,1)S(1)} %collective-permute-done.6.c.refs_2_, ...), custom_call_target="tpu_custom_call" | custom-call | tf_op jit(solution)/shard_map/lay/pallas_call | solution.py:298
  63.4 2.3 %collective-permute-start.9 = (bf16[256,1024]{1,0:T(8,128)(2,1)S(1)}, bf16[256,1024]{1,0:T(8,128)(2,1)S(1)}, u32[]{:S(2)}, u32[]{:S(2)}) collective-permute-start(bf16[256,1024]{1,0:T(8,128)(2,1)S(1)} %get-tuple-element.15.mine), channel_id=1, source_target_pairs={{0,8},{8,0},{1,9},{9,1},{2,10},{10,2},{3,11},{11,3},{4,12},{12,4},... | collective-permute-start | bytes 1572872 | tf_op jit(solution)/shard_map/ppermute | solution.py:362
  65.7 0.0 collective-permute-done.10.refs_0_
  65.7 0.1 collective-permute-start.11
  65.8 0.0 collective-permute-done.16.refs_0_
  65.8 0.4 collective-permute-start.17
  66.2 0.1 collective-permute-start.13
  66.3 1.4 %collective-permute-done.14.refs_4_ = bf16[4,256,128]{2,1,0:T(8,128)(2,1)S(1)} collective-permute-done((bf16[4,256,128]{2,1,0:T(8,128)(2,1)S(1)}, bf16[4,256,128]{2,1,0:T(8,128)(2,1)S(1)}, u32[]{:S(2)}, u32[]{:S(2)}) %collective-permute-start.14) | collective-permute-done | bytes 262176 | tf_op jit(solution)/shard_map/ppermute | solution.py:362
  67.7 2.6 %collective-permute-start.15 = (bf16[4,256,128]{2,1,0:T(8,128)(2,1)S(1)}, bf16[4,256,128]{2,1,0:T(8,128)(2,1)S(1)}, u32[]{:S(2)}, u32[]{:S(2)}) collective-permute-start(bf16[4,256,128]{2,1,0:T(8,128)(2,1)S(1)} %collective-permute-done.14.refs_4_), channel_id=1, source_target_pairs={{0,8},{8,0},{1,9},{9,1},{2,10},{10,2},{3,11},{11,3},{4,12},{12,4},... | collective-permute-start | bytes 786440 | tf_op jit(solution)/shard_map/ppermute | solution.py:362
  70.3 0.0 collective-permute-done.13.refs_3_
  70.3 1.2 %collective-permute-done.15.refs_5_ = bf16[4,256,128]{2,1,0:T(8,128)(2,1)S(1)} collective-permute-done((bf16[4,256,128]{2,1,0:T(8,128)(2,1)S(1)}, bf16[4,256,128]{2,1,0:T(8,128)(2,1)S(1)}, u32[]{:S(2)}, u32[]{:S(2)}) %collective-permute-start.15) | collective-permute-done | bytes 262176 | tf_op jit(solution)/shard_map/ppermute | solution.py:362
  71.5 0.0 collective-permute-done.9.theirs
  71.5 0.0 collective-permute-done.11.refs_1_
  71.5 1.8 %choose.1 = (bf16[256,1024]{1,0:T(8,128)(2,1)}, bf16[256,8192]{1,0:T(8,128)(2,1)}) custom-call(bf16[256,1024]{1,0:T(8,128)(2,1)S(1)} %get-tuple-element.15.mine, bf16[256,1024]{1,0:T(8,128)(2,1)S(1)} %collective-permute-done.9.theirs, bf16[8,256,128]{2,1,0:T(8,128)(2,1)S(1)} %collective-permute-done.10.refs_0_, ...), custom_call_target="tpu_custom_call", output_to_operand_aliasing={{1}: (8, {})} | custom-call | tf_op jit(solution)/shard_map/choose/pallas_call | solution.py:327
  73.3 0.0 collective-permute-done.17.refs_1_
  73.3 1.1 %finish.1 = bf16[256,8192]{1,0:T(8,128)(2,1)} custom-call(bf16[8,256,128]{2,1,0:T(8,128)(2,1)S(1)} %collective-permute-done.16.refs_0_, bf16[8,256,128]{2,1,0:T(8,128)(2,1)S(1)} %collective-permute-done.17.refs_1_, bf16[256,8192]{1,0:T(8,128)(2,1)} %get-tuple-element.18.refs_2_), custom_call_target="tpu_custom_call", output_to_operand_aliasing={{}: (2, {})} | custom-call | tf_op jit(solution)/shard_map/finish/pallas_call | solution.py:349
  (3 shorter events, 0.1 us)
Async XLA Ops:
  0.6 37.9 %copy-start.3 = (bf16[4,256,256]{2,1,0:T(8,128)(2,1)S(1)}, bf16[4,256,256]{2,1,0:T(8,128)(2,1)}, u32[]{:S(2)}) copy-start(bf16[4,256,256]{2,1,0:T(8,128)(2,1)} %constant.2.clone.table.basis) | copy-start | bytes 1572868
  0.6 37.9 %copy-start.1 = (f32[1,256,1024]{2,1,0:T(8,128)S(1)}, f32[1,256,1024]{2,1,0:T(8,128)}, u32[]{:S(2)}) copy-start(f32[1,256,1024]{2,1,0:T(8,128)} %param.6) | copy-start | bytes 3145732
  0.7 37.9 %copy-start.2 = (bf16[1,256,1024]{2,1,0:T(8,128)(2,1)S(1)}, bf16[1,256,1024]{2,1,0:T(8,128)(2,1)}, u32[]{:S(2)}) copy-start(bf16[1,256,1024]{2,1,0:T(8,128)(2,1)} %param.7) | copy-start | bytes 1572868
  0.7 28.4 %collective-permute-start.1 = (bf16[256,1024]{1,0:T(8,128)(2,1)}, bf16[256,1024]{1,0:T(8,128)(2,1)S(1)}, u32[]{:S(2)}, u32[]{:S(2)}) collective-permute-start(bf16[256,1024]{1,0:T(8,128)(2,1)} %param.5), channel_id=1, source_target_pairs={{0,8},{8,0},{1,9},{9,1},{2,10},{10,2},{3,11},{11,3},{4,12},{12,4},... | collective-permute-start | bytes 1572872 | tf_op jit(solution)/shard_map/ppermute | solution.py:362
  4.0 25.0 %collective-permute-start.2 = (bf16[4,256,256]{2,1,0:T(8,128)(2,1)}, bf16[4,256,256]{2,1,0:T(8,128)(2,1)S(1)}, u32[]{:S(2)}, u32[]{:S(2)}) collective-permute-start(bf16[4,256,256]{2,1,0:T(8,128)(2,1)} %constant.2.clone.table.basis), channel_id=1, source_target_pairs={{0,8},{8,0},{1,9},{9,1},{2,10},{10,2},{3,11},{11,3},{4,12},{12,4},... | collective-permute-start | bytes 1572872 | tf_op jit(solution)/shard_map/ppermute | solution.py:362
  7.9 30.7 %copy-start = (f32[16,8,128]{2,1,0:T(8,128)S(1)}, f32[16,8,128]{2,1,0:T(8,128)}, u32[]{:S(2)}) copy-start(f32[16,8,128]{2,1,0:T(8,128)} %extract.1.sent) | copy-start | bytes 196612
  26.1 2.9 %collective-permute-start = (f32[16,8,128]{2,1,0:T(8,128)S(1)}, f32[16,8,128]{2,1,0:T(8,128)S(1)}, u32[]{:S(2)}, u32[]{:S(2)}) collective-permute-start(f32[16,8,128]{2,1,0:T(8,128)S(1)} %all_to_all.5.refs_0_), channel_id=1, source_target_pairs={{0,8},{8,0},{1,9},{9,1},{2,10},{10,2},{3,11},{11,3},{4,12},{12,4},... | collective-permute-start | bytes 196616 | tf_op jit(solution)/shard_map/ppermute | solution.py:362
  31.3 3.2 %collective-permute-start.3 = (bf16[1,256,128]{2,1,0:T(8,128)(2,1)S(1)}, bf16[1,256,128]{2,1,0:T(8,128)(2,1)S(1)}, u32[]{:S(2)}, u32[]{:S(2)}) collective-permute-start(bf16[1,256,128]{2,1,0:T(8,128)(2,1)S(1)} %get-tuple-element.12.a), channel_id=1, source_target_pairs={{0,1},{1,0},{2,3},{3,2},{4,5},{5,4},{6,7},{7,6},{8,9},{9,8},{10,11... | collective-permute-start | bytes 196616 | tf_op jit(solution)/shard_map/ppermute | solution.py:362
  32.0 2.5 %collective-permute-start.4 = (bf16[1,256,128]{2,1,0:T(8,128)(2,1)S(1)}, bf16[1,256,128]{2,1,0:T(8,128)(2,1)S(1)}, u32[]{:S(2)}, u32[]{:S(2)}) collective-permute-start(bf16[1,256,128]{2,1,0:T(8,128)(2,1)S(1)} %get-tuple-element.13.c), channel_id=1, source_target_pairs={{0,8},{8,0},{1,9},{9,1},{2,10},{10,2},{3,11},{11,3},{4,12},{12,4},... | collective-permute-start | bytes 196616 | tf_op jit(solution)/shard_map/ppermute | solution.py:362
  34.6 7.2 %collective-permute-start.5 = (bf16[4,256,128]{2,1,0:T(8,128)(2,1)S(1)}, bf16[4,256,128]{2,1,0:T(8,128)(2,1)S(1)}, u32[]{:S(2)}, u32[]{:S(2)}) collective-permute-start(bf16[4,256,128]{2,1,0:T(8,128)(2,1)S(1)} %join_near.1.a.refs_0_), channel_id=1, source_target_pairs={{0,2},{2,0},{4,6},{6,4},{8,24},{10,26},{12,28},{14,30},{16,18},{18... | collective-permute-start | bytes 786440 | tf_op jit(solution)/shard_map/ppermute | solution.py:371
  34.9 8.5 %collective-permute-start.6 = (bf16[4,256,128]{2,1,0:T(8,128)(2,1)S(1)}, bf16[4,256,128]{2,1,0:T(8,128)(2,1)S(1)}, u32[]{:S(2)}, u32[]{:S(2)}) collective-permute-start(bf16[4,256,128]{2,1,0:T(8,128)(2,1)S(1)} %join_near.1.a.refs_0_), channel_id=1, source_target_pairs={{0,4},{2,6},{4,0},{6,2},{8,40},{10,42},{12,44},{14,46},{16,20},{18... | collective-permute-start | bytes 786440 | tf_op jit(solution)/shard_map/ppermute | solution.py:371
  36.7 9.5 %collective-permute-start.7 = (bf16[4,256,128]{2,1,0:T(8,128)(2,1)S(1)}, bf16[4,256,128]{2,1,0:T(8,128)(2,1)S(1)}, u32[]{:S(2)}, u32[]{:S(2)}) collective-permute-start(bf16[4,256,128]{2,1,0:T(8,128)(2,1)S(1)} %join_near.1.a.refs_0_), channel_id=1, source_target_pairs={{0,6},{2,4},{4,2},{6,0},{8,56},{10,58},{12,60},{14,62},{16,22},{18... | collective-permute-start | bytes 786440 | tf_op jit(solution)/shard_map/ppermute | solution.py:371
  46.3 15.9 %collective-permute-start.8 = (bf16[8,256,128]{2,1,0:T(8,128)(2,1)S(1)}, bf16[8,256,128]{2,1,0:T(8,128)(2,1)S(1)}, u32[]{:S(2)}, u32[]{:S(2)}) collective-permute-start(bf16[8,256,128]{2,1,0:T(8,128)(2,1)S(1)} %join_far.1.refs_4_), channel_id=1, source_target_pairs={{0,8},{8,0},{1,9},{9,1},{2,10},{10,2},{3,11},{11,3},{4,12},{12,4},... | collective-permute-start | bytes 1572872 | tf_op jit(solution)/shard_map/ppermute | solution.py:362
  50.5 15.2 %collective-permute-start.10 = (bf16[8,256,128]{2,1,0:T(8,128)(2,1)S(1)}, bf16[8,256,128]{2,1,0:T(8,128)(2,1)S(1)}, u32[]{:S(2)}, u32[]{:S(2)}) collective-permute-start(bf16[8,256,128]{2,1,0:T(8,128)(2,1)S(1)} %join_far.1.refs_4_), channel_id=1, source_target_pairs={{0,16},{2,18},{4,20},{6,22},{8,10},{10,8},{12,14},{14,12},{16,0},{... | collective-permute-start | bytes 1572872 | tf_op jit(solution)/shard_map/ppermute | solution.py:371
  50.5 15.3 %collective-permute-start.16 = (bf16[8,256,128]{2,1,0:T(8,128)(2,1)S(1)}, bf16[8,256,128]{2,1,0:T(8,128)(2,1)S(1)}, u32[]{:S(2)}, u32[]{:S(2)}) collective-permute-start(bf16[8,256,128]{2,1,0:T(8,128)(2,1)S(1)} %join_far.1.refs_4_), channel_id=1, source_target_pairs={{0,48},{2,50},{4,52},{6,54},{8,14},{10,12},{12,10},{14,8},{16,32},... | collective-permute-start | bytes 1572872 | tf_op jit(solution)/shard_map/ppermute | solution.py:371
  50.7 10.9 %collective-permute-start.12 = (bf16[4,256,128]{2,1,0:T(8,128)(2,1)S(1)}, bf16[4,256,128]{2,1,0:T(8,128)(2,1)S(1)}, u32[]{:S(2)}, u32[]{:S(2)}) collective-permute-start(bf16[4,256,128]{2,1,0:T(8,128)(2,1)S(1)} %join_own.1.own), channel_id=1, source_target_pairs={{0,32},{2,34},{4,36},{6,38},{8,12},{10,14},{12,8},{14,10},{16,48},... | collective-permute-start | bytes 786440 | tf_op jit(solution)/shard_map/ppermute | solution.py:371
  61.6 6.1 %collective-permute-start.14 = (bf16[4,256,128]{2,1,0:T(8,128)(2,1)S(1)}, bf16[4,256,128]{2,1,0:T(8,128)(2,1)S(1)}, u32[]{:S(2)}, u32[]{:S(2)}) collective-permute-start(bf16[4,256,128]{2,1,0:T(8,128)(2,1)S(1)} %collective-permute-done.12.refs_2_), channel_id=1, source_target_pairs={{0,1},{1,0},{2,3},{3,2},{4,5},{5,4},{6,7},{7,6},{8,9},{9,8},{10,11... | collective-permute-start | bytes 786440 | tf_op jit(solution)/shard_map/ppermute | solution.py:362
  63.4 8.1 %collective-permute-start.9 = (bf16[256,1024]{1,0:T(8,128)(2,1)S(1)}, bf16[256,1024]{1,0:T(8,128)(2,1)S(1)}, u32[]{:S(2)}, u32[]{:S(2)}) collective-permute-start(bf16[256,1024]{1,0:T(8,128)(2,1)S(1)} %get-tuple-element.15.mine), channel_id=1, source_target_pairs={{0,8},{8,0},{1,9},{9,1},{2,10},{10,2},{3,11},{11,3},{4,12},{12,4},... | collective-permute-start | bytes 1572872 | tf_op jit(solution)/shard_map/ppermute | solution.py:362
  65.7 5.8 %collective-permute-start.11 = (bf16[8,256,128]{2,1,0:T(8,128)(2,1)S(1)}, bf16[8,256,128]{2,1,0:T(8,128)(2,1)S(1)}, u32[]{:S(2)}, u32[]{:S(2)}) collective-permute-start(bf16[8,256,128]{2,1,0:T(8,128)(2,1)S(1)} %collective-permute-done.10.refs_0_), channel_id=1, source_target_pairs={{0,8},{8,0},{1,9},{9,1},{2,10},{10,2},{3,11},{11,3},{4,12},{12,4},... | collective-permute-start | bytes 1572872 | tf_op jit(solution)/shard_map/ppermute | solution.py:362
  65.8 7.5 %collective-permute-start.17 = (bf16[8,256,128]{2,1,0:T(8,128)(2,1)S(1)}, bf16[8,256,128]{2,1,0:T(8,128)(2,1)S(1)}, u32[]{:S(2)}, u32[]{:S(2)}) collective-permute-start(bf16[8,256,128]{2,1,0:T(8,128)(2,1)S(1)} %collective-permute-done.16.refs_0_), channel_id=1, source_target_pairs={{0,8},{8,0},{1,9},{9,1},{2,10},{10,2},{3,11},{11,3},{4,12},{12,4},... | collective-permute-start | bytes 1572872 | tf_op jit(solution)/shard_map/ppermute | solution.py:362
  66.2 4.1 %collective-permute-start.13 = (bf16[4,256,128]{2,1,0:T(8,128)(2,1)S(1)}, bf16[4,256,128]{2,1,0:T(8,128)(2,1)S(1)}, u32[]{:S(2)}, u32[]{:S(2)}) collective-permute-start(bf16[4,256,128]{2,1,0:T(8,128)(2,1)S(1)} %collective-permute-done.12.refs_2_), channel_id=1, source_target_pairs={{0,8},{8,0},{1,9},{9,1},{2,10},{10,2},{3,11},{11,3},{4,12},{12,4},... | collective-permute-start | bytes 786440 | tf_op jit(solution)/shard_map/ppermute | solution.py:362
  67.7 3.8 %collective-permute-start.15 = (bf16[4,256,128]{2,1,0:T(8,128)(2,1)S(1)}, bf16[4,256,128]{2,1,0:T(8,128)(2,1)S(1)}, u32[]{:S(2)}, u32[]{:S(2)}) collective-permute-start(bf16[4,256,128]{2,1,0:T(8,128)(2,1)S(1)} %collective-permute-done.14.refs_4_), channel_id=1, source_target_pairs={{0,8},{8,0},{1,9},{9,1},{2,10},{10,2},{3,11},{11,3},{4,12},{12,4},... | collective-permute-start | bytes 786440 | tf_op jit(solution)/shard_map/ppermute | solution.py:362

commit v5 on v4

--- a/solution.py
+++ b/solution.py
@@ -17,6 +17,7 @@
 step_rate = 0.02
 F32, BF16 = jnp.float32, jnp.bfloat16
 VMEM = pl.BlockSpec(memory_space=pltpu.VMEM)
+RING = (1, 3, 2)
 ANY = pl.BlockSpec(memory_space=pl.ANY)
 HBM = pl.BlockSpec(memory_space=pltpu.HBM)
 
@@ -127,7 +128,7 @@
     )(momentum, grad, positions, table)
 
 
-def kept_kernel(momentum, grad, sent, basis, out, token):
+def kept_kernel(momentum, grad, sent, basis, far, out, token):
     straight, turned = (basis[0], basis[1]), (basis[2], basis[3])
     grids = []
     for g in range(2):
@@ -147,19 +148,19 @@
     token[...] = jnp.zeros_like(token)
 
 
-def kept(momentum, grad, sent, table):
+def kept(momentum, grad, sent, table, far):
     block = pl.BlockSpec((256, 512), lambda g: (0, g))
     whole = lambda *shape: pl.BlockSpec(shape, lambda g: (0,) * len(shape))
     return pl.pallas_call(
         kept_kernel,
         grid=(2,),
-        in_specs=[block, block, pl.BlockSpec((2, 8, 128), lambda g: (g, 0, 0)), whole(4, 256, 256)],
+        in_specs=[block, block, pl.BlockSpec((2, 8, 128), lambda g: (g, 0, 0)), whole(4, 256, 256), ANY],
         out_specs=[block, whole(8, 128)],
         out_shape=[jax.ShapeDtypeStruct((256, 1024), F32), jax.ShapeDtypeStruct((8, 128), F32)],
         cost_estimate=pl.CostEstimate(flops=2 * 10**9, bytes_accessed=3 * 2**20, transcendentals=0),
         compiler_params=limit(12),
         name="kept",
-    )(momentum, grad, sent, table)
+    )(momentum, grad, sent, table, far)
 
 
 def decode_kernel(*refs):
@@ -218,62 +219,49 @@
     )(*arrays)
 
 
-def own_kernel(a, b, c, d, token, out):
+def far_kernel(a, b, c, d, out):
     for k, ref in enumerate((a, b, c, d)):
         out[k] = ref[0]
-
-
-def join_own(arrays, token):
-    return pl.pallas_call(
-        own_kernel,
-        in_specs=[VMEM] * 4 + [ANY],
-        out_specs=VMEM,
-        out_shape=jax.ShapeDtypeStruct((4, 256, 128), BF16),
-        compiler_params=limit(4),
-        name="join_own",
-    )(*arrays, token)
-
-
-def far_kernel(own, a, b, c, d, out):
-    out[:4] = own[...]
-    for k, ref in enumerate((a, b, c, d)):
         out[4 + k] = ref[1]
 
 
-def join_far(own, arrays):
+def join_far(arrays):
     return pl.pallas_call(
         far_kernel,
-        in_specs=[VMEM] * 5,
+        in_specs=[VMEM] * 4,
         out_specs=VMEM,
         out_shape=jax.ShapeDtypeStruct((8, 256, 128), BF16),
         compiler_params=limit(4),
         name="join_far",
-    )(own, *arrays)
+    )(*arrays)
 
 
 def piece_copies(groups, pieces, out, sems):
     core, x, y, zl = (lax.axis_index(name) for name in ("c", "x", "y", "zl"))
     copies = []
-    for n, (k2, zs) in enumerate(groups):
-        for other in range(2):
+    at = 0
+    for k2, zs, others in groups:
+        for other in others:
             at_core = jnp.bitwise_xor(core, other)
             for i, dz in enumerate(zs):
                 for k1 in range(4):
-                    dx = jnp.where(at_core == 0, k1, k2)
-                    dy = jnp.where(at_core == 0, k2, k1)
+                    first, second = (0, *RING)[k1], (0, *RING)[k2]
+                    dx = jnp.where(at_core == 0, first, second)
+                    dy = jnp.where(at_core == 0, second, first)
                     shard = jnp.bitwise_xor(x, dx) * 2 + jnp.bitwise_xor(zl, dz)
                     tile = shard * 8 + jnp.bitwise_xor(y, dy) * 2 + at_core
                     columns = pl.ds(pl.multiple_of(tile * 128, 128), 128)
                     copies.append(
                         pltpu.make_async_copy(
-                            pieces[2 * n + other].at[4 * i + k1], out.at[:, columns], sems.at[len(copies)]
+                            pieces[at].at[4 * i + k1], out.at[:, columns], sems.at[len(copies)]
                         )
                     )
+            at += 1
     return copies
 
 
 def count_copies(groups):
-    return sum(8 * len(zs) for _, zs in groups)
+    return sum(4 * len(zs) * len(others) for _, zs, others in groups)
 
 
 NEW_WEIGHT = jax.ShapeDtypeStruct((256, 8192), BF16)
@@ -281,33 +269,33 @@
 
 
 def lay_kernel(groups, *refs):
-    firsts, pieces, (laid, out, sems) = refs[:4], refs[4:-3], refs[-3:]
+    firsts, pieces, (laid, out, sems) = refs[:4], refs[5:-3], refs[-3:]
     copies = piece_copies(groups, pieces, out, sems)
     for copy in copies:
         copy.start()
     core, y = lax.axis_index("c"), lax.axis_index("y")
     for k in range(4):
         for other in range(2):
-            tile = jnp.bitwise_xor(y, k) * 2 + jnp.bitwise_xor(core, other)
+            tile = jnp.bitwise_xor(y, (0, *RING)[k]) * 2 + jnp.bitwise_xor(core, other)
             laid[:, pl.ds(pl.multiple_of(tile * 128, 128), 128)] = firsts[k][2 + other]
     for copy in copies:
         copy.wait()
 
 
-def lay(firsts, groups, pieces):
+def lay(firsts, token, groups, pieces):
     return pl.pallas_call(
         functools.partial(lay_kernel, groups),
-        in_specs=[VMEM] * 4 + [ANY] * len(pieces),
+        in_specs=[VMEM] * 4 + [ANY] * (1 + len(pieces)),
         out_specs=[VMEM, ANY],
         out_shape=[LAID, NEW_WEIGHT],
         scratch_shapes=[pltpu.SemaphoreType.DMA((count_copies(groups),))],
         compiler_params=limit(4),
         name="lay",
-    )(*firsts, *pieces)
+    )(*firsts, token, *pieces)
 
 
 def choose_kernel(groups, mine, theirs, *refs):
-    pieces, (direction, out, sems, sem) = refs[: 2 * len(groups)], refs[-4:]
+    pieces, (direction, out, sems, sem) = refs[:-5], refs[-4:]
     copies = piece_copies(groups, pieces, out, sems)
     for copy in copies:
         copy.start()
@@ -337,7 +325,7 @@
 
 
 def finish_kernel(groups, *refs):
-    pieces, (out, sems) = refs[: 2 * len(groups)], refs[-2:]
+    pieces, (out, sems) = refs[:-3], refs[-2:]
     copies = piece_copies(groups, pieces, out, sems)
     for copy in copies:
         copy.start()
@@ -381,23 +369,20 @@
     arrived = lax.all_to_all(sent, ("zh", "y"), 0, 0, tiled=True)
     fresh, smooth = decode([arrived, other_core(arrived)], other_core(weight), other_core(table))
     near = join_near([fresh, swapped(fresh, "zl", 2, 1), smooth, other_core(smooth)])
-    firsts = [near] + [crossed(near, 0, k) for k in (1, 2, 3)]
-    kept_state, token = kept(momentum[0], grad[0], sent, table)
-    own = join_own(firsts, token)
-    two = crossed(own, 1, 2)
-    far = join_far(own, firsts)
-    one, three = crossed(far, 1, 1), crossed(far, 1, 3)
-    two_z = swapped(two, "zl", 2, 1)
+    firsts = [near] + [crossed(near, 0, k) for k in RING]
+    far = join_far(firsts)
+    kept_state, token = kept(momentum[0], grad[0], sent, table, far)
+    one, two, three = (crossed(far, 1, k) for k in RING)
     both = lambda array: [array, other_core(array)]
-    laid, new_weight = lay(firsts, [(0, (0, 1))], both(far))
+    laid, new_weight = lay(firsts, token, [(0, (0, 1), (0,))], [far])
     direction, new_weight = choose(
         laid,
         other_core(laid),
-        [(1, (0, 1)), (2, (0,)), (2, (1,))],
-        both(one) + both(two) + both(two_z),
+        [(0, (0, 1), (1,)), (1, (0, 1), (0, 1))],
+        [other_core(far)] + both(one),
         new_weight,
     )
-    new_weight = finish([(3, (0, 1))], both(three), new_weight)
+    new_weight = finish([(2, (0, 1), (0, 1)), (3, (0, 1), (0, 1))], both(two) + both(three), new_weight)
     return (kept_state[None], direction, new_weight)
 
 

time: 74.8 us -> 68.7 us (0.918)
  waiting for transfers between devices: 17.7 us -> 11.8 us
    ppermute x6, waiting for transfers between devices: 12.4 us -> 8.42 us  [crossed(): return lax.ppermute(array, ('y', 'c', 'x'), perm)]
    ppermute x12 -> x10, waiting for transfers between devices: 5.31 us -> 3.36 us  [swapped(): return lax.ppermute(array, axis, [(i, i ^ k) for i in range(size)])]
    ppermute x12 -> x10, starting transfers between devices: 17.1 us -> 17.2 us  [swapped(): return lax.ppermute(array, axis, [(i, i ^ k) for i in range(size)])]
  transfers between devices with their start and end apart: 18 -> 16, of which waited for: 7 -> 6; matrix products, arithmetic and copies ran while one was open for 0% -> 0% of each run, Pallas kernels for 13% -> 14%
where the time goes in v5:
time: 68.7 us; the launch traced here: 68.6 us
  starting transfers between devices  24.2 us (35%)
  blocking collectives  18.3 us (27%)
  Pallas kernels  13.5 us (20%)
  waiting for transfers between devices  11.8 us (17%)
  between operations  0.73 us (1%)
    all_to_all x1, blocking collectives, per_device(): arrived = lax.all_to_all(sent, ('zh', 'y'), 0, 0, tiled=True)  18.3 us
    ppermute x10, starting transfers between devices, swapped(): return lax.ppermute(array, axis, [(i, i ^ k) for i in range(size)])  17.2 us
    ppermute x6, waiting for transfers between devices, crossed(): return lax.ppermute(array, ('y', 'c', 'x'), perm)  8.42 us
    ppermute x6, starting transfers between devices, crossed(): return lax.ppermute(array, ('y', 'c', 'x'), perm)  7.08 us
    pallas_call x1, Pallas kernels, extract(): pl.pallas_call(extract_kernel, in_specs=[HBM] * 4, out_specs=VMEM, out_sh...  3.91 us
    ppermute x10, waiting for transfers between devices, swapped(): return lax.ppermute(array, axis, [(i, i ^ k) for i in range(size)])  3.36 us
    pallas_call x1, Pallas kernels, kept(): pl.pallas_call(kept_kernel, grid=(2,), in_specs=[block, block, pl.BlockSp...  3.2 us
    pallas_call x1, Pallas kernels, decode(): pl.pallas_call(decode_kernel, in_specs=[VMEM] * 4, out_specs=[VMEM] * 2,...  2.3 us
  transfers between devices with their start and end apart: 16, of which 6 were waited for; matrix products, arithmetic and copies ran while one was open for 0% of the time, Pallas kernels for 14%

profile of v5, /device:TPU:1, one launch (start us, length us, event | category | flops | bytes accessed | tf_op | source)
XLA Modules:
  0.0 68.6 jit_solution(1655827191036174790)
XLA Ops:
  0.6 3.3 %collective-permute-start.1 = (bf16[256,1024]{1,0:T(8,128)(2,1)}, bf16[256,1024]{1,0:T(8,128)(2,1)S(1)}, u32[]{:S(2)}, u32[]{:S(2)}) collective-permute-start(bf16[256,1024]{1,0:T(8,128)(2,1)} %param.5), channel_id=1, source_target_pairs={{0,8},{8,0},{1,9},{9,1},{2,10},{10,2},{3,11},{11,3},{4,12},{12,4},... | collective-permute-start | bytes 1572872 | tf_op jit(solution)/shard_map/ppermute | solution.py:350
  4.0 0.1 collective-permute-start.2
  4.1 0.0 copy-start.1
  4.1 0.0 copy-start.2
  4.1 0.0 copy-start.3
  4.1 3.9 %extract.1.sent = f32[16,8,128]{2,1,0:T(8,128)} custom-call(f32[256,1024]{1,0:T(8,128)} %bitcast.4, bf16[256,1024]{1,0:T(8,128)(2,1)} %bitcast.6, s32[4,16,32]{2,1,0:T(8,128)} %bitcast.8, bf16[4,256,256]{2,1,0:T(8,128)(2,1)} %constant.2.clone.table.basis), custom_call_target="tpu_custom_call" | custom-call | flops 1000000000 | bytes 2097152 | tf_op jit(solution)/shard_map/extract/pallas_call | solution.py:112
  8.0 0.0 copy-start
  8.0 18.3 %all_to_all.5.refs_0_ = f32[16,8,128]{2,1,0:T(8,128)S(1)} all-to-all(f32[16,8,128]{2,1,0:T(8,128)} %extract.1.sent), channel_id=1, replica_groups=mesh['zh'=4,'y'=4,'c'=2,'x'=4,'zl'=2] {'zh','y'}, dimensions={0} | all-to-all | bytes 131072 | tf_op jit(solution)/shard_map/all_to_all | solution.py:369
  26.3 1.9 %collective-permute-start = (f32[16,8,128]{2,1,0:T(8,128)S(1)}, f32[16,8,128]{2,1,0:T(8,128)S(1)}, u32[]{:S(2)}, u32[]{:S(2)}) collective-permute-start(f32[16,8,128]{2,1,0:T(8,128)S(1)} %all_to_all.5.refs_0_), channel_id=1, source_target_pairs={{0,8},{8,0},{1,9},{9,1},{2,10},{10,2},{3,11},{11,3},{4,12},{12,4},... | collective-permute-start | bytes 196616 | tf_op jit(solution)/shard_map/ppermute | solution.py:350
  28.1 0.9 %collective-permute-done.refs_1_ = f32[16,8,128]{2,1,0:T(8,128)S(1)} collective-permute-done((f32[16,8,128]{2,1,0:T(8,128)S(1)}, f32[16,8,128]{2,1,0:T(8,128)S(1)}, u32[]{:S(2)}, u32[]{:S(2)}) %collective-permute-start) | collective-permute-done | bytes 65568 | tf_op jit(solution)/shard_map/ppermute | solution.py:350
  29.0 0.0 collective-permute-done.1.refs_2_
  29.0 0.0 collective-permute-done.2.refs_3_
  29.0 2.3 %decode.1 = (bf16[1,256,128]{2,1,0:T(8,128)(2,1)S(1)}, bf16[1,256,128]{2,1,0:T(8,128)(2,1)S(1)}) custom-call(f32[16,8,128]{2,1,0:T(8,128)S(1)} %all_to_all.5.refs_0_, f32[16,8,128]{2,1,0:T(8,128)S(1)} %collective-permute-done.refs_1_, bf16[256,1024]{1,0:T(8,128)(2,1)S(1)} %collective-permute-done.1.refs_2_, ...), custom_call_target="tpu_custom_call" | custom-call | flops 1000000000 | bytes 1048576 | tf_op jit(solution)/shard_map/decode/pallas_call | solution.py:195
  31.3 0.8 %collective-permute-start.3 = (bf16[1,256,128]{2,1,0:T(8,128)(2,1)S(1)}, bf16[1,256,128]{2,1,0:T(8,128)(2,1)S(1)}, u32[]{:S(2)}, u32[]{:S(2)}) collective-permute-start(bf16[1,256,128]{2,1,0:T(8,128)(2,1)S(1)} %get-tuple-element.11.a), channel_id=1, source_target_pairs={{0,1},{1,0},{2,3},{3,2},{4,5},{5,4},{6,7},{7,6},{8,9},{9,8},{10,11... | collective-permute-start | bytes 196616 | tf_op jit(solution)/shard_map/ppermute | solution.py:350
  32.1 0.6 collective-permute-start.4
  32.7 1.8 %collective-permute-done.3.b = bf16[1,256,128]{2,1,0:T(8,128)(2,1)S(1)} collective-permute-done((bf16[1,256,128]{2,1,0:T(8,128)(2,1)S(1)}, bf16[1,256,128]{2,1,0:T(8,128)(2,1)S(1)}, u32[]{:S(2)}, u32[]{:S(2)}) %collective-permute-start.3) | collective-permute-done | bytes 65568 | tf_op jit(solution)/shard_map/ppermute | solution.py:350
  34.5 0.0 collective-permute-done.4.d
  34.6 0.4 collective-permute-start.5
  34.9 1.2 %collective-permute-start.6 = (bf16[4,256,128]{2,1,0:T(8,128)(2,1)S(1)}, bf16[4,256,128]{2,1,0:T(8,128)(2,1)S(1)}, u32[]{:S(2)}, u32[]{:S(2)}) collective-permute-start(bf16[4,256,128]{2,1,0:T(8,128)(2,1)S(1)} %join_near.1.a.refs_0_), channel_id=1, source_target_pairs={{0,6},{2,4},{4,2},{6,0},{8,56},{10,58},{12,60},{14,62},{16,22},{18... | collective-permute-start | bytes 786440 | tf_op jit(solution)/shard_map/ppermute | solution.py:359
  36.1 1.8 %collective-permute-start.7 = (bf16[4,256,128]{2,1,0:T(8,128)(2,1)S(1)}, bf16[4,256,128]{2,1,0:T(8,128)(2,1)S(1)}, u32[]{:S(2)}, u32[]{:S(2)}) collective-permute-start(bf16[4,256,128]{2,1,0:T(8,128)(2,1)S(1)} %join_near.1.a.refs_0_), channel_id=1, source_target_pairs={{0,4},{2,6},{4,0},{6,2},{8,40},{10,42},{12,44},{14,46},{16,20},{18... | collective-permute-start | bytes 786440 | tf_op jit(solution)/shard_map/ppermute | solution.py:359
  37.9 2.3 %collective-permute-done.5.b.refs_1_ = bf16[4,256,128]{2,1,0:T(8,128)(2,1)S(1)} collective-permute-done((bf16[4,256,128]{2,1,0:T(8,128)(2,1)S(1)}, bf16[4,256,128]{2,1,0:T(8,128)(2,1)S(1)}, u32[]{:S(2)}, u32[]{:S(2)}) %collective-permute-start.5) | collective-permute-done | bytes 262176 | tf_op jit(solution)/shard_map/ppermute | solution.py:359
  40.2 4.3 %collective-permute-done.6.c.refs_2_ = bf16[4,256,128]{2,1,0:T(8,128)(2,1)S(1)} collective-permute-done((bf16[4,256,128]{2,1,0:T(8,128)(2,1)S(1)}, bf16[4,256,128]{2,1,0:T(8,128)(2,1)S(1)}, u32[]{:S(2)}, u32[]{:S(2)}) %collective-permute-start.6) | collective-permute-done | bytes 262176 | tf_op jit(solution)/shard_map/ppermute | solution.py:359
  44.4 0.0 collective-permute-done.7.d.refs_3_
  44.5 1.1 %collective-permute-start.10 = (bf16[8,256,128]{2,1,0:T(8,128)(2,1)S(1)}, bf16[8,256,128]{2,1,0:T(8,128)(2,1)S(1)}, u32[]{:S(2)}, u32[]{:S(2)}) collective-permute-start(bf16[8,256,128]{2,1,0:T(8,128)(2,1)S(1)} %join_far.1.far.refs_5_), channel_id=1, source_target_pairs={{0,16},{2,18},{4,20},{6,22},{8,10},{10,8},{12,14},{14,12},{16,0},{... | collective-permute-start | bytes 1572872 | tf_op jit(solution)/shard_map/ppermute | solution.py:359
  45.6 1.8 %collective-permute-start.12 = (bf16[8,256,128]{2,1,0:T(8,128)(2,1)S(1)}, bf16[8,256,128]{2,1,0:T(8,128)(2,1)S(1)}, u32[]{:S(2)}, u32[]{:S(2)}) collective-permute-start(bf16[8,256,128]{2,1,0:T(8,128)(2,1)S(1)} %join_far.1.far.refs_5_), channel_id=1, source_target_pairs={{0,48},{2,50},{4,52},{6,54},{8,14},{10,12},{12,10},{14,8},{16,32},... | collective-permute-start | bytes 1572872 | tf_op jit(solution)/shard_map/ppermute | solution.py:359
  47.4 0.8 %collective-permute-start.14 = (bf16[8,256,128]{2,1,0:T(8,128)(2,1)S(1)}, bf16[8,256,128]{2,1,0:T(8,128)(2,1)S(1)}, u32[]{:S(2)}, u32[]{:S(2)}) collective-permute-start(bf16[8,256,128]{2,1,0:T(8,128)(2,1)S(1)} %join_far.1.far.refs_5_), channel_id=1, source_target_pairs={{0,32},{2,34},{4,36},{6,38},{8,12},{10,14},{12,8},{14,10},{16,48},... | collective-permute-start | bytes 1572872 | tf_op jit(solution)/shard_map/ppermute | solution.py:359
  48.2 4.0 %collective-permute-start.9 = (bf16[8,256,128]{2,1,0:T(8,128)(2,1)S(1)}, bf16[8,256,128]{2,1,0:T(8,128)(2,1)S(1)}, u32[]{:S(2)}, u32[]{:S(2)}) collective-permute-start(bf16[8,256,128]{2,1,0:T(8,128)(2,1)S(1)} %join_far.1.far.refs_5_), channel_id=1, source_target_pairs={{0,8},{8,0},{1,9},{9,1},{2,10},{10,2},{3,11},{11,3},{4,12},{12,4},... | collective-permute-start | bytes 1572872 | tf_op jit(solution)/shard_map/ppermute | solution.py:350
  52.2 0.0 copy-done.1
  52.2 0.0 copy-done.2
  52.2 0.0 copy-done.3
  52.2 0.0 copy-done
  52.3 3.2 %kept.1 = (f32[256,1024]{1,0:T(8,128)}, f32[8,128]{1,0:T(8,128)S(1)}) custom-call(f32[256,1024]{1,0:T(8,128)S(1)} %bitcast.5, bf16[256,1024]{1,0:T(8,128)(2,1)S(1)} %bitcast.7, f32[16,8,128]{2,1,0:T(8,128)S(1)} %copy-done, bf16[4,256,256]{2,1,0:T(8,128)(2,1)S(1)} %copy-done.3, bf16[8,256,128]{2,1,0:T(8,128)(2,1)S(1)} %join_far.1.far.refs_5_), custom_call_target="tpu_custom_call" | custom-call | flops 2000000000 | bytes 3145728 | tf_op jit(solution)/shard_map/kept/pallas_call | solution.py:154
  55.5 0.9 %lay.1 = (bf16[256,1024]{1,0:T(8,128)(2,1)S(1)}, bf16[256,8192]{1,0:T(8,128)(2,1)}) custom-call(bf16[4,256,128]{2,1,0:T(8,128)(2,1)S(1)} %join_near.1.a.refs_0_, bf16[4,256,128]{2,1,0:T(8,128)(2,1)S(1)} %collective-permute-done.5.b.refs_1_, bf16[4,256,128]{2,1,0:T(8,128)(2,1)S(1)} %collective-permute-done.6.c.refs_2_, ...), custom_call_target="tpu_custom_call" | custom-call | tf_op jit(solution)/shard_map/lay/pallas_call | solution.py:286
  56.4 0.1 collective-permute-start.8
  56.5 0.0 collective-permute-done.10.refs_1_
  56.5 0.8 %collective-permute-start.11 = (bf16[8,256,128]{2,1,0:T(8,128)(2,1)S(1)}, bf16[8,256,128]{2,1,0:T(8,128)(2,1)S(1)}, u32[]{:S(2)}, u32[]{:S(2)}) collective-permute-start(bf16[8,256,128]{2,1,0:T(8,128)(2,1)S(1)} %collective-permute-done.10.refs_1_), channel_id=1, source_target_pairs={{0,8},{8,0},{1,9},{9,1},{2,10},{10,2},{3,11},{11,3},{4,12},{12,4},... | collective-permute-start | bytes 1572872 | tf_op jit(solution)/shard_map/ppermute | solution.py:350
  57.3 1.9 %collective-permute-done.12.refs_0_ = bf16[8,256,128]{2,1,0:T(8,128)(2,1)S(1)} collective-permute-done((bf16[8,256,128]{2,1,0:T(8,128)(2,1)S(1)}, bf16[8,256,128]{2,1,0:T(8,128)(2,1)S(1)}, u32[]{:S(2)}, u32[]{:S(2)}) %collective-permute-start.12) | collective-permute-done | bytes 524320 | tf_op jit(solution)/shard_map/ppermute | solution.py:359
  59.2 5.5 %collective-permute-start.13 = (bf16[8,256,128]{2,1,0:T(8,128)(2,1)S(1)}, bf16[8,256,128]{2,1,0:T(8,128)(2,1)S(1)}, u32[]{:S(2)}, u32[]{:S(2)}) collective-permute-start(bf16[8,256,128]{2,1,0:T(8,128)(2,1)S(1)} %collective-permute-done.12.refs_0_), channel_id=1, source_target_pairs={{0,8},{8,0},{1,9},{9,1},{2,10},{10,2},{3,11},{11,3},{4,12},{12,4},... | collective-permute-start | bytes 1572872 | tf_op jit(solution)/shard_map/ppermute | solution.py:350
  64.7 0.0 collective-permute-done.14.refs_2_
  64.7 0.0 collective-permute-start.15
  64.7 0.0 collective-permute-done.8.theirs
  64.7 0.0 collective-permute-done.9.refs_0_
  64.7 0.0 collective-permute-done.11.refs_2_
  64.7 1.6 %choose.1 = (bf16[256,1024]{1,0:T(8,128)(2,1)}, bf16[256,8192]{1,0:T(8,128)(2,1)}) custom-call(bf16[256,1024]{1,0:T(8,128)(2,1)S(1)} %get-tuple-element.15.mine, bf16[256,1024]{1,0:T(8,128)(2,1)S(1)} %collective-permute-done.8.theirs, bf16[8,256,128]{2,1,0:T(8,128)(2,1)S(1)} %collective-permute-done.9.refs_0_, ...), custom_call_target="tpu_custom_call", output_to_operand_aliasing={{1}: (5, {})} | custom-call | tf_op jit(solution)/shard_map/choose/pallas_call | solution.py:315
  66.3 0.0 collective-permute-done.13.refs_1_
  66.3 0.7 collective-permute-done.15.refs_3_
  67.0 1.6 %finish.1 = bf16[256,8192]{1,0:T(8,128)(2,1)} custom-call(bf16[8,256,128]{2,1,0:T(8,128)(2,1)S(1)} %collective-permute-done.12.refs_0_, bf16[8,256,128]{2,1,0:T(8,128)(2,1)S(1)} %collective-permute-done.13.refs_1_, bf16[8,256,128]{2,1,0:T(8,128)(2,1)S(1)} %collective-permute-done.14.refs_2_, ...), custom_call_target="tpu_custom_call", output_to_operand_aliasing={{}: (4, {})} | custom-call | tf_op jit(solution)/shard_map/finish/pallas_call | solution.py:337
  (2 shorter events, 0.1 us)
Async XLA Ops:
  0.6 28.4 %collective-permute-start.1 = (bf16[256,1024]{1,0:T(8,128)(2,1)}, bf16[256,1024]{1,0:T(8,128)(2,1)S(1)}, u32[]{:S(2)}, u32[]{:S(2)}) collective-permute-start(bf16[256,1024]{1,0:T(8,128)(2,1)} %param.5), channel_id=1, source_target_pairs={{0,8},{8,0},{1,9},{9,1},{2,10},{10,2},{3,11},{11,3},{4,12},{12,4},... | collective-permute-start | bytes 1572872 | tf_op jit(solution)/shard_map/ppermute | solution.py:350
  4.0 25.1 %collective-permute-start.2 = (bf16[4,256,256]{2,1,0:T(8,128)(2,1)}, bf16[4,256,256]{2,1,0:T(8,128)(2,1)S(1)}, u32[]{:S(2)}, u32[]{:S(2)}) collective-permute-start(bf16[4,256,256]{2,1,0:T(8,128)(2,1)} %constant.2.clone.table.basis), channel_id=1, source_target_pairs={{0,8},{8,0},{1,9},{9,1},{2,10},{10,2},{3,11},{11,3},{4,12},{12,4},... | collective-permute-start | bytes 1572872 | tf_op jit(solution)/shard_map/ppermute | solution.py:350
  4.1 48.2 %copy-start.1 = (f32[1,256,1024]{2,1,0:T(8,128)S(1)}, f32[1,256,1024]{2,1,0:T(8,128)}, u32[]{:S(2)}) copy-start(f32[1,256,1024]{2,1,0:T(8,128)} %param.6) | copy-start | bytes 3145732
  4.1 48.2 %copy-start.2 = (bf16[1,256,1024]{2,1,0:T(8,128)(2,1)S(1)}, bf16[1,256,1024]{2,1,0:T(8,128)(2,1)}, u32[]{:S(2)}) copy-start(bf16[1,256,1024]{2,1,0:T(8,128)(2,1)} %param.7) | copy-start | bytes 1572868
  4.1 48.2 %copy-start.3 = (bf16[4,256,256]{2,1,0:T(8,128)(2,1)S(1)}, bf16[4,256,256]{2,1,0:T(8,128)(2,1)}, u32[]{:S(2)}) copy-start(bf16[4,256,256]{2,1,0:T(8,128)(2,1)} %constant.2.clone.table.basis) | copy-start | bytes 1572868
  8.0 44.3 %copy-start = (f32[16,8,128]{2,1,0:T(8,128)S(1)}, f32[16,8,128]{2,1,0:T(8,128)}, u32[]{:S(2)}) copy-start(f32[16,8,128]{2,1,0:T(8,128)} %extract.1.sent) | copy-start | bytes 196612
  26.3 2.8 %collective-permute-start = (f32[16,8,128]{2,1,0:T(8,128)S(1)}, f32[16,8,128]{2,1,0:T(8,128)S(1)}, u32[]{:S(2)}, u32[]{:S(2)}) collective-permute-start(f32[16,8,128]{2,1,0:T(8,128)S(1)} %all_to_all.5.refs_0_), channel_id=1, source_target_pairs={{0,8},{8,0},{1,9},{9,1},{2,10},{10,2},{3,11},{11,3},{4,12},{12,4},... | collective-permute-start | bytes 196616 | tf_op jit(solution)/shard_map/ppermute | solution.py:350
  31.3 3.2 %collective-permute-start.3 = (bf16[1,256,128]{2,1,0:T(8,128)(2,1)S(1)}, bf16[1,256,128]{2,1,0:T(8,128)(2,1)S(1)}, u32[]{:S(2)}, u32[]{:S(2)}) collective-permute-start(bf16[1,256,128]{2,1,0:T(8,128)(2,1)S(1)} %get-tuple-element.11.a), channel_id=1, source_target_pairs={{0,1},{1,0},{2,3},{3,2},{4,5},{5,4},{6,7},{7,6},{8,9},{9,8},{10,11... | collective-permute-start | bytes 196616 | tf_op jit(solution)/shard_map/ppermute | solution.py:350
  32.1 2.4 %collective-permute-start.4 = (bf16[1,256,128]{2,1,0:T(8,128)(2,1)S(1)}, bf16[1,256,128]{2,1,0:T(8,128)(2,1)S(1)}, u32[]{:S(2)}, u32[]{:S(2)}) collective-permute-start(bf16[1,256,128]{2,1,0:T(8,128)(2,1)S(1)} %get-tuple-element.12.c), channel_id=1, source_target_pairs={{0,8},{8,0},{1,9},{9,1},{2,10},{10,2},{3,11},{11,3},{4,12},{12,4},... | collective-permute-start | bytes 196616 | tf_op jit(solution)/shard_map/ppermute | solution.py:350
  34.6 5.6 %collective-permute-start.5 = (bf16[4,256,128]{2,1,0:T(8,128)(2,1)S(1)}, bf16[4,256,128]{2,1,0:T(8,128)(2,1)S(1)}, u32[]{:S(2)}, u32[]{:S(2)}) collective-permute-start(bf16[4,256,128]{2,1,0:T(8,128)(2,1)S(1)} %join_near.1.a.refs_0_), channel_id=1, source_target_pairs={{0,2},{2,0},{4,6},{6,4},{8,24},{10,26},{12,28},{14,30},{16,18},{18... | collective-permute-start | bytes 786440 | tf_op jit(solution)/shard_map/ppermute | solution.py:359
  34.9 9.5 %collective-permute-start.6 = (bf16[4,256,128]{2,1,0:T(8,128)(2,1)S(1)}, bf16[4,256,128]{2,1,0:T(8,128)(2,1)S(1)}, u32[]{:S(2)}, u32[]{:S(2)}) collective-permute-start(bf16[4,256,128]{2,1,0:T(8,128)(2,1)S(1)} %join_near.1.a.refs_0_), channel_id=1, source_target_pairs={{0,6},{2,4},{4,2},{6,0},{8,56},{10,58},{12,60},{14,62},{16,22},{18... | collective-permute-start | bytes 786440 | tf_op jit(solution)/shard_map/ppermute | solution.py:359
  36.1 8.3 %collective-permute-start.7 = (bf16[4,256,128]{2,1,0:T(8,128)(2,1)S(1)}, bf16[4,256,128]{2,1,0:T(8,128)(2,1)S(1)}, u32[]{:S(2)}, u32[]{:S(2)}) collective-permute-start(bf16[4,256,128]{2,1,0:T(8,128)(2,1)S(1)} %join_near.1.a.refs_0_), channel_id=1, source_target_pairs={{0,4},{2,6},{4,0},{6,2},{8,40},{10,42},{12,44},{14,46},{16,20},{18... | collective-permute-start | bytes 786440 | tf_op jit(solution)/shard_map/ppermute | solution.py:359
  44.5 12.0 %collective-permute-start.10 = (bf16[8,256,128]{2,1,0:T(8,128)(2,1)S(1)}, bf16[8,256,128]{2,1,0:T(8,128)(2,1)S(1)}, u32[]{:S(2)}, u32[]{:S(2)}) collective-permute-start(bf16[8,256,128]{2,1,0:T(8,128)(2,1)S(1)} %join_far.1.far.refs_5_), channel_id=1, source_target_pairs={{0,16},{2,18},{4,20},{6,22},{8,10},{10,8},{12,14},{14,12},{16,0},{... | collective-permute-start | bytes 1572872 | tf_op jit(solution)/shard_map/ppermute | solution.py:359
  45.6 13.6 %collective-permute-start.12 = (bf16[8,256,128]{2,1,0:T(8,128)(2,1)S(1)}, bf16[8,256,128]{2,1,0:T(8,128)(2,1)S(1)}, u32[]{:S(2)}, u32[]{:S(2)}) collective-permute-start(bf16[8,256,128]{2,1,0:T(8,128)(2,1)S(1)} %join_far.1.far.refs_5_), channel_id=1, source_target_pairs={{0,48},{2,50},{4,52},{6,54},{8,14},{10,12},{12,10},{14,8},{16,32},... | collective-permute-start | bytes 1572872 | tf_op jit(solution)/shard_map/ppermute | solution.py:359
  47.4 17.3 %collective-permute-start.14 = (bf16[8,256,128]{2,1,0:T(8,128)(2,1)S(1)}, bf16[8,256,128]{2,1,0:T(8,128)(2,1)S(1)}, u32[]{:S(2)}, u32[]{:S(2)}) collective-permute-start(bf16[8,256,128]{2,1,0:T(8,128)(2,1)S(1)} %join_far.1.far.refs_5_), channel_id=1, source_target_pairs={{0,32},{2,34},{4,36},{6,38},{8,12},{10,14},{12,8},{14,10},{16,48},... | collective-permute-start | bytes 1572872 | tf_op jit(solution)/shard_map/ppermute | solution.py:359
  48.2 16.5 %collective-permute-start.9 = (bf16[8,256,128]{2,1,0:T(8,128)(2,1)S(1)}, bf16[8,256,128]{2,1,0:T(8,128)(2,1)S(1)}, u32[]{:S(2)}, u32[]{:S(2)}) collective-permute-start(bf16[8,256,128]{2,1,0:T(8,128)(2,1)S(1)} %join_far.1.far.refs_5_), channel_id=1, source_target_pairs={{0,8},{8,0},{1,9},{9,1},{2,10},{10,2},{3,11},{11,3},{4,12},{12,4},... | collective-permute-start | bytes 1572872 | tf_op jit(solution)/shard_map/ppermute | solution.py:350
  56.4 8.3 %collective-permute-start.8 = (bf16[256,1024]{1,0:T(8,128)(2,1)S(1)}, bf16[256,1024]{1,0:T(8,128)(2,1)S(1)}, u32[]{:S(2)}, u32[]{:S(2)}) collective-permute-start(bf16[256,1024]{1,0:T(8,128)(2,1)S(1)} %get-tuple-element.15.mine), channel_id=1, source_target_pairs={{0,8},{8,0},{1,9},{9,1},{2,10},{10,2},{3,11},{11,3},{4,12},{12,4},... | collective-permute-start | bytes 1572872 | tf_op jit(solution)/shard_map/ppermute | solution.py:350
  56.5 8.2 %collective-permute-start.11 = (bf16[8,256,128]{2,1,0:T(8,128)(2,1)S(1)}, bf16[8,256,128]{2,1,0:T(8,128)(2,1)S(1)}, u32[]{:S(2)}, u32[]{:S(2)}) collective-permute-start(bf16[8,256,128]{2,1,0:T(8,128)(2,1)S(1)} %collective-permute-done.10.refs_1_), channel_id=1, source_target_pairs={{0,8},{8,0},{1,9},{9,1},{2,10},{10,2},{3,11},{11,3},{4,12},{12,4},... | collective-permute-start | bytes 1572872 | tf_op jit(solution)/shard_map/ppermute | solution.py:350
  59.2 7.1 %collective-permute-start.13 = (bf16[8,256,128]{2,1,0:T(8,128)(2,1)S(1)}, bf16[8,256,128]{2,1,0:T(8,128)(2,1)S(1)}, u32[]{:S(2)}, u32[]{:S(2)}) collective-permute-start(bf16[8,256,128]{2,1,0:T(8,128)(2,1)S(1)} %collective-permute-done.12.refs_0_), channel_id=1, source_target_pairs={{0,8},{8,0},{1,9},{9,1},{2,10},{10,2},{3,11},{11,3},{4,12},{12,4},... | collective-permute-start | bytes 1572872 | tf_op jit(solution)/shard_map/ppermute | solution.py:350
  64.7 2.3 %collective-permute-start.15 = (bf16[8,256,128]{2,1,0:T(8,128)(2,1)S(1)}, bf16[8,256,128]{2,1,0:T(8,128)(2,1)S(1)}, u32[]{:S(2)}, u32[]{:S(2)}) collective-permute-start(bf16[8,256,128]{2,1,0:T(8,128)(2,1)S(1)} %collective-permute-done.14.refs_2_), channel_id=1, source_target_pairs={{0,8},{8,0},{1,9},{9,1},{2,10},{10,2},{3,11},{11,3},{4,12},{12,4},... | collective-permute-start | bytes 1572872 | tf_op jit(solution)/shard_map/ppermute | solution.py:350

commit v6 on v5

--- a/solution.py
+++ b/solution.py
@@ -50,7 +50,9 @@
 
 
 def product(dot, left, right):
-    return dot(left[0], right[0]) + dot(left[0], right[1]) + dot(left[1], right[0])
+    lines = left[0].shape[0]
+    both = dot(jnp.concatenate(left, axis=0), right[0])
+    return both[:lines] + both[lines:] + dot(left[0], right[1])
 
 
 def one_hot_rows(place, lines, dtype):
@@ -75,7 +77,7 @@
         copies.append((momentum.at[:, columns], m_in.at[half]))
         copies.append((grad.at[:, columns], g_in.at[half]))
         if half == 0:
-            copies.append((table.at[pl.ds(0, 2)], basis))
+            copies.append((table, basis))
             copies.append((positions, p_in))
     copies = [pltpu.make_async_copy(*pair, sems.at[n]) for n, pair in enumerate(copies)]
     for copy in copies:
@@ -86,11 +88,11 @@
         if half == 0:
             for x in range(4):
                 places[:, 32 * x : 32 * x + 32] = p_in[x]
-        straight = (basis[0], basis[1])
+        straight, turned = (basis[0], basis[1]), (basis[2], basis[3])
         moved = beta_decay * m_in[half] + g_in[half].astype(F32)
         moved = [two_parts(moved[:, 256 * g : 256 * g + 256]) for g in range(2)]
         rows = [two_parts(product(rows_by_rows, straight, value)) for value in moved]
-        coeff = [two_parts(product(rows_by_rows, value, straight)) for value in rows]
+        coeff = [two_parts(product(rows_by_cols, value, turned)) for value in rows]
         for g in range(2):
             lines = []
             for q in range(4):
@@ -118,7 +120,7 @@
             pltpu.VMEM((2, 256, 512), F32),
             pltpu.VMEM((2, 256, 512), BF16),
             pltpu.VMEM((4, 16, 32), jnp.int32),
-            pltpu.VMEM((2, 256, 256), BF16),
+            pltpu.VMEM((4, 256, 256), BF16),
             pltpu.VMEM((16, 128), jnp.int32),
             pltpu.SemaphoreType.DMA((6,)),
         ],
@@ -163,16 +165,12 @@
     )(momentum, grad, sent, table, far)
 
 
-def decode_kernel(*refs):
-    entries, (weight, basis, fresh, smooth_out) = refs[:2], refs[2:]
+def gather_entries(arrived, totals):
     core = lax.axis_index("c")
-    place = pl.multiple_of((lax.axis_index("y") * 2 + core) * 128, 128)
     tiles = []
-    for ref in entries:
-        for source in range(16):
-            tile = ref[source]
-            tiles.append(jnp.where(core == 0, tile[:4], tile[4:]))
-    totals = [jnp.zeros((2 * GROUP, 4 * GROUP), F32)] * 2
+    for source in range(16):
+        tile = arrived[source]
+        tiles.append(jnp.where(core == 0, tile[:4], tile[4:]))
     for pair in range(0, len(tiles), 2):
         for j in range(2):
             lefts, hots = [], []
@@ -181,9 +179,31 @@
                 lefts.append(jnp.concatenate(spread(tile[2 * j : 2 * j + 1], line), axis=0))
                 hots.append(one_hot_rows(row, 4 * GROUP, BF16))
             found = rows_by_rows(jnp.concatenate(lefts, axis=1), jnp.concatenate(hots, axis=1))
-            totals[j] = totals[j] + found
-    blocks = [total[:GROUP] + total[GROUP:] for total in totals]
-    grid = two_parts(jnp.concatenate(blocks, axis=0))
+            totals[j] = found if totals[j] is None else totals[j] + found
+    return [total[:GROUP] + total[GROUP:] for total in totals]
+
+
+def begin_kernel(arrived, out):
+    for j, total in enumerate(gather_entries(arrived, [None, None])):
+        out[GROUP * j : GROUP * (j + 1)] = total
+
+
+def begin(arrived):
+    return pl.pallas_call(
+        begin_kernel,
+        in_specs=[VMEM],
+        out_specs=VMEM,
+        out_shape=jax.ShapeDtypeStruct((2 * GROUP, 4 * GROUP), F32),
+        cost_estimate=pl.CostEstimate(flops=10**9, bytes_accessed=2**20, transcendentals=0),
+        compiler_params=limit(8),
+        name="begin",
+    )(arrived)
+
+
+def decode_kernel(begun, arrived, weight, basis, fresh, smooth_out):
+    place = pl.multiple_of((lax.axis_index("y") * 2 + lax.axis_index("c")) * 128, 128)
+    blocks = gather_entries(arrived, [None, None])
+    grid = two_parts(begun[...] + jnp.concatenate(blocks, axis=0))
     half = product(rows_by_rows, (basis[2], basis[3]), grid)
     dense = product(rows_by_cols, two_parts(half), (basis[0, :128, :128], basis[1, :128, :128]))
     smooth = jnp.tanh(dense)
@@ -191,16 +211,16 @@
     fresh[0] = (weight[:, pl.ds(place, 128)].astype(F32) - step_rate * smooth).astype(BF16)
 
 
-def decode(entries, weight, table):
+def decode(begun, arrived, weight, table):
     return pl.pallas_call(
         decode_kernel,
         in_specs=[VMEM] * 4,
         out_specs=[VMEM] * 2,
         out_shape=[jax.ShapeDtypeStruct((1, 256, 128), BF16)] * 2,
         cost_estimate=pl.CostEstimate(flops=10**9, bytes_accessed=2**20, transcendentals=32768),
-        compiler_params=limit(12),
+        compiler_params=limit(8),
         name="decode",
-    )(*entries, weight, table)
+    )(begun, arrived, weight, table)
 
 
 def near_kernel(a, b, c, d, out):
@@ -367,22 +387,23 @@
     table = jnp.asarray(basis_parts())
     sent = extract(momentum[0], grad[0], positions[0], table)
     arrived = lax.all_to_all(sent, ("zh", "y"), 0, 0, tiled=True)
-    fresh, smooth = decode([arrived, other_core(arrived)], other_core(weight), other_core(table))
+    fresh, smooth = decode(begin(arrived), other_core(arrived), other_core(weight), other_core(table))
     near = join_near([fresh, swapped(fresh, "zl", 2, 1), smooth, other_core(smooth)])
     firsts = [near] + [crossed(near, 0, k) for k in RING]
     far = join_far(firsts)
     kept_state, token = kept(momentum[0], grad[0], sent, table, far)
     one, two, three = (crossed(far, 1, k) for k in RING)
-    both = lambda array: [array, other_core(array)]
-    laid, new_weight = lay(firsts, token, [(0, (0, 1), (0,))], [far])
+    laid, new_weight = lay(firsts, token, [(0, (0, 1), (0,)), (1, (0, 1), (0,))], [far, one])
     direction, new_weight = choose(
         laid,
         other_core(laid),
-        [(0, (0, 1), (1,)), (1, (0, 1), (0, 1))],
-        [other_core(far)] + both(one),
+        [(0, (0, 1), (1,)), (1, (0, 1), (1,)), (2, (0, 1), (0,)), (3, (0, 1), (0,))],
+        [other_core(far), other_core(one), two, three],
         new_weight,
     )
-    new_weight = finish([(2, (0, 1), (0, 1)), (3, (0, 1), (0, 1))], both(two) + both(three), new_weight)
+    new_weight = finish(
+        [(2, (0, 1), (1,)), (3, (0, 1), (1,))], [other_core(two), other_core(three)], new_weight
+    )
     return (kept_state[None], direction, new_weight)
 
 

time: 68.7 us -> 67.3 us (0.980)
  waiting for transfers between devices: 11.8 us -> 9.46 us
  starting transfers between devices: 24.2 us -> 25.2 us
    ppermute x6, waiting for transfers between devices: 8.42 us -> 7.17 us  [crossed(): return lax.ppermute(array, ('y', 'c', 'x'), perm)]
    ppermute x10, waiting for transfers between devices: 3.36 us -> 2.29 us  [swapped(): return lax.ppermute(array, axis, [(i, i ^ k) for i in range(size)])]
    ppermute x10, starting transfers between devices: 17.2 us -> 18.1 us  [swapped(): return lax.ppermute(array, axis, [(i, i ^ k) for i in range(size)])]
    pallas_call x0 -> x1, Pallas kernels: none -> 0.94 us  [begin(): pl.pallas_call(begin_kernel, in_specs=[VMEM], out_specs=VMEM, out_shape=j...]
    pallas_call x1, Pallas kernels: 2.3 us -> 1.45 us  [decode(): pl.pallas_call(decode_kernel, in_specs=[VMEM] * 4, out_specs=[VMEM] * 2,...]
  transfers between devices with their start and end apart: 16 -> 16, of which waited for: 6 -> 5; matrix products, arithmetic and copies ran while one was open for 0% -> 0% of each run, Pallas kernels for 14% -> 16%
where the time goes in v6:
time: 67.3 us; the launch traced here: 67.1 us
  starting transfers between devices  25.2 us (37%)
  blocking collectives  18.1 us (27%)
  Pallas kernels  13.5 us (20%)
  waiting for transfers between devices  9.46 us (14%)
  between operations  0.75 us (1%)
    ppermute x10, starting transfers between devices, swapped(): return lax.ppermute(array, axis, [(i, i ^ k) for i in range(size)])  18.1 us
    all_to_all x1, blocking collectives, per_device(): arrived = lax.all_to_all(sent, ('zh', 'y'), 0, 0, tiled=True)  18.1 us
    ppermute x6, waiting for transfers between devices, crossed(): return lax.ppermute(array, ('y', 'c', 'x'), perm)  7.17 us
    ppermute x6, starting transfers between devices, crossed(): return lax.ppermute(array, ('y', 'c', 'x'), perm)  7.09 us
    pallas_call x1, Pallas kernels, extract(): pl.pallas_call(extract_kernel, in_specs=[HBM] * 4, out_specs=VMEM, out_sh...  3.82 us
    pallas_call x1, Pallas kernels, kept(): pl.pallas_call(kept_kernel, grid=(2,), in_specs=[block, block, pl.BlockSp...  3.2 us
    ppermute x10, waiting for transfers between devices, swapped(): return lax.ppermute(array, axis, [(i, i ^ k) for i in range(size)])  2.29 us
    pallas_call x1, Pallas kernels, choose(): pl.pallas_call(functools.partial(choose_kernel, groups), in_specs=[ANY] *...  1.84 us
  transfers between devices with their start and end apart: 16, of which 5 were waited for; matrix products, arithmetic and copies ran while one was open for 0% of the time, Pallas kernels for 16%

profile of v6, /device:TPU:1, one launch (start us, length us, event | category | flops | bytes accessed | tf_op | source)
XLA Modules:
  0.0 67.1 jit_solution(13074446316901341716)
XLA Ops:
  0.6 3.3 %collective-permute-start.1 = (bf16[256,1024]{1,0:T(8,128)(2,1)}, bf16[256,1024]{1,0:T(8,128)(2,1)S(1)}, u32[]{:S(2)}, u32[]{:S(2)}) collective-permute-start(bf16[256,1024]{1,0:T(8,128)(2,1)} %param.5), channel_id=1, source_target_pairs={{0,8},{8,0},{1,9},{9,1},{2,10},{10,2},{3,11},{11,3},{4,12},{12,4},... | collective-permute-start | bytes 1572872 | tf_op jit(solution)/shard_map/ppermute | solution.py:370
  4.0 0.1 collective-permute-start.2
  4.1 3.8 %extract.1.sent = f32[16,8,128]{2,1,0:T(8,128)} custom-call(f32[256,1024]{1,0:T(8,128)} %bitcast.4, bf16[256,1024]{1,0:T(8,128)(2,1)} %bitcast.6, s32[4,16,32]{2,1,0:T(8,128)} %bitcast.8, bf16[4,256,256]{2,1,0:T(8,128)(2,1)} %constant.2.clone.table.basis), custom_call_target="tpu_custom_call" | custom-call | flops 1000000000 | bytes 2097152 | tf_op jit(solution)/shard_map/extract/pallas_call | solution.py:114
  7.9 18.1 %all_to_all.5.arrived = f32[16,8,128]{2,1,0:T(8,128)S(1)} all-to-all(f32[16,8,128]{2,1,0:T(8,128)} %extract.1.sent), channel_id=1, replica_groups=mesh['zh'=4,'y'=4,'c'=2,'x'=4,'zl'=2] {'zh','y'}, dimensions={0} | all-to-all | bytes 131072 | tf_op jit(solution)/shard_map/all_to_all | solution.py:389
  26.0 0.0 copy-start
  26.0 0.0 copy-start.1
  26.0 0.0 copy-start.2
  26.0 0.0 copy-start.3
  26.0 1.9 %collective-permute-start = (f32[16,8,128]{2,1,0:T(8,128)S(1)}, f32[16,8,128]{2,1,0:T(8,128)S(1)}, u32[]{:S(2)}, u32[]{:S(2)}) collective-permute-start(f32[16,8,128]{2,1,0:T(8,128)S(1)} %all_to_all.5.arrived), channel_id=1, source_target_pairs={{0,8},{8,0},{1,9},{9,1},{2,10},{10,2},{3,11},{11,3},{4,12},{12,4},... | collective-permute-start | bytes 196616 | tf_op jit(solution)/shard_map/ppermute | solution.py:370
  28.0 0.9 %begin.1.begun = f32[128,256]{1,0:T(8,128)S(1)} custom-call(f32[16,8,128]{2,1,0:T(8,128)S(1)} %all_to_all.5.arrived), custom_call_target="tpu_custom_call" | custom-call | flops 1000000000 | bytes 1048576 | tf_op jit(solution)/shard_map/begin/pallas_call | solution.py:192
  28.9 0.0 collective-permute-done.arrived
  28.9 0.0 collective-permute-done.1.weight
  28.9 0.0 collective-permute-done.2.basis
  28.9 1.4 %decode.1 = (bf16[1,256,128]{2,1,0:T(8,128)(2,1)S(1)}, bf16[1,256,128]{2,1,0:T(8,128)(2,1)S(1)}) custom-call(f32[128,256]{1,0:T(8,128)S(1)} %begin.1.begun, f32[16,8,128]{2,1,0:T(8,128)S(1)} %collective-permute-done.arrived, bf16[256,1024]{1,0:T(8,128)(2,1)S(1)} %collective-permute-done.1.weight, bf16[4,256,256]{2,1,0:T(8,128)(2,1)S(1)} %collective-permute-done.2.basis), custom_call_target="tpu_custom_call" | custom-call | flops 1000000000 | bytes 1048576 | tf_op jit(solution)/shard_map/decode/pallas_call | solution.py:215
  30.4 0.8 %collective-permute-start.3 = (bf16[1,256,128]{2,1,0:T(8,128)(2,1)S(1)}, bf16[1,256,128]{2,1,0:T(8,128)(2,1)S(1)}, u32[]{:S(2)}, u32[]{:S(2)}) collective-permute-start(bf16[1,256,128]{2,1,0:T(8,128)(2,1)S(1)} %get-tuple-element.11.a), channel_id=1, source_target_pairs={{0,1},{1,0},{2,3},{3,2},{4,5},{5,4},{6,7},{7,6},{8,9},{9,8},{10,11... | collective-permute-start | bytes 196616 | tf_op jit(solution)/shard_map/ppermute | solution.py:370
  31.2 0.6 collective-permute-start.4
  31.7 1.9 %collective-permute-done.3.b = bf16[1,256,128]{2,1,0:T(8,128)(2,1)S(1)} collective-permute-done((bf16[1,256,128]{2,1,0:T(8,128)(2,1)S(1)}, bf16[1,256,128]{2,1,0:T(8,128)(2,1)S(1)}, u32[]{:S(2)}, u32[]{:S(2)}) %collective-permute-start.3) | collective-permute-done | bytes 65568 | tf_op jit(solution)/shard_map/ppermute | solution.py:370
  33.6 0.0 collective-permute-done.4.d
  33.6 0.4 collective-permute-start.5
  34.0 1.2 %collective-permute-start.6 = (bf16[4,256,128]{2,1,0:T(8,128)(2,1)S(1)}, bf16[4,256,128]{2,1,0:T(8,128)(2,1)S(1)}, u32[]{:S(2)}, u32[]{:S(2)}) collective-permute-start(bf16[4,256,128]{2,1,0:T(8,128)(2,1)S(1)} %join_near.1.a.refs_0_), channel_id=1, source_target_pairs={{0,6},{2,4},{4,2},{6,0},{8,56},{10,58},{12,60},{14,62},{16,22},{18... | collective-permute-start | bytes 786440 | tf_op jit(solution)/shard_map/ppermute | solution.py:379
  35.2 1.8 %collective-permute-start.7 = (bf16[4,256,128]{2,1,0:T(8,128)(2,1)S(1)}, bf16[4,256,128]{2,1,0:T(8,128)(2,1)S(1)}, u32[]{:S(2)}, u32[]{:S(2)}) collective-permute-start(bf16[4,256,128]{2,1,0:T(8,128)(2,1)S(1)} %join_near.1.a.refs_0_), channel_id=1, source_target_pairs={{0,4},{2,6},{4,0},{6,2},{8,40},{10,42},{12,44},{14,46},{16,20},{18... | collective-permute-start | bytes 786440 | tf_op jit(solution)/shard_map/ppermute | solution.py:379
  37.0 2.3 %collective-permute-done.5.b.refs_1_ = bf16[4,256,128]{2,1,0:T(8,128)(2,1)S(1)} collective-permute-done((bf16[4,256,128]{2,1,0:T(8,128)(2,1)S(1)}, bf16[4,256,128]{2,1,0:T(8,128)(2,1)S(1)}, u32[]{:S(2)}, u32[]{:S(2)}) %collective-permute-start.5) | collective-permute-done | bytes 262176 | tf_op jit(solution)/shard_map/ppermute | solution.py:379
  39.2 4.3 %collective-permute-done.6.c.refs_2_ = bf16[4,256,128]{2,1,0:T(8,128)(2,1)S(1)} collective-permute-done((bf16[4,256,128]{2,1,0:T(8,128)(2,1)S(1)}, bf16[4,256,128]{2,1,0:T(8,128)(2,1)S(1)}, u32[]{:S(2)}, u32[]{:S(2)}) %collective-permute-start.6) | collective-permute-done | bytes 262176 | tf_op jit(solution)/shard_map/ppermute | solution.py:379
  43.5 0.0 collective-permute-done.7.d.refs_3_
  43.6 1.1 %collective-permute-start.8 = (bf16[8,256,128]{2,1,0:T(8,128)(2,1)S(1)}, bf16[8,256,128]{2,1,0:T(8,128)(2,1)S(1)}, u32[]{:S(2)}, u32[]{:S(2)}) collective-permute-start(bf16[8,256,128]{2,1,0:T(8,128)(2,1)S(1)} %join_far.1.far.refs_5_), channel_id=1, source_target_pairs={{0,16},{2,18},{4,20},{6,22},{8,10},{10,8},{12,14},{14,12},{16,0},{... | collective-permute-start | bytes 1572872 | tf_op jit(solution)/shard_map/ppermute | solution.py:379
  44.7 1.8 %collective-permute-start.12 = (bf16[8,256,128]{2,1,0:T(8,128)(2,1)S(1)}, bf16[8,256,128]{2,1,0:T(8,128)(2,1)S(1)}, u32[]{:S(2)}, u32[]{:S(2)}) collective-permute-start(bf16[8,256,128]{2,1,0:T(8,128)(2,1)S(1)} %join_far.1.far.refs_5_), channel_id=1, source_target_pairs={{0,48},{2,50},{4,52},{6,54},{8,14},{10,12},{12,10},{14,8},{16,32},... | collective-permute-start | bytes 1572872 | tf_op jit(solution)/shard_map/ppermute | solution.py:379
  46.5 0.8 %collective-permute-start.13 = (bf16[8,256,128]{2,1,0:T(8,128)(2,1)S(1)}, bf16[8,256,128]{2,1,0:T(8,128)(2,1)S(1)}, u32[]{:S(2)}, u32[]{:S(2)}) collective-permute-start(bf16[8,256,128]{2,1,0:T(8,128)(2,1)S(1)} %join_far.1.far.refs_5_), channel_id=1, source_target_pairs={{0,32},{2,34},{4,36},{6,38},{8,12},{10,14},{12,8},{14,10},{16,48},... | collective-permute-start | bytes 1572872 | tf_op jit(solution)/shard_map/ppermute | solution.py:379
  47.3 3.9 %collective-permute-start.10 = (bf16[8,256,128]{2,1,0:T(8,128)(2,1)S(1)}, bf16[8,256,128]{2,1,0:T(8,128)(2,1)S(1)}, u32[]{:S(2)}, u32[]{:S(2)}) collective-permute-start(bf16[8,256,128]{2,1,0:T(8,128)(2,1)S(1)} %join_far.1.far.refs_5_), channel_id=1, source_target_pairs={{0,8},{8,0},{1,9},{9,1},{2,10},{10,2},{3,11},{11,3},{4,12},{12,4},... | collective-permute-start | bytes 1572872 | tf_op jit(solution)/shard_map/ppermute | solution.py:370
  51.2 0.0 copy-done
  51.3 0.0 copy-done.1
  51.3 0.0 copy-done.2
  51.3 0.0 copy-done.3
  51.3 3.2 %kept.1 = (f32[256,1024]{1,0:T(8,128)}, f32[8,128]{1,0:T(8,128)S(1)}) custom-call(f32[256,1024]{1,0:T(8,128)S(1)} %bitcast.5, bf16[256,1024]{1,0:T(8,128)(2,1)S(1)} %bitcast.7, f32[16,8,128]{2,1,0:T(8,128)S(1)} %copy-done, bf16[4,256,256]{2,1,0:T(8,128)(2,1)S(1)} %copy-done.3, bf16[8,256,128]{2,1,0:T(8,128)(2,1)S(1)} %join_far.1.far.refs_5_), custom_call_target="tpu_custom_call" | custom-call | flops 2000000000 | bytes 3145728 | tf_op jit(solution)/shard_map/kept/pallas_call | solution.py:156
  54.5 0.0 collective-permute-done.8.refs_6_
  54.5 1.1 %lay.1 = (bf16[256,1024]{1,0:T(8,128)(2,1)S(1)}, bf16[256,8192]{1,0:T(8,128)(2,1)}) custom-call(bf16[4,256,128]{2,1,0:T(8,128)(2,1)S(1)} %join_near.1.a.refs_0_, bf16[4,256,128]{2,1,0:T(8,128)(2,1)S(1)} %collective-permute-done.5.b.refs_1_, bf16[4,256,128]{2,1,0:T(8,128)(2,1)S(1)} %collective-permute-done.6.c.refs_2_, ...), custom_call_target="tpu_custom_call" | custom-call | tf_op jit(solution)/shard_map/lay/pallas_call | solution.py:306
  55.6 2.0 %collective-permute-start.9 = (bf16[256,1024]{1,0:T(8,128)(2,1)S(1)}, bf16[256,1024]{1,0:T(8,128)(2,1)S(1)}, u32[]{:S(2)}, u32[]{:S(2)}) collective-permute-start(bf16[256,1024]{1,0:T(8,128)(2,1)S(1)} %get-tuple-element.15.mine), channel_id=1, source_target_pairs={{0,8},{8,0},{1,9},{9,1},{2,10},{10,2},{3,11},{11,3},{4,12},{12,4},... | collective-permute-start | bytes 1572872 | tf_op jit(solution)/shard_map/ppermute | solution.py:370
  57.5 0.1 collective-permute-start.11
  57.6 0.6 collective-permute-done.12.refs_2_
  58.3 5.5 %collective-permute-start.14 = (bf16[8,256,128]{2,1,0:T(8,128)(2,1)S(1)}, bf16[8,256,128]{2,1,0:T(8,128)(2,1)S(1)}, u32[]{:S(2)}, u32[]{:S(2)}) collective-permute-start(bf16[8,256,128]{2,1,0:T(8,128)(2,1)S(1)} %collective-permute-done.12.refs_2_), channel_id=1, source_target_pairs={{0,8},{8,0},{1,9},{9,1},{2,10},{10,2},{3,11},{11,3},{4,12},{12,4},... | collective-permute-start | bytes 1572872 | tf_op jit(solution)/shard_map/ppermute | solution.py:370
  63.7 0.0 collective-permute-done.13.refs_3_
  63.7 0.0 collective-permute-start.15
  63.7 0.0 collective-permute-done.10.refs_0_
  63.7 0.0 collective-permute-done.9.theirs
  63.7 0.0 collective-permute-done.11.refs_1_
  63.7 1.8 %choose.1 = (bf16[256,1024]{1,0:T(8,128)(2,1)}, bf16[256,8192]{1,0:T(8,128)(2,1)}) custom-call(bf16[256,1024]{1,0:T(8,128)(2,1)S(1)} %get-tuple-element.15.mine, bf16[256,1024]{1,0:T(8,128)(2,1)S(1)} %collective-permute-done.9.theirs, bf16[8,256,128]{2,1,0:T(8,128)(2,1)S(1)} %collective-permute-done.10.refs_0_, ...), custom_call_target="tpu_custom_call", output_to_operand_aliasing={{1}: (6, {})} | custom-call | tf_op jit(solution)/shard_map/choose/pallas_call | solution.py:335
  65.6 0.0 collective-permute-done.14.refs_0_
  65.6 0.4 collective-permute-done.15.refs_1_
  66.0 1.1 %finish.1 = bf16[256,8192]{1,0:T(8,128)(2,1)} custom-call(bf16[8,256,128]{2,1,0:T(8,128)(2,1)S(1)} %collective-permute-done.14.refs_0_, bf16[8,256,128]{2,1,0:T(8,128)(2,1)S(1)} %collective-permute-done.15.refs_1_, bf16[256,8192]{1,0:T(8,128)(2,1)} %get-tuple-element.18.refs_2_), custom_call_target="tpu_custom_call", output_to_operand_aliasing={{}: (2, {})} | custom-call | tf_op jit(solution)/shard_map/finish/pallas_call | solution.py:357
  (2 shorter events, 0.1 us)
Async XLA Ops:
  0.6 28.3 %collective-permute-start.1 = (bf16[256,1024]{1,0:T(8,128)(2,1)}, bf16[256,1024]{1,0:T(8,128)(2,1)S(1)}, u32[]{:S(2)}, u32[]{:S(2)}) collective-permute-start(bf16[256,1024]{1,0:T(8,128)(2,1)} %param.5), channel_id=1, source_target_pairs={{0,8},{8,0},{1,9},{9,1},{2,10},{10,2},{3,11},{11,3},{4,12},{12,4},... | collective-permute-start | bytes 1572872 | tf_op jit(solution)/shard_map/ppermute | solution.py:370
  4.0 25.0 %collective-permute-start.2 = (bf16[4,256,256]{2,1,0:T(8,128)(2,1)}, bf16[4,256,256]{2,1,0:T(8,128)(2,1)S(1)}, u32[]{:S(2)}, u32[]{:S(2)}) collective-permute-start(bf16[4,256,256]{2,1,0:T(8,128)(2,1)} %constant.2.clone.table.basis), channel_id=1, source_target_pairs={{0,8},{8,0},{1,9},{9,1},{2,10},{10,2},{3,11},{11,3},{4,12},{12,4},... | collective-permute-start | bytes 1572872 | tf_op jit(solution)/shard_map/ppermute | solution.py:370
  26.0 25.2 %copy-start = (f32[16,8,128]{2,1,0:T(8,128)S(1)}, f32[16,8,128]{2,1,0:T(8,128)}, u32[]{:S(2)}) copy-start(f32[16,8,128]{2,1,0:T(8,128)} %extract.1.sent) | copy-start | bytes 196612
  26.0 25.2 %copy-start.1 = (f32[1,256,1024]{2,1,0:T(8,128)S(1)}, f32[1,256,1024]{2,1,0:T(8,128)}, u32[]{:S(2)}) copy-start(f32[1,256,1024]{2,1,0:T(8,128)} %param.6) | copy-start | bytes 3145732
  26.0 25.2 %copy-start.2 = (bf16[1,256,1024]{2,1,0:T(8,128)(2,1)S(1)}, bf16[1,256,1024]{2,1,0:T(8,128)(2,1)}, u32[]{:S(2)}) copy-start(bf16[1,256,1024]{2,1,0:T(8,128)(2,1)} %param.7) | copy-start | bytes 1572868
  26.0 25.2 %copy-start.3 = (bf16[4,256,256]{2,1,0:T(8,128)(2,1)S(1)}, bf16[4,256,256]{2,1,0:T(8,128)(2,1)}, u32[]{:S(2)}) copy-start(bf16[4,256,256]{2,1,0:T(8,128)(2,1)} %constant.2.clone.table.basis) | copy-start | bytes 1572868
  26.0 2.9 %collective-permute-start = (f32[16,8,128]{2,1,0:T(8,128)S(1)}, f32[16,8,128]{2,1,0:T(8,128)S(1)}, u32[]{:S(2)}, u32[]{:S(2)}) collective-permute-start(f32[16,8,128]{2,1,0:T(8,128)S(1)} %all_to_all.5.arrived), channel_id=1, source_target_pairs={{0,8},{8,0},{1,9},{9,1},{2,10},{10,2},{3,11},{11,3},{4,12},{12,4},... | collective-permute-start | bytes 196616 | tf_op jit(solution)/shard_map/ppermute | solution.py:370
  30.4 3.2 %collective-permute-start.3 = (bf16[1,256,128]{2,1,0:T(8,128)(2,1)S(1)}, bf16[1,256,128]{2,1,0:T(8,128)(2,1)S(1)}, u32[]{:S(2)}, u32[]{:S(2)}) collective-permute-start(bf16[1,256,128]{2,1,0:T(8,128)(2,1)S(1)} %get-tuple-element.11.a), channel_id=1, source_target_pairs={{0,1},{1,0},{2,3},{3,2},{4,5},{5,4},{6,7},{7,6},{8,9},{9,8},{10,11... | collective-permute-start | bytes 196616 | tf_op jit(solution)/shard_map/ppermute | solution.py:370
  31.2 2.4 %collective-permute-start.4 = (bf16[1,256,128]{2,1,0:T(8,128)(2,1)S(1)}, bf16[1,256,128]{2,1,0:T(8,128)(2,1)S(1)}, u32[]{:S(2)}, u32[]{:S(2)}) collective-permute-start(bf16[1,256,128]{2,1,0:T(8,128)(2,1)S(1)} %get-tuple-element.12.c), channel_id=1, source_target_pairs={{0,8},{8,0},{1,9},{9,1},{2,10},{10,2},{3,11},{11,3},{4,12},{12,4},... | collective-permute-start | bytes 196616 | tf_op jit(solution)/shard_map/ppermute | solution.py:370
  33.6 5.6 %collective-permute-start.5 = (bf16[4,256,128]{2,1,0:T(8,128)(2,1)S(1)}, bf16[4,256,128]{2,1,0:T(8,128)(2,1)S(1)}, u32[]{:S(2)}, u32[]{:S(2)}) collective-permute-start(bf16[4,256,128]{2,1,0:T(8,128)(2,1)S(1)} %join_near.1.a.refs_0_), channel_id=1, source_target_pairs={{0,2},{2,0},{4,6},{6,4},{8,24},{10,26},{12,28},{14,30},{16,18},{18... | collective-permute-start | bytes 786440 | tf_op jit(solution)/shard_map/ppermute | solution.py:379
  34.0 9.5 %collective-permute-start.6 = (bf16[4,256,128]{2,1,0:T(8,128)(2,1)S(1)}, bf16[4,256,128]{2,1,0:T(8,128)(2,1)S(1)}, u32[]{:S(2)}, u32[]{:S(2)}) collective-permute-start(bf16[4,256,128]{2,1,0:T(8,128)(2,1)S(1)} %join_near.1.a.refs_0_), channel_id=1, source_target_pairs={{0,6},{2,4},{4,2},{6,0},{8,56},{10,58},{12,60},{14,62},{16,22},{18... | collective-permute-start | bytes 786440 | tf_op jit(solution)/shard_map/ppermute | solution.py:379
  35.2 8.3 %collective-permute-start.7 = (bf16[4,256,128]{2,1,0:T(8,128)(2,1)S(1)}, bf16[4,256,128]{2,1,0:T(8,128)(2,1)S(1)}, u32[]{:S(2)}, u32[]{:S(2)}) collective-permute-start(bf16[4,256,128]{2,1,0:T(8,128)(2,1)S(1)} %join_near.1.a.refs_0_), channel_id=1, source_target_pairs={{0,4},{2,6},{4,0},{6,2},{8,40},{10,42},{12,44},{14,46},{16,20},{18... | collective-permute-start | bytes 786440 | tf_op jit(solution)/shard_map/ppermute | solution.py:379
  43.6 10.9 %collective-permute-start.8 = (bf16[8,256,128]{2,1,0:T(8,128)(2,1)S(1)}, bf16[8,256,128]{2,1,0:T(8,128)(2,1)S(1)}, u32[]{:S(2)}, u32[]{:S(2)}) collective-permute-start(bf16[8,256,128]{2,1,0:T(8,128)(2,1)S(1)} %join_far.1.far.refs_5_), channel_id=1, source_target_pairs={{0,16},{2,18},{4,20},{6,22},{8,10},{10,8},{12,14},{14,12},{16,0},{... | collective-permute-start | bytes 1572872 | tf_op jit(solution)/shard_map/ppermute | solution.py:379
  44.7 13.6 %collective-permute-start.12 = (bf16[8,256,128]{2,1,0:T(8,128)(2,1)S(1)}, bf16[8,256,128]{2,1,0:T(8,128)(2,1)S(1)}, u32[]{:S(2)}, u32[]{:S(2)}) collective-permute-start(bf16[8,256,128]{2,1,0:T(8,128)(2,1)S(1)} %join_far.1.far.refs_5_), channel_id=1, source_target_pairs={{0,48},{2,50},{4,52},{6,54},{8,14},{10,12},{12,10},{14,8},{16,32},... | collective-permute-start | bytes 1572872 | tf_op jit(solution)/shard_map/ppermute | solution.py:379
  46.5 17.2 %collective-permute-start.13 = (bf16[8,256,128]{2,1,0:T(8,128)(2,1)S(1)}, bf16[8,256,128]{2,1,0:T(8,128)(2,1)S(1)}, u32[]{:S(2)}, u32[]{:S(2)}) collective-permute-start(bf16[8,256,128]{2,1,0:T(8,128)(2,1)S(1)} %join_far.1.far.refs_5_), channel_id=1, source_target_pairs={{0,32},{2,34},{4,36},{6,38},{8,12},{10,14},{12,8},{14,10},{16,48},... | collective-permute-start | bytes 1572872 | tf_op jit(solution)/shard_map/ppermute | solution.py:379
  47.3 16.4 %collective-permute-start.10 = (bf16[8,256,128]{2,1,0:T(8,128)(2,1)S(1)}, bf16[8,256,128]{2,1,0:T(8,128)(2,1)S(1)}, u32[]{:S(2)}, u32[]{:S(2)}) collective-permute-start(bf16[8,256,128]{2,1,0:T(8,128)(2,1)S(1)} %join_far.1.far.refs_5_), channel_id=1, source_target_pairs={{0,8},{8,0},{1,9},{9,1},{2,10},{10,2},{3,11},{11,3},{4,12},{12,4},... | collective-permute-start | bytes 1572872 | tf_op jit(solution)/shard_map/ppermute | solution.py:370
  55.6 8.1 %collective-permute-start.9 = (bf16[256,1024]{1,0:T(8,128)(2,1)S(1)}, bf16[256,1024]{1,0:T(8,128)(2,1)S(1)}, u32[]{:S(2)}, u32[]{:S(2)}) collective-permute-start(bf16[256,1024]{1,0:T(8,128)(2,1)S(1)} %get-tuple-element.15.mine), channel_id=1, source_target_pairs={{0,8},{8,0},{1,9},{9,1},{2,10},{10,2},{3,11},{11,3},{4,12},{12,4},... | collective-permute-start | bytes 1572872 | tf_op jit(solution)/shard_map/ppermute | solution.py:370
  57.5 6.2 %collective-permute-start.11 = (bf16[8,256,128]{2,1,0:T(8,128)(2,1)S(1)}, bf16[8,256,128]{2,1,0:T(8,128)(2,1)S(1)}, u32[]{:S(2)}, u32[]{:S(2)}) collective-permute-start(bf16[8,256,128]{2,1,0:T(8,128)(2,1)S(1)} %collective-permute-done.8.refs_6_), channel_id=1, source_target_pairs={{0,8},{8,0},{1,9},{9,1},{2,10},{10,2},{3,11},{11,3},{4,12},{12,4},... | collective-permute-start | bytes 1572872 | tf_op jit(solution)/shard_map/ppermute | solution.py:370
  58.3 7.3 %collective-permute-start.14 = (bf16[8,256,128]{2,1,0:T(8,128)(2,1)S(1)}, bf16[8,256,128]{2,1,0:T(8,128)(2,1)S(1)}, u32[]{:S(2)}, u32[]{:S(2)}) collective-permute-start(bf16[8,256,128]{2,1,0:T(8,128)(2,1)S(1)} %collective-permute-done.12.refs_2_), channel_id=1, source_target_pairs={{0,8},{8,0},{1,9},{9,1},{2,10},{10,2},{3,11},{11,3},{4,12},{12,4},... | collective-permute-start | bytes 1572872 | tf_op jit(solution)/shard_map/ppermute | solution.py:370
  63.7 2.3 %collective-permute-start.15 = (bf16[8,256,128]{2,1,0:T(8,128)(2,1)S(1)}, bf16[8,256,128]{2,1,0:T(8,128)(2,1)S(1)}, u32[]{:S(2)}, u32[]{:S(2)}) collective-permute-start(bf16[8,256,128]{2,1,0:T(8,128)(2,1)S(1)} %collective-permute-done.13.refs_3_), channel_id=1, source_target_pairs={{0,8},{8,0},{1,9},{9,1},{2,10},{10,2},{3,11},{11,3},{4,12},{12,4},... | collective-permute-start | bytes 1572872 | tf_op jit(solution)/shard_map/ppermute | solution.py:370

commit v7 on v6

--- a/solution.py
+++ b/solution.py
@@ -223,32 +223,48 @@
     )(begun, arrived, weight, table)
 
 
-def near_kernel(a, b, c, d, out):
-    for k, ref in enumerate((a, b, c, d)):
+def near_kernel(a, b, c, out):
+    for k, ref in enumerate((a, b, c)):
         out[k] = ref[0]
 
 
 def join_near(arrays):
     return pl.pallas_call(
         near_kernel,
-        in_specs=[VMEM] * 4,
+        in_specs=[VMEM] * 3,
+        out_specs=VMEM,
+        out_shape=jax.ShapeDtypeStruct((3, 256, 128), BF16),
+        compiler_params=limit(4),
+        name="join_near",
+    )(*arrays)
+
+
+def four_kernel(near, fresh_z, out):
+    out[:3] = near[...]
+    out[3] = fresh_z[0]
+
+
+def join_four(near, fresh_z):
+    return pl.pallas_call(
+        four_kernel,
+        in_specs=[VMEM] * 2,
         out_specs=VMEM,
         out_shape=jax.ShapeDtypeStruct((4, 256, 128), BF16),
         compiler_params=limit(4),
-        name="join_near",
-    )(*arrays)
-
-
-def far_kernel(a, b, c, d, out):
-    for k, ref in enumerate((a, b, c, d)):
+        name="join_four",
+    )(near, fresh_z)
+
+
+def far_kernel(a, b, c, across, a_z, b_z, c_z, out):
+    for k, ref in enumerate((a, b, c, across, a_z, b_z, c_z)):
         out[k] = ref[0]
-        out[4 + k] = ref[1]
+    out[7] = across[3]
 
 
 def join_far(arrays):
     return pl.pallas_call(
         far_kernel,
-        in_specs=[VMEM] * 4,
+        in_specs=[VMEM] * 7,
         out_specs=VMEM,
         out_shape=jax.ShapeDtypeStruct((8, 256, 128), BF16),
         compiler_params=limit(4),
@@ -297,7 +313,7 @@
     for k in range(4):
         for other in range(2):
             tile = jnp.bitwise_xor(y, (0, *RING)[k]) * 2 + jnp.bitwise_xor(core, other)
-            laid[:, pl.ds(pl.multiple_of(tile * 128, 128), 128)] = firsts[k][2 + other]
+            laid[:, pl.ds(pl.multiple_of(tile * 128, 128), 128)] = firsts[k][1 + other]
     for copy in copies:
         copy.wait()
 
@@ -388,9 +404,13 @@
     sent = extract(momentum[0], grad[0], positions[0], table)
     arrived = lax.all_to_all(sent, ("zh", "y"), 0, 0, tiled=True)
     fresh, smooth = decode(begin(arrived), other_core(arrived), other_core(weight), other_core(table))
-    near = join_near([fresh, swapped(fresh, "zl", 2, 1), smooth, other_core(smooth)])
-    firsts = [near] + [crossed(near, 0, k) for k in RING]
-    far = join_far(firsts)
+    fresh_z = swapped(fresh, "zl", 2, 1)
+    near = join_near([fresh, smooth, other_core(smooth)])
+    beside = [crossed(near, 0, k) for k in RING[:2]]
+    across = crossed(join_four(near, fresh_z), 0, RING[2])
+    firsts = [near, *beside, across]
+    firsts_z = [fresh_z] + [crossed(fresh_z, 0, k) for k in RING[:2]]
+    far = join_far(firsts + firsts_z)
     kept_state, token = kept(momentum[0], grad[0], sent, table, far)
     one, two, three = (crossed(far, 1, k) for k in RING)
     laid, new_weight = lay(firsts, token, [(0, (0, 1), (0,)), (1, (0, 1), (0,))], [far, one])

time: 67.3 us -> 67 us (level)
  starting transfers between devices: 25.2 us -> 24 us
  waiting for transfers between devices: 9.46 us -> 10.2 us
    ppermute x10, starting transfers between devices: 18.1 us -> 15.8 us  [swapped(): return lax.ppermute(array, axis, [(i, i ^ k) for i in range(size)])]
    ppermute x6 -> x8, starting transfers between devices: 7.09 us -> 8.22 us  [crossed(): return lax.ppermute(array, ('y', 'c', 'x'), perm)]
    ppermute x10, waiting for transfers between devices: 2.29 us -> 3.16 us  [swapped(): return lax.ppermute(array, axis, [(i, i ^ k) for i in range(size)])]
    ppermute x6 -> x8, waiting for transfers between devices: 7.17 us -> 7.05 us  [crossed(): return lax.ppermute(array, ('y', 'c', 'x'), perm)]
  transfers between devices with their start and end apart: 16 -> 18, of which waited for: 5 -> 6; matrix products, arithmetic and copies ran while one was open for 0% -> 0% of each run, Pallas kernels for 16% -> 16%
where the time goes in v7:
time: 67 us; the launch traced here: 66.8 us
  starting transfers between devices  24 us (36%)
  blocking collectives  18.1 us (27%)
  Pallas kernels  13.5 us (20%)
  waiting for transfers between devices  10.2 us (15%)
  between operations  0.92 us (1%)
    all_to_all x1, blocking collectives, per_device(): arrived = lax.all_to_all(sent, ('zh', 'y'), 0, 0, tiled=True)  18.1 us
    ppermute x10, starting transfers between devices, swapped(): return lax.ppermute(array, axis, [(i, i ^ k) for i in range(size)])  15.8 us
    ppermute x8, starting transfers between devices, crossed(): return lax.ppermute(array, ('y', 'c', 'x'), perm)  8.22 us
    ppermute x8, waiting for transfers between devices, crossed(): return lax.ppermute(array, ('y', 'c', 'x'), perm)  7.05 us
    pallas_call x1, Pallas kernels, extract(): pl.pallas_call(extract_kernel, in_specs=[HBM] * 4, out_specs=VMEM, out_sh...  3.82 us
    pallas_call x1, Pallas kernels, kept(): pl.pallas_call(kept_kernel, grid=(2,), in_specs=[block, block, pl.BlockSp...  3.2 us
    ppermute x10, waiting for transfers between devices, swapped(): return lax.ppermute(array, axis, [(i, i ^ k) for i in range(size)])  3.16 us
    pallas_call x1, Pallas kernels, choose(): pl.pallas_call(functools.partial(choose_kernel, groups), in_specs=[ANY] *...  1.84 us
  transfers between devices with their start and end apart: 18, of which 6 were waited for; matrix products, arithmetic and copies ran while one was open for 0% of the time, Pallas kernels for 16%

profile of v7, /device:TPU:1, one launch (start us, length us, event | category | flops | bytes accessed | tf_op | source)
XLA Modules:
  0.0 66.8 jit_solution(14738155548420440184)
XLA Ops:
  0.6 3.3 %collective-permute-start.1 = (bf16[256,1024]{1,0:T(8,128)(2,1)}, bf16[256,1024]{1,0:T(8,128)(2,1)S(1)}, u32[]{:S(2)}, u32[]{:S(2)}) collective-permute-start(bf16[256,1024]{1,0:T(8,128)(2,1)} %param.5), channel_id=1, source_target_pairs={{0,8},{8,0},{1,9},{9,1},{2,10},{10,2},{3,11},{11,3},{4,12},{12,4},... | collective-permute-start | bytes 1572872 | tf_op jit(solution)/shard_map/ppermute | solution.py:386
  4.0 0.1 collective-permute-start.2
  4.1 3.8 %extract.1.sent = f32[16,8,128]{2,1,0:T(8,128)} custom-call(f32[256,1024]{1,0:T(8,128)} %bitcast.4, bf16[256,1024]{1,0:T(8,128)(2,1)} %bitcast.6, s32[4,16,32]{2,1,0:T(8,128)} %bitcast.8, bf16[4,256,256]{2,1,0:T(8,128)(2,1)} %constant.2.clone.table.basis), custom_call_target="tpu_custom_call" | custom-call | flops 1000000000 | bytes 2097152 | tf_op jit(solution)/shard_map/extract/pallas_call | solution.py:114
  7.9 18.1 %all_to_all.5.arrived = f32[16,8,128]{2,1,0:T(8,128)S(1)} all-to-all(f32[16,8,128]{2,1,0:T(8,128)} %extract.1.sent), channel_id=1, replica_groups=mesh['zh'=4,'y'=4,'c'=2,'x'=4,'zl'=2] {'zh','y'}, dimensions={0} | all-to-all | bytes 131072 | tf_op jit(solution)/shard_map/all_to_all | solution.py:405
  26.0 0.0 copy-start
  26.0 0.0 copy-start.1
  26.0 0.0 copy-start.2
  26.0 0.0 copy-start.3
  26.0 1.9 %collective-permute-start = (f32[16,8,128]{2,1,0:T(8,128)S(1)}, f32[16,8,128]{2,1,0:T(8,128)S(1)}, u32[]{:S(2)}, u32[]{:S(2)}) collective-permute-start(f32[16,8,128]{2,1,0:T(8,128)S(1)} %all_to_all.5.arrived), channel_id=1, source_target_pairs={{0,8},{8,0},{1,9},{9,1},{2,10},{10,2},{3,11},{11,3},{4,12},{12,4},... | collective-permute-start | bytes 196616 | tf_op jit(solution)/shard_map/ppermute | solution.py:386
  28.0 0.9 %begin.1.begun = f32[128,256]{1,0:T(8,128)S(1)} custom-call(f32[16,8,128]{2,1,0:T(8,128)S(1)} %all_to_all.5.arrived), custom_call_target="tpu_custom_call" | custom-call | flops 1000000000 | bytes 1048576 | tf_op jit(solution)/shard_map/begin/pallas_call | solution.py:192
  28.9 0.0 collective-permute-done.arrived
  28.9 0.0 collective-permute-done.1.weight
  28.9 0.0 collective-permute-done.2.basis
  28.9 1.4 %decode.1 = (bf16[1,256,128]{2,1,0:T(8,128)(2,1)S(1)}, bf16[1,256,128]{2,1,0:T(8,128)(2,1)S(1)}) custom-call(f32[128,256]{1,0:T(8,128)S(1)} %begin.1.begun, f32[16,8,128]{2,1,0:T(8,128)S(1)} %collective-permute-done.arrived, bf16[256,1024]{1,0:T(8,128)(2,1)S(1)} %collective-permute-done.1.weight, bf16[4,256,256]{2,1,0:T(8,128)(2,1)S(1)} %collective-permute-done.2.basis), custom_call_target="tpu_custom_call" | custom-call | flops 1000000000 | bytes 1048576 | tf_op jit(solution)/shard_map/decode/pallas_call | solution.py:215
  30.4 0.4 collective-permute-start.3
  30.8 0.7 %collective-permute-start.6 = (bf16[1,256,128]{2,1,0:T(8,128)(2,1)S(1)}, bf16[1,256,128]{2,1,0:T(8,128)(2,1)S(1)}, u32[]{:S(2)}, u32[]{:S(2)}) collective-permute-start(bf16[1,256,128]{2,1,0:T(8,128)(2,1)S(1)} %get-tuple-element.11.a), channel_id=1, source_target_pairs={{0,1},{1,0},{2,3},{3,2},{4,5},{5,4},{6,7},{7,6},{8,9},{9,8},{10,11... | collective-permute-start | bytes 196616 | tf_op jit(solution)/shard_map/ppermute | solution.py:386
  31.4 0.3 collective-permute-done.3.c
  31.7 2.5 %collective-permute-done.6.fresh_z.a_z = bf16[1,256,128]{2,1,0:T(8,128)(2,1)S(1)} collective-permute-done((bf16[1,256,128]{2,1,0:T(8,128)(2,1)S(1)}, bf16[1,256,128]{2,1,0:T(8,128)(2,1)S(1)}, u32[]{:S(2)}, u32[]{:S(2)}) %collective-permute-start.6) | collective-permute-done | bytes 65568 | tf_op jit(solution)/shard_map/ppermute | solution.py:386
  34.2 0.9 %collective-permute-start.7 = (bf16[4,256,128]{2,1,0:T(8,128)(2,1)S(1)}, bf16[4,256,128]{2,1,0:T(8,128)(2,1)S(1)}, u32[]{:S(2)}, u32[]{:S(2)}) collective-permute-start(bf16[4,256,128]{2,1,0:T(8,128)(2,1)S(1)} %join_four.1), channel_id=1, source_target_pairs={{0,4},{2,6},{4,0},{6,2},{8,40},{10,42},{12,44},{14,46},{16,20},{18... | collective-permute-start | bytes 786440 | tf_op jit(solution)/shard_map/ppermute | solution.py:395
  35.2 0.4 collective-permute-start.4
  35.5 2.1 %collective-permute-start.5 = (bf16[3,256,128]{2,1,0:T(8,128)(2,1)S(1)}, bf16[3,256,128]{2,1,0:T(8,128)(2,1)S(1)}, u32[]{:S(2)}, u32[]{:S(2)}) collective-permute-start(bf16[3,256,128]{2,1,0:T(8,128)(2,1)S(1)} %join_near.1.near.a.refs_0_), channel_id=1, source_target_pairs={{0,6},{2,4},{4,2},{6,0},{8,56},{10,58},{12,60},{14,62},{16,22},{18... | collective-permute-start | bytes 589832 | tf_op jit(solution)/shard_map/ppermute | solution.py:395
  37.6 0.3 collective-permute-start.8
  37.8 0.8 %collective-permute-start.9 = (bf16[1,256,128]{2,1,0:T(8,128)(2,1)S(1)}, bf16[1,256,128]{2,1,0:T(8,128)(2,1)S(1)}, u32[]{:S(2)}, u32[]{:S(2)}) collective-permute-start(bf16[1,256,128]{2,1,0:T(8,128)(2,1)S(1)} %collective-permute-done.6.fresh_z.a_z), channel_id=1, source_target_pairs={{0,6},{2,4},{4,2},{6,0},{8,56},{10,58},{12,60},{14,62},{16,22},{18... | collective-permute-start | bytes 196616 | tf_op jit(solution)/shard_map/ppermute | solution.py:395
  38.7 3.7 %collective-permute-done.8.b_z = bf16[1,256,128]{2,1,0:T(8,128)(2,1)S(1)} collective-permute-done((bf16[1,256,128]{2,1,0:T(8,128)(2,1)S(1)}, bf16[1,256,128]{2,1,0:T(8,128)(2,1)S(1)}, u32[]{:S(2)}, u32[]{:S(2)}) %collective-permute-start.8) | collective-permute-done | bytes 65568 | tf_op jit(solution)/shard_map/ppermute | solution.py:395
  42.4 1.8 %collective-permute-done.9.c_z = bf16[1,256,128]{2,1,0:T(8,128)(2,1)S(1)} collective-permute-done((bf16[1,256,128]{2,1,0:T(8,128)(2,1)S(1)}, bf16[1,256,128]{2,1,0:T(8,128)(2,1)S(1)}, u32[]{:S(2)}, u32[]{:S(2)}) %collective-permute-start.9) | collective-permute-done | bytes 65568 | tf_op jit(solution)/shard_map/ppermute | solution.py:395
  44.2 0.0 collective-permute-done.4.b.refs_1_
  44.2 0.0 collective-permute-done.5.c.refs_2_
  44.2 0.0 collective-permute-done.7.across.refs_3_
  44.2 1.0 %collective-permute-start.10 = (bf16[8,256,128]{2,1,0:T(8,128)(2,1)S(1)}, bf16[8,256,128]{2,1,0:T(8,128)(2,1)S(1)}, u32[]{:S(2)}, u32[]{:S(2)}) collective-permute-start(bf16[8,256,128]{2,1,0:T(8,128)(2,1)S(1)} %join_far.1.far.refs_5_), channel_id=1, source_target_pairs={{0,16},{2,18},{4,20},{6,22},{8,10},{10,8},{12,14},{14,12},{16,0},{... | collective-permute-start | bytes 1572872 | tf_op jit(solution)/shard_map/ppermute | solution.py:395
  45.2 1.8 %collective-permute-start.14 = (bf16[8,256,128]{2,1,0:T(8,128)(2,1)S(1)}, bf16[8,256,128]{2,1,0:T(8,128)(2,1)S(1)}, u32[]{:S(2)}, u32[]{:S(2)}) collective-permute-start(bf16[8,256,128]{2,1,0:T(8,128)(2,1)S(1)} %join_far.1.far.refs_5_), channel_id=1, source_target_pairs={{0,48},{2,50},{4,52},{6,54},{8,14},{10,12},{12,10},{14,8},{16,32},... | collective-permute-start | bytes 1572872 | tf_op jit(solution)/shard_map/ppermute | solution.py:395
  47.0 0.9 %collective-permute-start.15 = (bf16[8,256,128]{2,1,0:T(8,128)(2,1)S(1)}, bf16[8,256,128]{2,1,0:T(8,128)(2,1)S(1)}, u32[]{:S(2)}, u32[]{:S(2)}) collective-permute-start(bf16[8,256,128]{2,1,0:T(8,128)(2,1)S(1)} %join_far.1.far.refs_5_), channel_id=1, source_target_pairs={{0,32},{2,34},{4,36},{6,38},{8,12},{10,14},{12,8},{14,10},{16,48},... | collective-permute-start | bytes 1572872 | tf_op jit(solution)/shard_map/ppermute | solution.py:395
  48.0 2.8 %collective-permute-start.12 = (bf16[8,256,128]{2,1,0:T(8,128)(2,1)S(1)}, bf16[8,256,128]{2,1,0:T(8,128)(2,1)S(1)}, u32[]{:S(2)}, u32[]{:S(2)}) collective-permute-start(bf16[8,256,128]{2,1,0:T(8,128)(2,1)S(1)} %join_far.1.far.refs_5_), channel_id=1, source_target_pairs={{0,8},{8,0},{1,9},{9,1},{2,10},{10,2},{3,11},{11,3},{4,12},{12,4},... | collective-permute-start | bytes 1572872 | tf_op jit(solution)/shard_map/ppermute | solution.py:386
  50.8 0.0 copy-done
  50.8 0.0 copy-done.1
  50.8 0.0 copy-done.2
  50.8 0.0 copy-done.3
  50.8 3.2 %kept.1 = (f32[256,1024]{1,0:T(8,128)}, f32[8,128]{1,0:T(8,128)S(1)}) custom-call(f32[256,1024]{1,0:T(8,128)S(1)} %bitcast.5, bf16[256,1024]{1,0:T(8,128)(2,1)S(1)} %bitcast.7, f32[16,8,128]{2,1,0:T(8,128)S(1)} %copy-done, bf16[4,256,256]{2,1,0:T(8,128)(2,1)S(1)} %copy-done.3, bf16[8,256,128]{2,1,0:T(8,128)(2,1)S(1)} %join_far.1.far.refs_5_), custom_call_target="tpu_custom_call" | custom-call | flops 2000000000 | bytes 3145728 | tf_op jit(solution)/shard_map/kept/pallas_call | solution.py:156
  54.0 0.0 collective-permute-done.10.refs_6_
  54.0 1.1 %lay.1 = (bf16[256,1024]{1,0:T(8,128)(2,1)S(1)}, bf16[256,8192]{1,0:T(8,128)(2,1)}) custom-call(bf16[3,256,128]{2,1,0:T(8,128)(2,1)S(1)} %join_near.1.near.a.refs_0_, bf16[3,256,128]{2,1,0:T(8,128)(2,1)S(1)} %collective-permute-done.4.b.refs_1_, bf16[3,256,128]{2,1,0:T(8,128)(2,1)S(1)} %collective-permute-done.5.c.refs_2_, ...), custom_call_target="tpu_custom_call" | custom-call | tf_op jit(solution)/shard_map/lay/pallas_call | solution.py:322
  55.1 2.0 %collective-permute-start.11 = (bf16[256,1024]{1,0:T(8,128)(2,1)S(1)}, bf16[256,1024]{1,0:T(8,128)(2,1)S(1)}, u32[]{:S(2)}, u32[]{:S(2)}) collective-permute-start(bf16[256,1024]{1,0:T(8,128)(2,1)S(1)} %get-tuple-element.15.mine), channel_id=1, source_target_pairs={{0,8},{8,0},{1,9},{9,1},{2,10},{10,2},{3,11},{11,3},{4,12},{12,4},... | collective-permute-start | bytes 1572872 | tf_op jit(solution)/shard_map/ppermute | solution.py:386
  57.1 0.1 collective-permute-start.13
  57.2 1.6 %collective-permute-done.14.refs_2_ = bf16[8,256,128]{2,1,0:T(8,128)(2,1)S(1)} collective-permute-done((bf16[8,256,128]{2,1,0:T(8,128)(2,1)S(1)}, bf16[8,256,128]{2,1,0:T(8,128)(2,1)S(1)}, u32[]{:S(2)}, u32[]{:S(2)}) %collective-permute-start.14) | collective-permute-done | bytes 524320 | tf_op jit(solution)/shard_map/ppermute | solution.py:395
  58.8 4.5 %collective-permute-start.16 = (bf16[8,256,128]{2,1,0:T(8,128)(2,1)S(1)}, bf16[8,256,128]{2,1,0:T(8,128)(2,1)S(1)}, u32[]{:S(2)}, u32[]{:S(2)}) collective-permute-start(bf16[8,256,128]{2,1,0:T(8,128)(2,1)S(1)} %collective-permute-done.14.refs_2_), channel_id=1, source_target_pairs={{0,8},{8,0},{1,9},{9,1},{2,10},{10,2},{3,11},{11,3},{4,12},{12,4},... | collective-permute-start | bytes 1572872 | tf_op jit(solution)/shard_map/ppermute | solution.py:386
  63.3 0.0 collective-permute-done.15.refs_3_
  63.3 0.0 collective-permute-start.17
  63.3 0.0 collective-permute-done.12.refs_0_
  63.3 0.0 collective-permute-done.11.theirs
  63.3 0.0 collective-permute-done.13.refs_1_
  63.3 1.8 %choose.1 = (bf16[256,1024]{1,0:T(8,128)(2,1)}, bf16[256,8192]{1,0:T(8,128)(2,1)}) custom-call(bf16[256,1024]{1,0:T(8,128)(2,1)S(1)} %get-tuple-element.15.mine, bf16[256,1024]{1,0:T(8,128)(2,1)S(1)} %collective-permute-done.11.theirs, bf16[8,256,128]{2,1,0:T(8,128)(2,1)S(1)} %collective-permute-done.12.refs_0_, ...), custom_call_target="tpu_custom_call", output_to_operand_aliasing={{1}: (6, {})} | custom-call | tf_op jit(solution)/shard_map/choose/pallas_call | solution.py:351
  65.2 0.0 collective-permute-done.16.refs_0_
  65.2 0.4 collective-permute-done.17.refs_1_
  65.6 1.1 %finish.1 = bf16[256,8192]{1,0:T(8,128)(2,1)} custom-call(bf16[8,256,128]{2,1,0:T(8,128)(2,1)S(1)} %collective-permute-done.16.refs_0_, bf16[8,256,128]{2,1,0:T(8,128)(2,1)S(1)} %collective-permute-done.17.refs_1_, bf16[256,8192]{1,0:T(8,128)(2,1)} %get-tuple-element.18.refs_2_), custom_call_target="tpu_custom_call", output_to_operand_aliasing={{}: (2, {})} | custom-call | tf_op jit(solution)/shard_map/finish/pallas_call | solution.py:373
  (3 shorter events, 0.1 us)
Async XLA Ops:
  0.6 28.3 %collective-permute-start.1 = (bf16[256,1024]{1,0:T(8,128)(2,1)}, bf16[256,1024]{1,0:T(8,128)(2,1)S(1)}, u32[]{:S(2)}, u32[]{:S(2)}) collective-permute-start(bf16[256,1024]{1,0:T(8,128)(2,1)} %param.5), channel_id=1, source_target_pairs={{0,8},{8,0},{1,9},{9,1},{2,10},{10,2},{3,11},{11,3},{4,12},{12,4},... | collective-permute-start | bytes 1572872 | tf_op jit(solution)/shard_map/ppermute | solution.py:386
  4.0 25.0 %collective-permute-start.2 = (bf16[4,256,256]{2,1,0:T(8,128)(2,1)}, bf16[4,256,256]{2,1,0:T(8,128)(2,1)S(1)}, u32[]{:S(2)}, u32[]{:S(2)}) collective-permute-start(bf16[4,256,256]{2,1,0:T(8,128)(2,1)} %constant.2.clone.table.basis), channel_id=1, source_target_pairs={{0,8},{8,0},{1,9},{9,1},{2,10},{10,2},{3,11},{11,3},{4,12},{12,4},... | collective-permute-start | bytes 1572872 | tf_op jit(solution)/shard_map/ppermute | solution.py:386
  26.0 24.8 %copy-start = (f32[16,8,128]{2,1,0:T(8,128)S(1)}, f32[16,8,128]{2,1,0:T(8,128)}, u32[]{:S(2)}) copy-start(f32[16,8,128]{2,1,0:T(8,128)} %extract.1.sent) | copy-start | bytes 196612
  26.0 24.8 %copy-start.1 = (f32[1,256,1024]{2,1,0:T(8,128)S(1)}, f32[1,256,1024]{2,1,0:T(8,128)}, u32[]{:S(2)}) copy-start(f32[1,256,1024]{2,1,0:T(8,128)} %param.6) | copy-start | bytes 3145732
  26.0 24.8 %copy-start.2 = (bf16[1,256,1024]{2,1,0:T(8,128)(2,1)S(1)}, bf16[1,256,1024]{2,1,0:T(8,128)(2,1)}, u32[]{:S(2)}) copy-start(bf16[1,256,1024]{2,1,0:T(8,128)(2,1)} %param.7) | copy-start | bytes 1572868
  26.0 24.8 %copy-start.3 = (bf16[4,256,256]{2,1,0:T(8,128)(2,1)S(1)}, bf16[4,256,256]{2,1,0:T(8,128)(2,1)}, u32[]{:S(2)}) copy-start(bf16[4,256,256]{2,1,0:T(8,128)(2,1)} %constant.2.clone.table.basis) | copy-start | bytes 1572868
  26.0 2.9 %collective-permute-start = (f32[16,8,128]{2,1,0:T(8,128)S(1)}, f32[16,8,128]{2,1,0:T(8,128)S(1)}, u32[]{:S(2)}, u32[]{:S(2)}) collective-permute-start(f32[16,8,128]{2,1,0:T(8,128)S(1)} %all_to_all.5.arrived), channel_id=1, source_target_pairs={{0,8},{8,0},{1,9},{9,1},{2,10},{10,2},{3,11},{11,3},{4,12},{12,4},... | collective-permute-start | bytes 196616 | tf_op jit(solution)/shard_map/ppermute | solution.py:386
  30.4 1.3 %collective-permute-start.3 = (bf16[1,256,128]{2,1,0:T(8,128)(2,1)S(1)}, bf16[1,256,128]{2,1,0:T(8,128)(2,1)S(1)}, u32[]{:S(2)}, u32[]{:S(2)}) collective-permute-start(bf16[1,256,128]{2,1,0:T(8,128)(2,1)S(1)} %get-tuple-element.12.b), channel_id=1, source_target_pairs={{0,8},{8,0},{1,9},{9,1},{2,10},{10,2},{3,11},{11,3},{4,12},{12,4},... | collective-permute-start | bytes 196616 | tf_op jit(solution)/shard_map/ppermute | solution.py:386
  30.8 3.5 %collective-permute-start.6 = (bf16[1,256,128]{2,1,0:T(8,128)(2,1)S(1)}, bf16[1,256,128]{2,1,0:T(8,128)(2,1)S(1)}, u32[]{:S(2)}, u32[]{:S(2)}) collective-permute-start(bf16[1,256,128]{2,1,0:T(8,128)(2,1)S(1)} %get-tuple-element.11.a), channel_id=1, source_target_pairs={{0,1},{1,0},{2,3},{3,2},{4,5},{5,4},{6,7},{7,6},{8,9},{9,8},{10,11... | collective-permute-start | bytes 196616 | tf_op jit(solution)/shard_map/ppermute | solution.py:386
  34.2 9.9 %collective-permute-start.7 = (bf16[4,256,128]{2,1,0:T(8,128)(2,1)S(1)}, bf16[4,256,128]{2,1,0:T(8,128)(2,1)S(1)}, u32[]{:S(2)}, u32[]{:S(2)}) collective-permute-start(bf16[4,256,128]{2,1,0:T(8,128)(2,1)S(1)} %join_four.1), channel_id=1, source_target_pairs={{0,4},{2,6},{4,0},{6,2},{8,40},{10,42},{12,44},{14,46},{16,20},{18... | collective-permute-start | bytes 786440 | tf_op jit(solution)/shard_map/ppermute | solution.py:395
  35.2 9.0 %collective-permute-start.4 = (bf16[3,256,128]{2,1,0:T(8,128)(2,1)S(1)}, bf16[3,256,128]{2,1,0:T(8,128)(2,1)S(1)}, u32[]{:S(2)}, u32[]{:S(2)}) collective-permute-start(bf16[3,256,128]{2,1,0:T(8,128)(2,1)S(1)} %join_near.1.near.a.refs_0_), channel_id=1, source_target_pairs={{0,2},{2,0},{4,6},{6,4},{8,24},{10,26},{12,28},{14,30},{16,18},{18... | collective-permute-start | bytes 589832 | tf_op jit(solution)/shard_map/ppermute | solution.py:395
  35.5 8.6 %collective-permute-start.5 = (bf16[3,256,128]{2,1,0:T(8,128)(2,1)S(1)}, bf16[3,256,128]{2,1,0:T(8,128)(2,1)S(1)}, u32[]{:S(2)}, u32[]{:S(2)}) collective-permute-start(bf16[3,256,128]{2,1,0:T(8,128)(2,1)S(1)} %join_near.1.near.a.refs_0_), channel_id=1, source_target_pairs={{0,6},{2,4},{4,2},{6,0},{8,56},{10,58},{12,60},{14,62},{16,22},{18... | collective-permute-start | bytes 589832 | tf_op jit(solution)/shard_map/ppermute | solution.py:395
  37.6 4.8 %collective-permute-start.8 = (bf16[1,256,128]{2,1,0:T(8,128)(2,1)S(1)}, bf16[1,256,128]{2,1,0:T(8,128)(2,1)S(1)}, u32[]{:S(2)}, u32[]{:S(2)}) collective-permute-start(bf16[1,256,128]{2,1,0:T(8,128)(2,1)S(1)} %collective-permute-done.6.fresh_z.a_z), channel_id=1, source_target_pairs={{0,2},{2,0},{4,6},{6,4},{8,24},{10,26},{12,28},{14,30},{16,18},{18... | collective-permute-start | bytes 196616 | tf_op jit(solution)/shard_map/ppermute | solution.py:395
  37.8 6.3 %collective-permute-start.9 = (bf16[1,256,128]{2,1,0:T(8,128)(2,1)S(1)}, bf16[1,256,128]{2,1,0:T(8,128)(2,1)S(1)}, u32[]{:S(2)}, u32[]{:S(2)}) collective-permute-start(bf16[1,256,128]{2,1,0:T(8,128)(2,1)S(1)} %collective-permute-done.6.fresh_z.a_z), channel_id=1, source_target_pairs={{0,6},{2,4},{4,2},{6,0},{8,56},{10,58},{12,60},{14,62},{16,22},{18... | collective-permute-start | bytes 196616 | tf_op jit(solution)/shard_map/ppermute | solution.py:395
  44.2 9.8 %collective-permute-start.10 = (bf16[8,256,128]{2,1,0:T(8,128)(2,1)S(1)}, bf16[8,256,128]{2,1,0:T(8,128)(2,1)S(1)}, u32[]{:S(2)}, u32[]{:S(2)}) collective-permute-start(bf16[8,256,128]{2,1,0:T(8,128)(2,1)S(1)} %join_far.1.far.refs_5_), channel_id=1, source_target_pairs={{0,16},{2,18},{4,20},{6,22},{8,10},{10,8},{12,14},{14,12},{16,0},{... | collective-permute-start | bytes 1572872 | tf_op jit(solution)/shard_map/ppermute | solution.py:395
  45.2 13.6 %collective-permute-start.14 = (bf16[8,256,128]{2,1,0:T(8,128)(2,1)S(1)}, bf16[8,256,128]{2,1,0:T(8,128)(2,1)S(1)}, u32[]{:S(2)}, u32[]{:S(2)}) collective-permute-start(bf16[8,256,128]{2,1,0:T(8,128)(2,1)S(1)} %join_far.1.far.refs_5_), channel_id=1, source_target_pairs={{0,48},{2,50},{4,52},{6,54},{8,14},{10,12},{12,10},{14,8},{16,32},... | collective-permute-start | bytes 1572872 | tf_op jit(solution)/shard_map/ppermute | solution.py:395
  47.0 16.2 %collective-permute-start.15 = (bf16[8,256,128]{2,1,0:T(8,128)(2,1)S(1)}, bf16[8,256,128]{2,1,0:T(8,128)(2,1)S(1)}, u32[]{:S(2)}, u32[]{:S(2)}) collective-permute-start(bf16[8,256,128]{2,1,0:T(8,128)(2,1)S(1)} %join_far.1.far.refs_5_), channel_id=1, source_target_pairs={{0,32},{2,34},{4,36},{6,38},{8,12},{10,14},{12,8},{14,10},{16,48},... | collective-permute-start | bytes 1572872 | tf_op jit(solution)/shard_map/ppermute | solution.py:395
  48.0 15.3 %collective-permute-start.12 = (bf16[8,256,128]{2,1,0:T(8,128)(2,1)S(1)}, bf16[8,256,128]{2,1,0:T(8,128)(2,1)S(1)}, u32[]{:S(2)}, u32[]{:S(2)}) collective-permute-start(bf16[8,256,128]{2,1,0:T(8,128)(2,1)S(1)} %join_far.1.far.refs_5_), channel_id=1, source_target_pairs={{0,8},{8,0},{1,9},{9,1},{2,10},{10,2},{3,11},{11,3},{4,12},{12,4},... | collective-permute-start | bytes 1572872 | tf_op jit(solution)/shard_map/ppermute | solution.py:386
  55.1 8.1 %collective-permute-start.11 = (bf16[256,1024]{1,0:T(8,128)(2,1)S(1)}, bf16[256,1024]{1,0:T(8,128)(2,1)S(1)}, u32[]{:S(2)}, u32[]{:S(2)}) collective-permute-start(bf16[256,1024]{1,0:T(8,128)(2,1)S(1)} %get-tuple-element.15.mine), channel_id=1, source_target_pairs={{0,8},{8,0},{1,9},{9,1},{2,10},{10,2},{3,11},{11,3},{4,12},{12,4},... | collective-permute-start | bytes 1572872 | tf_op jit(solution)/shard_map/ppermute | solution.py:386
  57.1 6.2 %collective-permute-start.13 = (bf16[8,256,128]{2,1,0:T(8,128)(2,1)S(1)}, bf16[8,256,128]{2,1,0:T(8,128)(2,1)S(1)}, u32[]{:S(2)}, u32[]{:S(2)}) collective-permute-start(bf16[8,256,128]{2,1,0:T(8,128)(2,1)S(1)} %collective-permute-done.10.refs_6_), channel_id=1, source_target_pairs={{0,8},{8,0},{1,9},{9,1},{2,10},{10,2},{3,11},{11,3},{4,12},{12,4},... | collective-permute-start | bytes 1572872 | tf_op jit(solution)/shard_map/ppermute | solution.py:386
  58.8 6.4 %collective-permute-start.16 = (bf16[8,256,128]{2,1,0:T(8,128)(2,1)S(1)}, bf16[8,256,128]{2,1,0:T(8,128)(2,1)S(1)}, u32[]{:S(2)}, u32[]{:S(2)}) collective-permute-start(bf16[8,256,128]{2,1,0:T(8,128)(2,1)S(1)} %collective-permute-done.14.refs_2_), channel_id=1, source_target_pairs={{0,8},{8,0},{1,9},{9,1},{2,10},{10,2},{3,11},{11,3},{4,12},{12,4},... | collective-permute-start | bytes 1572872 | tf_op jit(solution)/shard_map/ppermute | solution.py:386
  63.3 2.3 %collective-permute-start.17 = (bf16[8,256,128]{2,1,0:T(8,128)(2,1)S(1)}, bf16[8,256,128]{2,1,0:T(8,128)(2,1)S(1)}, u32[]{:S(2)}, u32[]{:S(2)}) collective-permute-start(bf16[8,256,128]{2,1,0:T(8,128)(2,1)S(1)} %collective-permute-done.15.refs_3_), channel_id=1, source_target_pairs={{0,8},{8,0},{1,9},{9,1},{2,10},{10,2},{3,11},{11,3},{4,12},{12,4},... | collective-permute-start | bytes 1572872 | tf_op jit(solution)/shard_map/ppermute | solution.py:386

commit v8 on v7

--- a/solution.py
+++ b/solution.py
@@ -17,7 +17,7 @@
 step_rate = 0.02
 F32, BF16 = jnp.float32, jnp.bfloat16
 VMEM = pl.BlockSpec(memory_space=pltpu.VMEM)
-RING = (1, 3, 2)
+RING = (3, 1, 2)
 ANY = pl.BlockSpec(memory_space=pl.ANY)
 HBM = pl.BlockSpec(memory_space=pltpu.HBM)
 

time: 67 us -> 67.1 us (level)
  transfers between devices with their start and end apart: 18 -> 18, of which waited for: 6 -> 4; matrix products, arithmetic and copies ran while one was open for 0% -> 0% of each run, Pallas kernels for 16% -> 16%
where the time goes in v8:
time: 67.1 us; the launch traced here: 66.9 us
  starting transfers between devices  23.9 us (36%)
  blocking collectives  18.1 us (27%)
  Pallas kernels  13.5 us (20%)
  waiting for transfers between devices  10.5 us (16%)
  between operations  0.92 us (1%)
    all_to_all x1, blocking collectives, per_device(): arrived = lax.all_to_all(sent, ('zh', 'y'), 0, 0, tiled=True)  18.1 us
    ppermute x10, starting transfers between devices, swapped(): return lax.ppermute(array, axis, [(i, i ^ k) for i in range(size)])  15.4 us
    ppermute x8, starting transfers between devices, crossed(): return lax.ppermute(array, ('y', 'c', 'x'), perm)  8.41 us
    ppermute x8, waiting for transfers between devices, crossed(): return lax.ppermute(array, ('y', 'c', 'x'), perm)  7.69 us
    pallas_call x1, Pallas kernels, extract(): pl.pallas_call(extract_kernel, in_specs=[HBM] * 4, out_specs=VMEM, out_sh...  3.82 us
    pallas_call x1, Pallas kernels, kept(): pl.pallas_call(kept_kernel, grid=(2,), in_specs=[block, block, pl.BlockSp...  3.2 us
    ppermute x10, waiting for transfers between devices, swapped(): return lax.ppermute(array, axis, [(i, i ^ k) for i in range(size)])  2.77 us
    pallas_call x1, Pallas kernels, choose(): pl.pallas_call(functools.partial(choose_kernel, groups), in_specs=[ANY] *...  1.84 us
  transfers between devices with their start and end apart: 18, of which 4 were waited for; matrix products, arithmetic and copies ran while one was open for 0% of the time, Pallas kernels for 16%

profile of v8, /device:TPU:1, one launch (start us, length us, event | category | flops | bytes accessed | tf_op | source)
XLA Modules:
  0.0 66.9 jit_solution(9461566579455078434)
XLA Ops:
  0.6 3.3 %collective-permute-start.1 = (bf16[256,1024]{1,0:T(8,128)(2,1)}, bf16[256,1024]{1,0:T(8,128)(2,1)S(1)}, u32[]{:S(2)}, u32[]{:S(2)}) collective-permute-start(bf16[256,1024]{1,0:T(8,128)(2,1)} %param.5), channel_id=1, source_target_pairs={{0,8},{8,0},{1,9},{9,1},{2,10},{10,2},{3,11},{11,3},{4,12},{12,4},... | collective-permute-start | bytes 1572872 | tf_op jit(solution)/shard_map/ppermute | solution.py:386
  4.0 0.1 collective-permute-start.2
  4.1 3.8 %extract.1.sent = f32[16,8,128]{2,1,0:T(8,128)} custom-call(f32[256,1024]{1,0:T(8,128)} %bitcast.4, bf16[256,1024]{1,0:T(8,128)(2,1)} %bitcast.6, s32[4,16,32]{2,1,0:T(8,128)} %bitcast.8, bf16[4,256,256]{2,1,0:T(8,128)(2,1)} %constant.2.clone.table.basis), custom_call_target="tpu_custom_call" | custom-call | flops 1000000000 | bytes 2097152 | tf_op jit(solution)/shard_map/extract/pallas_call | solution.py:114
  7.9 18.1 %all_to_all.5.arrived = f32[16,8,128]{2,1,0:T(8,128)S(1)} all-to-all(f32[16,8,128]{2,1,0:T(8,128)} %extract.1.sent), channel_id=1, replica_groups=mesh['zh'=4,'y'=4,'c'=2,'x'=4,'zl'=2] {'zh','y'}, dimensions={0} | all-to-all | bytes 131072 | tf_op jit(solution)/shard_map/all_to_all | solution.py:405
  26.0 0.0 copy-start
  26.0 0.0 copy-start.1
  26.0 0.0 copy-start.2
  26.0 0.0 copy-start.3
  26.0 1.9 %collective-permute-start = (f32[16,8,128]{2,1,0:T(8,128)S(1)}, f32[16,8,128]{2,1,0:T(8,128)S(1)}, u32[]{:S(2)}, u32[]{:S(2)}) collective-permute-start(f32[16,8,128]{2,1,0:T(8,128)S(1)} %all_to_all.5.arrived), channel_id=1, source_target_pairs={{0,8},{8,0},{1,9},{9,1},{2,10},{10,2},{3,11},{11,3},{4,12},{12,4},... | collective-permute-start | bytes 196616 | tf_op jit(solution)/shard_map/ppermute | solution.py:386
  28.0 0.9 %begin.1.begun = f32[128,256]{1,0:T(8,128)S(1)} custom-call(f32[16,8,128]{2,1,0:T(8,128)S(1)} %all_to_all.5.arrived), custom_call_target="tpu_custom_call" | custom-call | flops 1000000000 | bytes 1048576 | tf_op jit(solution)/shard_map/begin/pallas_call | solution.py:192
  28.9 0.0 collective-permute-done.arrived
  28.9 0.0 collective-permute-done.1.weight
  28.9 0.0 collective-permute-done.2.basis
  28.9 1.4 %decode.1 = (bf16[1,256,128]{2,1,0:T(8,128)(2,1)S(1)}, bf16[1,256,128]{2,1,0:T(8,128)(2,1)S(1)}) custom-call(f32[128,256]{1,0:T(8,128)S(1)} %begin.1.begun, f32[16,8,128]{2,1,0:T(8,128)S(1)} %collective-permute-done.arrived, bf16[256,1024]{1,0:T(8,128)(2,1)S(1)} %collective-permute-done.1.weight, bf16[4,256,256]{2,1,0:T(8,128)(2,1)S(1)} %collective-permute-done.2.basis), custom_call_target="tpu_custom_call" | custom-call | flops 1000000000 | bytes 1048576 | tf_op jit(solution)/shard_map/decode/pallas_call | solution.py:215
  30.4 0.4 collective-permute-start.3
  30.8 0.7 %collective-permute-start.6 = (bf16[1,256,128]{2,1,0:T(8,128)(2,1)S(1)}, bf16[1,256,128]{2,1,0:T(8,128)(2,1)S(1)}, u32[]{:S(2)}, u32[]{:S(2)}) collective-permute-start(bf16[1,256,128]{2,1,0:T(8,128)(2,1)S(1)} %get-tuple-element.11.a), channel_id=1, source_target_pairs={{0,1},{1,0},{2,3},{3,2},{4,5},{5,4},{6,7},{7,6},{8,9},{9,8},{10,11... | collective-permute-start | bytes 196616 | tf_op jit(solution)/shard_map/ppermute | solution.py:386
  31.4 0.3 collective-permute-done.3.c
  31.7 2.5 %collective-permute-done.6.fresh_z.a_z = bf16[1,256,128]{2,1,0:T(8,128)(2,1)S(1)} collective-permute-done((bf16[1,256,128]{2,1,0:T(8,128)(2,1)S(1)}, bf16[1,256,128]{2,1,0:T(8,128)(2,1)S(1)}, u32[]{:S(2)}, u32[]{:S(2)}) %collective-permute-start.6) | collective-permute-done | bytes 65568 | tf_op jit(solution)/shard_map/ppermute | solution.py:386
  34.2 0.9 %collective-permute-start.7 = (bf16[4,256,128]{2,1,0:T(8,128)(2,1)S(1)}, bf16[4,256,128]{2,1,0:T(8,128)(2,1)S(1)}, u32[]{:S(2)}, u32[]{:S(2)}) collective-permute-start(bf16[4,256,128]{2,1,0:T(8,128)(2,1)S(1)} %join_four.1), channel_id=1, source_target_pairs={{0,4},{2,6},{4,0},{6,2},{8,40},{10,42},{12,44},{14,46},{16,20},{18... | collective-permute-start | bytes 786440 | tf_op jit(solution)/shard_map/ppermute | solution.py:395
  35.2 1.8 %collective-permute-start.4 = (bf16[3,256,128]{2,1,0:T(8,128)(2,1)S(1)}, bf16[3,256,128]{2,1,0:T(8,128)(2,1)S(1)}, u32[]{:S(2)}, u32[]{:S(2)}) collective-permute-start(bf16[3,256,128]{2,1,0:T(8,128)(2,1)S(1)} %join_near.1.near.a.refs_0_), channel_id=1, source_target_pairs={{0,6},{2,4},{4,2},{6,0},{8,56},{10,58},{12,60},{14,62},{16,22},{18... | collective-permute-start | bytes 589832 | tf_op jit(solution)/shard_map/ppermute | solution.py:395
  37.0 0.0 collective-permute-start.5
  37.0 0.9 %collective-permute-start.8 = (bf16[1,256,128]{2,1,0:T(8,128)(2,1)S(1)}, bf16[1,256,128]{2,1,0:T(8,128)(2,1)S(1)}, u32[]{:S(2)}, u32[]{:S(2)}) collective-permute-start(bf16[1,256,128]{2,1,0:T(8,128)(2,1)S(1)} %collective-permute-done.6.fresh_z.a_z), channel_id=1, source_target_pairs={{0,6},{2,4},{4,2},{6,0},{8,56},{10,58},{12,60},{14,62},{16,22},{18... | collective-permute-start | bytes 196616 | tf_op jit(solution)/shard_map/ppermute | solution.py:395
  37.8 0.9 %collective-permute-start.9 = (bf16[1,256,128]{2,1,0:T(8,128)(2,1)S(1)}, bf16[1,256,128]{2,1,0:T(8,128)(2,1)S(1)}, u32[]{:S(2)}, u32[]{:S(2)}) collective-permute-start(bf16[1,256,128]{2,1,0:T(8,128)(2,1)S(1)} %collective-permute-done.6.fresh_z.a_z), channel_id=1, source_target_pairs={{0,2},{2,0},{4,6},{6,4},{8,24},{10,26},{12,28},{14,30},{16,18},{18... | collective-permute-start | bytes 196616 | tf_op jit(solution)/shard_map/ppermute | solution.py:395
  38.7 5.5 %collective-permute-done.8.b_z = bf16[1,256,128]{2,1,0:T(8,128)(2,1)S(1)} collective-permute-done((bf16[1,256,128]{2,1,0:T(8,128)(2,1)S(1)}, bf16[1,256,128]{2,1,0:T(8,128)(2,1)S(1)}, u32[]{:S(2)}, u32[]{:S(2)}) %collective-permute-start.8) | collective-permute-done | bytes 65568 | tf_op jit(solution)/shard_map/ppermute | solution.py:395
  44.2 0.0 collective-permute-done.9.c_z
  44.2 0.0 collective-permute-done.4.b.refs_1_
  44.2 0.0 collective-permute-done.5.c.refs_2_
  44.2 0.0 collective-permute-done.7.across.refs_3_
  44.2 2.6 %collective-permute-start.10 = (bf16[8,256,128]{2,1,0:T(8,128)(2,1)S(1)}, bf16[8,256,128]{2,1,0:T(8,128)(2,1)S(1)}, u32[]{:S(2)}, u32[]{:S(2)}) collective-permute-start(bf16[8,256,128]{2,1,0:T(8,128)(2,1)S(1)} %join_far.1.far.refs_5_), channel_id=1, source_target_pairs={{0,48},{2,50},{4,52},{6,54},{8,14},{10,12},{12,10},{14,8},{16,32},... | collective-permute-start | bytes 1572872 | tf_op jit(solution)/shard_map/ppermute | solution.py:395
  46.8 0.0 collective-permute-start.14
  46.8 1.4 %collective-permute-start.15 = (bf16[8,256,128]{2,1,0:T(8,128)(2,1)S(1)}, bf16[8,256,128]{2,1,0:T(8,128)(2,1)S(1)}, u32[]{:S(2)}, u32[]{:S(2)}) collective-permute-start(bf16[8,256,128]{2,1,0:T(8,128)(2,1)S(1)} %join_far.1.far.refs_5_), channel_id=1, source_target_pairs={{0,32},{2,34},{4,36},{6,38},{8,12},{10,14},{12,8},{14,10},{16,48},... | collective-permute-start | bytes 1572872 | tf_op jit(solution)/shard_map/ppermute | solution.py:395
  48.2 2.8 %collective-permute-start.12 = (bf16[8,256,128]{2,1,0:T(8,128)(2,1)S(1)}, bf16[8,256,128]{2,1,0:T(8,128)(2,1)S(1)}, u32[]{:S(2)}, u32[]{:S(2)}) collective-permute-start(bf16[8,256,128]{2,1,0:T(8,128)(2,1)S(1)} %join_far.1.far.refs_5_), channel_id=1, source_target_pairs={{0,8},{8,0},{1,9},{9,1},{2,10},{10,2},{3,11},{11,3},{4,12},{12,4},... | collective-permute-start | bytes 1572872 | tf_op jit(solution)/shard_map/ppermute | solution.py:386
  51.0 0.0 copy-done
  51.0 0.0 copy-done.1
  51.0 0.0 copy-done.2
  51.0 0.0 copy-done.3
  51.0 3.2 %kept.1 = (f32[256,1024]{1,0:T(8,128)}, f32[8,128]{1,0:T(8,128)S(1)}) custom-call(f32[256,1024]{1,0:T(8,128)S(1)} %bitcast.5, bf16[256,1024]{1,0:T(8,128)(2,1)S(1)} %bitcast.7, f32[16,8,128]{2,1,0:T(8,128)S(1)} %copy-done, bf16[4,256,256]{2,1,0:T(8,128)(2,1)S(1)} %copy-done.3, bf16[8,256,128]{2,1,0:T(8,128)(2,1)S(1)} %join_far.1.far.refs_5_), custom_call_target="tpu_custom_call" | custom-call | flops 2000000000 | bytes 3145728 | tf_op jit(solution)/shard_map/kept/pallas_call | solution.py:156
  54.2 0.0 collective-permute-done.10.refs_6_
  54.2 1.1 %lay.1 = (bf16[256,1024]{1,0:T(8,128)(2,1)S(1)}, bf16[256,8192]{1,0:T(8,128)(2,1)}) custom-call(bf16[3,256,128]{2,1,0:T(8,128)(2,1)S(1)} %join_near.1.near.a.refs_0_, bf16[3,256,128]{2,1,0:T(8,128)(2,1)S(1)} %collective-permute-done.4.b.refs_1_, bf16[3,256,128]{2,1,0:T(8,128)(2,1)S(1)} %collective-permute-done.5.c.refs_2_, ...), custom_call_target="tpu_custom_call" | custom-call | tf_op jit(solution)/shard_map/lay/pallas_call | solution.py:322
  55.3 2.6 %collective-permute-start.11 = (bf16[256,1024]{1,0:T(8,128)(2,1)S(1)}, bf16[256,1024]{1,0:T(8,128)(2,1)S(1)}, u32[]{:S(2)}, u32[]{:S(2)}) collective-permute-start(bf16[256,1024]{1,0:T(8,128)(2,1)S(1)} %get-tuple-element.15.mine), channel_id=1, source_target_pairs={{0,8},{8,0},{1,9},{9,1},{2,10},{10,2},{3,11},{11,3},{4,12},{12,4},... | collective-permute-start | bytes 1572872 | tf_op jit(solution)/shard_map/ppermute | solution.py:386
  57.9 0.1 collective-permute-start.13
  58.0 0.0 collective-permute-done.14.refs_2_
  58.0 0.4 collective-permute-start.16
  58.4 2.2 %collective-permute-done.15.refs_3_ = bf16[8,256,128]{2,1,0:T(8,128)(2,1)S(1)} collective-permute-done((bf16[8,256,128]{2,1,0:T(8,128)(2,1)S(1)}, bf16[8,256,128]{2,1,0:T(8,128)(2,1)S(1)}, u32[]{:S(2)}, u32[]{:S(2)}) %collective-permute-start.15) | collective-permute-done | bytes 524320 | tf_op jit(solution)/shard_map/ppermute | solution.py:395
  60.6 3.1 %collective-permute-start.17 = (bf16[8,256,128]{2,1,0:T(8,128)(2,1)S(1)}, bf16[8,256,128]{2,1,0:T(8,128)(2,1)S(1)}, u32[]{:S(2)}, u32[]{:S(2)}) collective-permute-start(bf16[8,256,128]{2,1,0:T(8,128)(2,1)S(1)} %collective-permute-done.15.refs_3_), channel_id=1, source_target_pairs={{0,8},{8,0},{1,9},{9,1},{2,10},{10,2},{3,11},{11,3},{4,12},{12,4},... | collective-permute-start | bytes 1572872 | tf_op jit(solution)/shard_map/ppermute | solution.py:386
  63.8 0.0 collective-permute-done.12.refs_0_
  63.8 0.0 collective-permute-done.11.theirs
  63.8 0.0 collective-permute-done.13.refs_1_
  63.8 1.8 %choose.1 = (bf16[256,1024]{1,0:T(8,128)(2,1)}, bf16[256,8192]{1,0:T(8,128)(2,1)}) custom-call(bf16[256,1024]{1,0:T(8,128)(2,1)S(1)} %get-tuple-element.15.mine, bf16[256,1024]{1,0:T(8,128)(2,1)S(1)} %collective-permute-done.11.theirs, bf16[8,256,128]{2,1,0:T(8,128)(2,1)S(1)} %collective-permute-done.12.refs_0_, ...), custom_call_target="tpu_custom_call", output_to_operand_aliasing={{1}: (6, {})} | custom-call | tf_op jit(solution)/shard_map/choose/pallas_call | solution.py:351
  65.6 0.0 collective-permute-done.16.refs_0_
  65.7 0.0 collective-permute-done.17.refs_1_
  65.7 1.1 %finish.1 = bf16[256,8192]{1,0:T(8,128)(2,1)} custom-call(bf16[8,256,128]{2,1,0:T(8,128)(2,1)S(1)} %collective-permute-done.16.refs_0_, bf16[8,256,128]{2,1,0:T(8,128)(2,1)S(1)} %collective-permute-done.17.refs_1_, bf16[256,8192]{1,0:T(8,128)(2,1)} %get-tuple-element.18.refs_2_), custom_call_target="tpu_custom_call", output_to_operand_aliasing={{}: (2, {})} | custom-call | tf_op jit(solution)/shard_map/finish/pallas_call | solution.py:373
  (3 shorter events, 0.1 us)
Async XLA Ops:
  0.6 28.3 %collective-permute-start.1 = (bf16[256,1024]{1,0:T(8,128)(2,1)}, bf16[256,1024]{1,0:T(8,128)(2,1)S(1)}, u32[]{:S(2)}, u32[]{:S(2)}) collective-permute-start(bf16[256,1024]{1,0:T(8,128)(2,1)} %param.5), channel_id=1, source_target_pairs={{0,8},{8,0},{1,9},{9,1},{2,10},{10,2},{3,11},{11,3},{4,12},{12,4},... | collective-permute-start | bytes 1572872 | tf_op jit(solution)/shard_map/ppermute | solution.py:386
  4.0 25.0 %collective-permute-start.2 = (bf16[4,256,256]{2,1,0:T(8,128)(2,1)}, bf16[4,256,256]{2,1,0:T(8,128)(2,1)S(1)}, u32[]{:S(2)}, u32[]{:S(2)}) collective-permute-start(bf16[4,256,256]{2,1,0:T(8,128)(2,1)} %constant.2.clone.table.basis), channel_id=1, source_target_pairs={{0,8},{8,0},{1,9},{9,1},{2,10},{10,2},{3,11},{11,3},{4,12},{12,4},... | collective-permute-start | bytes 1572872 | tf_op jit(solution)/shard_map/ppermute | solution.py:386
  26.0 25.0 %copy-start = (f32[16,8,128]{2,1,0:T(8,128)S(1)}, f32[16,8,128]{2,1,0:T(8,128)}, u32[]{:S(2)}) copy-start(f32[16,8,128]{2,1,0:T(8,128)} %extract.1.sent) | copy-start | bytes 196612
  26.0 25.0 %copy-start.1 = (f32[1,256,1024]{2,1,0:T(8,128)S(1)}, f32[1,256,1024]{2,1,0:T(8,128)}, u32[]{:S(2)}) copy-start(f32[1,256,1024]{2,1,0:T(8,128)} %param.6) | copy-start | bytes 3145732
  26.0 25.0 %copy-start.2 = (bf16[1,256,1024]{2,1,0:T(8,128)(2,1)S(1)}, bf16[1,256,1024]{2,1,0:T(8,128)(2,1)}, u32[]{:S(2)}) copy-start(bf16[1,256,1024]{2,1,0:T(8,128)(2,1)} %param.7) | copy-start | bytes 1572868
  26.0 25.0 %copy-start.3 = (bf16[4,256,256]{2,1,0:T(8,128)(2,1)S(1)}, bf16[4,256,256]{2,1,0:T(8,128)(2,1)}, u32[]{:S(2)}) copy-start(bf16[4,256,256]{2,1,0:T(8,128)(2,1)} %constant.2.clone.table.basis) | copy-start | bytes 1572868
  26.0 2.9 %collective-permute-start = (f32[16,8,128]{2,1,0:T(8,128)S(1)}, f32[16,8,128]{2,1,0:T(8,128)S(1)}, u32[]{:S(2)}, u32[]{:S(2)}) collective-permute-start(f32[16,8,128]{2,1,0:T(8,128)S(1)} %all_to_all.5.arrived), channel_id=1, source_target_pairs={{0,8},{8,0},{1,9},{9,1},{2,10},{10,2},{3,11},{11,3},{4,12},{12,4},... | collective-permute-start | bytes 196616 | tf_op jit(solution)/shard_map/ppermute | solution.py:386
  30.4 1.3 %collective-permute-start.3 = (bf16[1,256,128]{2,1,0:T(8,128)(2,1)S(1)}, bf16[1,256,128]{2,1,0:T(8,128)(2,1)S(1)}, u32[]{:S(2)}, u32[]{:S(2)}) collective-permute-start(bf16[1,256,128]{2,1,0:T(8,128)(2,1)S(1)} %get-tuple-element.12.b), channel_id=1, source_target_pairs={{0,8},{8,0},{1,9},{9,1},{2,10},{10,2},{3,11},{11,3},{4,12},{12,4},... | collective-permute-start | bytes 196616 | tf_op jit(solution)/shard_map/ppermute | solution.py:386
  30.8 3.5 %collective-permute-start.6 = (bf16[1,256,128]{2,1,0:T(8,128)(2,1)S(1)}, bf16[1,256,128]{2,1,0:T(8,128)(2,1)S(1)}, u32[]{:S(2)}, u32[]{:S(2)}) collective-permute-start(bf16[1,256,128]{2,1,0:T(8,128)(2,1)S(1)} %get-tuple-element.11.a), channel_id=1, source_target_pairs={{0,1},{1,0},{2,3},{3,2},{4,5},{5,4},{6,7},{7,6},{8,9},{9,8},{10,11... | collective-permute-start | bytes 196616 | tf_op jit(solution)/shard_map/ppermute | solution.py:386
  34.2 9.9 %collective-permute-start.7 = (bf16[4,256,128]{2,1,0:T(8,128)(2,1)S(1)}, bf16[4,256,128]{2,1,0:T(8,128)(2,1)S(1)}, u32[]{:S(2)}, u32[]{:S(2)}) collective-permute-start(bf16[4,256,128]{2,1,0:T(8,128)(2,1)S(1)} %join_four.1), channel_id=1, source_target_pairs={{0,4},{2,6},{4,0},{6,2},{8,40},{10,42},{12,44},{14,46},{16,20},{18... | collective-permute-start | bytes 786440 | tf_op jit(solution)/shard_map/ppermute | solution.py:395
  35.2 9.0 %collective-permute-start.4 = (bf16[3,256,128]{2,1,0:T(8,128)(2,1)S(1)}, bf16[3,256,128]{2,1,0:T(8,128)(2,1)S(1)}, u32[]{:S(2)}, u32[]{:S(2)}) collective-permute-start(bf16[3,256,128]{2,1,0:T(8,128)(2,1)S(1)} %join_near.1.near.a.refs_0_), channel_id=1, source_target_pairs={{0,6},{2,4},{4,2},{6,0},{8,56},{10,58},{12,60},{14,62},{16,22},{18... | collective-permute-start | bytes 589832 | tf_op jit(solution)/shard_map/ppermute | solution.py:395
  37.0 7.2 %collective-permute-start.5 = (bf16[3,256,128]{2,1,0:T(8,128)(2,1)S(1)}, bf16[3,256,128]{2,1,0:T(8,128)(2,1)S(1)}, u32[]{:S(2)}, u32[]{:S(2)}) collective-permute-start(bf16[3,256,128]{2,1,0:T(8,128)(2,1)S(1)} %join_near.1.near.a.refs_0_), channel_id=1, source_target_pairs={{0,2},{2,0},{4,6},{6,4},{8,24},{10,26},{12,28},{14,30},{16,18},{18... | collective-permute-start | bytes 589832 | tf_op jit(solution)/shard_map/ppermute | solution.py:395
  37.0 7.2 %collective-permute-start.8 = (bf16[1,256,128]{2,1,0:T(8,128)(2,1)S(1)}, bf16[1,256,128]{2,1,0:T(8,128)(2,1)S(1)}, u32[]{:S(2)}, u32[]{:S(2)}) collective-permute-start(bf16[1,256,128]{2,1,0:T(8,128)(2,1)S(1)} %collective-permute-done.6.fresh_z.a_z), channel_id=1, source_target_pairs={{0,6},{2,4},{4,2},{6,0},{8,56},{10,58},{12,60},{14,62},{16,22},{18... | collective-permute-start | bytes 196616 | tf_op jit(solution)/shard_map/ppermute | solution.py:395
  37.8 6.3 %collective-permute-start.9 = (bf16[1,256,128]{2,1,0:T(8,128)(2,1)S(1)}, bf16[1,256,128]{2,1,0:T(8,128)(2,1)S(1)}, u32[]{:S(2)}, u32[]{:S(2)}) collective-permute-start(bf16[1,256,128]{2,1,0:T(8,128)(2,1)S(1)} %collective-permute-done.6.fresh_z.a_z), channel_id=1, source_target_pairs={{0,2},{2,0},{4,6},{6,4},{8,24},{10,26},{12,28},{14,30},{16,18},{18... | collective-permute-start | bytes 196616 | tf_op jit(solution)/shard_map/ppermute | solution.py:395
  44.2 10.0 %collective-permute-start.10 = (bf16[8,256,128]{2,1,0:T(8,128)(2,1)S(1)}, bf16[8,256,128]{2,1,0:T(8,128)(2,1)S(1)}, u32[]{:S(2)}, u32[]{:S(2)}) collective-permute-start(bf16[8,256,128]{2,1,0:T(8,128)(2,1)S(1)} %join_far.1.far.refs_5_), channel_id=1, source_target_pairs={{0,48},{2,50},{4,52},{6,54},{8,14},{10,12},{12,10},{14,8},{16,32},... | collective-permute-start | bytes 1572872 | tf_op jit(solution)/shard_map/ppermute | solution.py:395
  46.8 11.2 %collective-permute-start.14 = (bf16[8,256,128]{2,1,0:T(8,128)(2,1)S(1)}, bf16[8,256,128]{2,1,0:T(8,128)(2,1)S(1)}, u32[]{:S(2)}, u32[]{:S(2)}) collective-permute-start(bf16[8,256,128]{2,1,0:T(8,128)(2,1)S(1)} %join_far.1.far.refs_5_), channel_id=1, source_target_pairs={{0,16},{2,18},{4,20},{6,22},{8,10},{10,8},{12,14},{14,12},{16,0},{... | collective-permute-start | bytes 1572872 | tf_op jit(solution)/shard_map/ppermute | solution.py:395
  46.8 13.8 %collective-permute-start.15 = (bf16[8,256,128]{2,1,0:T(8,128)(2,1)S(1)}, bf16[8,256,128]{2,1,0:T(8,128)(2,1)S(1)}, u32[]{:S(2)}, u32[]{:S(2)}) collective-permute-start(bf16[8,256,128]{2,1,0:T(8,128)(2,1)S(1)} %join_far.1.far.refs_5_), channel_id=1, source_target_pairs={{0,32},{2,34},{4,36},{6,38},{8,12},{10,14},{12,8},{14,10},{16,48},... | collective-permute-start | bytes 1572872 | tf_op jit(solution)/shard_map/ppermute | solution.py:395
  48.2 15.6 %collective-permute-start.12 = (bf16[8,256,128]{2,1,0:T(8,128)(2,1)S(1)}, bf16[8,256,128]{2,1,0:T(8,128)(2,1)S(1)}, u32[]{:S(2)}, u32[]{:S(2)}) collective-permute-start(bf16[8,256,128]{2,1,0:T(8,128)(2,1)S(1)} %join_far.1.far.refs_5_), channel_id=1, source_target_pairs={{0,8},{8,0},{1,9},{9,1},{2,10},{10,2},{3,11},{11,3},{4,12},{12,4},... | collective-permute-start | bytes 1572872 | tf_op jit(solution)/shard_map/ppermute | solution.py:386
  55.3 8.4 %collective-permute-start.11 = (bf16[256,1024]{1,0:T(8,128)(2,1)S(1)}, bf16[256,1024]{1,0:T(8,128)(2,1)S(1)}, u32[]{:S(2)}, u32[]{:S(2)}) collective-permute-start(bf16[256,1024]{1,0:T(8,128)(2,1)S(1)} %get-tuple-element.15.mine), channel_id=1, source_target_pairs={{0,8},{8,0},{1,9},{9,1},{2,10},{10,2},{3,11},{11,3},{4,12},{12,4},... | collective-permute-start | bytes 1572872 | tf_op jit(solution)/shard_map/ppermute | solution.py:386
  57.9 5.9 %collective-permute-start.13 = (bf16[8,256,128]{2,1,0:T(8,128)(2,1)S(1)}, bf16[8,256,128]{2,1,0:T(8,128)(2,1)S(1)}, u32[]{:S(2)}, u32[]{:S(2)}) collective-permute-start(bf16[8,256,128]{2,1,0:T(8,128)(2,1)S(1)} %collective-permute-done.10.refs_6_), channel_id=1, source_target_pairs={{0,8},{8,0},{1,9},{9,1},{2,10},{10,2},{3,11},{11,3},{4,12},{12,4},... | collective-permute-start | bytes 1572872 | tf_op jit(solution)/shard_map/ppermute | solution.py:386
  58.0 7.6 %collective-permute-start.16 = (bf16[8,256,128]{2,1,0:T(8,128)(2,1)S(1)}, bf16[8,256,128]{2,1,0:T(8,128)(2,1)S(1)}, u32[]{:S(2)}, u32[]{:S(2)}) collective-permute-start(bf16[8,256,128]{2,1,0:T(8,128)(2,1)S(1)} %collective-permute-done.14.refs_2_), channel_id=1, source_target_pairs={{0,8},{8,0},{1,9},{9,1},{2,10},{10,2},{3,11},{11,3},{4,12},{12,4},... | collective-permute-start | bytes 1572872 | tf_op jit(solution)/shard_map/ppermute | solution.py:386
  60.6 5.0 %collective-permute-start.17 = (bf16[8,256,128]{2,1,0:T(8,128)(2,1)S(1)}, bf16[8,256,128]{2,1,0:T(8,128)(2,1)S(1)}, u32[]{:S(2)}, u32[]{:S(2)}) collective-permute-start(bf16[8,256,128]{2,1,0:T(8,128)(2,1)S(1)} %collective-permute-done.15.refs_3_), channel_id=1, source_target_pairs={{0,8},{8,0},{1,9},{9,1},{2,10},{10,2},{3,11},{11,3},{4,12},{12,4},... | collective-permute-start | bytes 1572872 | tf_op jit(solution)/shard_map/ppermute | solution.py:386
